TPU v7x, 32 devices: a whole 2x2x4 slice. The times are simulated.
32 devices in a mesh: groups: 2 (over x), slab: 16 (over z, y, core).
Axes of the slice: x: 2, y: 2, z: 4, core: 2. Of those that a mesh axis runs over, the one named last changes fastest.
Arguments:
- trial_modes: bfloat16 [32, 4096, 384], P(('groups', 'slab')), parts along dimension 0, may hold values from -6 to 6
- onsite_blocks: bfloat16 [32, 96, 128, 128], P(('groups', 'slab')), parts along dimension 0, may hold values from -18 to 18
- onsite_rows: int32 [32, 96], P(('groups', 'slab')), parts along dimension 0, may hold values from 0 to 31
- onsite_cols: int32 [32, 96], P(('groups', 'slab')), parts along dimension 0, may hold values from 0 to 31
- coupling_blocks: bfloat16 [32, 16, 128, 128], P(('groups', 'slab')), parts along dimension 0, may hold values from -48 to 48
- coupling_rows: int32 [32, 16], P(('groups', 'slab')), parts along dimension 0, may hold values from 28 to 31
- coupling_cols: int32 [32, 16], P(('groups', 'slab')), parts along dimension 0, may hold values from 0 to 3
- potential_step: float32 [32], P(('groups', 'slab')), parts along dimension 0, may hold values from -0.6 to 0.6
Outputs:
- onsite_reduced: float32 [32, 384, 384], P(('groups', 'slab')), parts along dimension 0
- coupling_right: float32 [32, 384, 384], P(('groups', 'slab')), parts along dimension 0
- coupling_left: float32 [32, 384, 384], P(('groups', 'slab')), parts along dimension 0
There are 2 independent parts, one for each index of `groups`. A program takes and returns all parts, laid end to end along the dimension named above; each array names one. Nothing has to cross between parts.
Inputs may be any that keep to these rules, and one draw needn't show every extreme that they name: `coupling_cols`: every coupling block lies in the last 4 block rows of its slab and the first 4 block columns of the next slab.
All inputs are finite; a program needn't handle non-finite values.
Results may differ from a plain program's by a relative error of at most 0.0067.
Values may be sent and summed in bfloat16 or wider, within the bound.
No kernel may reach another device: no remote copies, remote signals or barrier semaphores. Data moves between devices by JAX's collectives and lax.ppermute only.
A program may use at most 128 MiB of HBM per device.

v0:
```python
import functools

import jax
import jax.numpy as jnp
from jax import lax
from jax.experimental import pallas as pl
from jax.experimental.pallas import tpu as pltpu
from jax.sharding import PartitionSpec as P

F32 = jnp.float32
BF16 = jnp.bfloat16
VMEM_LIMIT = 56 * 1024 * 1024
SURFACE = 4
TILE = 128
ROWS = 8


def lane(value, k):
    return jnp.broadcast_to(value[:, k : k + 1], value.shape)


def row(value, k):
    return jnp.broadcast_to(value[k : k + 1, :], value.shape)


def exact_dot(a, b, dims):
    return lax.dot_general(
        a, b, (dims, ((), ())), precision=lax.Precision.HIGHEST, preferred_element_type=F32
    )


def bf_dot(a, b, dims):
    return lax.dot_general(a, b, (dims, ((), ())), preferred_element_type=F32)


NN = ((1,), (0,))
TN = ((0,), (0,))
NT = ((1,), (1,))


def factor_tile(a_rows, x_rows):
    panels = len(a_rows)
    for g in range(panels):
        here, here_x = a_rows[g], x_rows[g]
        columns = [lane(here, ROWS * g + j) for j in range(ROWS)]
        s = {(i, j): row(columns[j], i) for j in range(ROWS) for i in range(j, ROWS)}
        r = []
        for k in range(ROWS):
            r.append(lax.rsqrt(s[k, k]))
            for i in range(k + 1, ROWS):
                s[i, k] = s[i, k] * r[k]
            for j in range(k + 1, ROWS):
                for i in range(j, ROWS):
                    s[i, j] = s[i, j] - s[i, k] * s[j, k]
        z, zx = [], []
        for k in range(ROWS):
            top, top_x = row(here, k), row(here_x, k)
            for m in range(k):
                top = top - s[k, m] * z[m]
                top_x = top_x - s[k, m] * zx[m]
            z.append(top * r[k])
            zx.append(top_x * r[k])
        sub = lax.broadcasted_iota(jnp.int32, here.shape, 0)
        packed_x = zx[0]
        for k in range(1, ROWS):
            packed_x = jnp.where(sub == k, zx[k], packed_x)
        x_rows[g] = packed_x
        for i in range(g + 1, panels):
            below = []
            for k in range(ROWS):
                c = lane(a_rows[i], ROWS * g + k)
                for m in range(k):
                    c = c - below[m] * s[k, m]
                below.append(c * r[k])
            a_rows[i] = a_rows[i] - sum(below[k] * z[k] for k in range(ROWS))
            x_rows[i] = x_rows[i] - sum(below[k] * zx[k] for k in range(ROWS))
    return x_rows


def factor_kernel(u_hbm, f_ref, head_ref, tail_ref, u_ref, gram_ref, inv_ref, x_ref, sems):
    orbitals, modes = u_ref.shape
    chunks = sems.shape[0]
    step = orbitals // chunks
    copies = [
        pltpu.make_async_copy(
            u_hbm.at[pl.ds(c * step, step)], u_ref.at[pl.ds(c * step, step)], sems.at[c]
        )
        for c in range(chunks)
    ]
    for copy in copies:
        copy.start()
    for c, copy in enumerate(copies):
        copy.wait()
        part = u_ref[pl.ds(c * step, step), :]
        product = bf_dot(part, part, TN)
        gram_ref[...] = product if c == 0 else gram_ref[...] + product

    tiles = modes // TILE
    inv_ref[...] = jnp.zeros_like(inv_ref)

    def one_tile(b, carry):
        base = pl.multiple_of(b * TILE, TILE)
        here = pl.ds(base, TILE)
        tile = gram_ref[here, here]
        sub = lax.broadcasted_iota(jnp.int32, (ROWS, TILE), 0)
        col = lax.broadcasted_iota(jnp.int32, (ROWS, TILE), 1)
        a_rows = [tile[ROWS * g : ROWS * (g + 1), :] for g in range(TILE // ROWS)]
        x_rows = [(col == sub + ROWS * g).astype(F32) for g in range(TILE // ROWS)]
        x_rows = factor_tile(a_rows, x_rows)
        for g in range(TILE // ROWS):
            x_ref[ROWS * g : ROWS * (g + 1), :] = x_rows[g]
        for static_b in range(tiles):

            @pl.when(b == static_b)
            def _():
                lo, hi = static_b * TILE, (static_b + 1) * TILE
                x = x_ref[...]
                inv_ref[lo:hi, lo:hi] = x
                if static_b:
                    inv_ref[lo:hi, :lo] = exact_dot(x, inv_ref[lo:hi, :lo], NN)
                if static_b + 1 < tiles:
                    upper = exact_dot(x, gram_ref[lo:hi, hi:], NN)
                    gram_ref[hi:, hi:] = gram_ref[hi:, hi:] - exact_dot(upper, upper, TN)
                    inv_ref[hi:, :hi] = inv_ref[hi:, :hi] - exact_dot(
                        upper, inv_ref[lo:hi, :hi], TN
                    )

        return carry

    lax.fori_loop(0, tiles, one_tile, 0)
    factor = inv_ref[...].T.astype(BF16)
    f_ref[...] = factor
    surface = head_ref.shape[0]
    head_ref[...] = bf_dot(u_ref[:surface, :], factor, NN).astype(BF16)
    tail_ref[...] = bf_dot(u_ref[orbitals - surface :, :], factor, NN).astype(BF16)


def apply_blocks(acc_ref, source_ref, blocks_ref, rows_ref, cols_ref, row_base, unroll):
    acc_ref[...] = jnp.zeros_like(acc_ref)

    def some(q, carry):
        for t in range(unroll):
            j = q * unroll + t
            to = pl.multiple_of((rows_ref[j] - row_base) * TILE, TILE)
            at = pl.multiple_of(cols_ref[j] * TILE, TILE)
            product = bf_dot(blocks_ref[j], source_ref[pl.ds(at, TILE), :], NN)
            acc_ref[pl.ds(to, TILE), :] = acc_ref[pl.ds(to, TILE), :] + product
        return carry

    count = blocks_ref.shape[0]
    lax.fori_loop(0, count // unroll, some, 0)
    for j in range(count - count % unroll, count):
        some_j = j
        to = pl.multiple_of((rows_ref[some_j] - row_base) * TILE, TILE)
        at = pl.multiple_of(cols_ref[some_j] * TILE, TILE)
        product = bf_dot(blocks_ref[some_j], source_ref[pl.ds(at, TILE), :], NN)
        acc_ref[pl.ds(to, TILE), :] = acc_ref[pl.ds(to, TILE), :] + product


def spread_kernel(rows_ref, cols_ref, u_ref, blocks_ref, order_ref, out_ref, acc_ref):
    apply_blocks(acc_ref, u_ref, blocks_ref, rows_ref, cols_ref, 0, 4)
    out_ref[...] = acc_ref[...].astype(BF16)


def couple_kernel(
    row_base, rows_ref, cols_ref, next_ref, blocks_ref, tail_ref, order_ref, right_ref, left_ref, acc_ref
):
    apply_blocks(acc_ref, next_ref, blocks_ref, rows_ref, cols_ref, row_base, 4)
    couple = bf_dot(tail_ref[...], acc_ref[...].astype(BF16), TN)
    right_ref[...] = couple
    left_ref[...] = couple.T


def split(value):
    high = value.astype(BF16)
    return high, (value - high.astype(F32)).astype(BF16)


def onsite_kernel(place_ref, u_ref, spread_ref, f_ref, steps_ref, order_ref, out_ref):
    modes = f_ref.shape[0]
    w = bf_dot(u_ref[...], spread_ref[...], TN)
    w = w + w.T
    f = f_ref[...]
    high, low = split(w)
    half = bf_dot(high, f, NN) + bf_dot(low, f, NN)
    high, low = split(half)
    full = bf_dot(f, high, TN) + bf_dot(f, low, TN)
    steps = steps_ref[...]
    reached = lax.broadcasted_iota(jnp.int32, steps.shape, 0) <= place_ref[0]
    potential = jnp.sum(jnp.where(reached, steps, 0.0), axis=0, keepdims=True)[:, :1]
    i = lax.broadcasted_iota(jnp.int32, (modes, modes), 0)
    j = lax.broadcasted_iota(jnp.int32, (modes, modes), 1)
    out_ref[...] = full + jnp.where(i == j, potential, 0.0)


def struct(shape, dtype):
    return jax.ShapeDtypeStruct(shape, dtype)


ANY = pl.BlockSpec(memory_space=pl.ANY)
INTO_VMEM = pl.BlockSpec(memory_space=pltpu.VMEM)
INTO_SMEM = pl.BlockSpec(memory_space=pltpu.SMEM)
PARAMS = pltpu.CompilerParams(vmem_limit_bytes=VMEM_LIMIT)


def passed_along(block, axis, distance):
    devices = range(lax.axis_size(axis))
    route = [(i - distance, i) for i in devices if i - distance in devices]
    return lax.ppermute(block, axis, route)


def cost(flops, moved):
    return pl.CostEstimate(flops=flops, bytes_accessed=moved, transcendentals=0)


def shards(
    trial_modes,
    onsite_blocks,
    onsite_rows,
    onsite_cols,
    coupling_blocks,
    coupling_rows,
    coupling_cols,
    potential_step,
):
    u = trial_modes[0]
    orbitals, modes = u.shape
    surface = SURFACE * TILE
    count = onsite_blocks.shape[1]
    links = coupling_blocks.shape[1]
    steps = lax.all_gather(
        lax.optimization_barrier(jnp.broadcast_to(potential_step[:, None], (1, TILE))),
        "slab",
        tiled=True,
    )
    place = lax.axis_index("slab").astype(jnp.int32).reshape(1)

    factor, head, tail = pl.pallas_call(
        factor_kernel,
        out_shape=(
            struct((modes, modes), BF16),
            struct((surface, modes), BF16),
            struct((surface, modes), BF16),
        ),
        in_specs=[ANY],
        out_specs=(INTO_VMEM,) * 3,
        scratch_shapes=[
            pltpu.VMEM((orbitals, modes), BF16),
            pltpu.VMEM((modes, modes), F32),
            pltpu.VMEM((modes, modes), F32),
            pltpu.VMEM((TILE, TILE), F32),
            pltpu.SemaphoreType.DMA((8,)),
        ],
        compiler_params=PARAMS,
        cost_estimate=cost(2 * orbitals * modes * modes, orbitals * modes * 2),
        name="factor",
    )(u)
    incoming = passed_along(head, "slab", -1)

    spread = pl.pallas_call(
        spread_kernel,
        out_shape=struct((orbitals, modes), BF16),
        in_specs=[INTO_SMEM, INTO_SMEM, INTO_VMEM, INTO_VMEM, ANY],
        out_specs=INTO_VMEM,
        scratch_shapes=[pltpu.VMEM((orbitals, modes), F32)],
        compiler_params=PARAMS,
        cost_estimate=cost(2 * count * TILE * TILE * modes, 3 * orbitals * modes * 2),
        name="spread",
    )(onsite_rows[0], onsite_cols[0], u, onsite_blocks[0], factor)

    right, left = pl.pallas_call(
        functools.partial(couple_kernel, orbitals // TILE - SURFACE),
        out_shape=(struct((modes, modes), F32),) * 2,
        in_specs=[INTO_SMEM, INTO_SMEM, INTO_VMEM, INTO_VMEM, INTO_VMEM, ANY],
        out_specs=(INTO_VMEM,) * 2,
        scratch_shapes=[pltpu.VMEM((surface, modes), F32)],
        compiler_params=PARAMS,
        cost_estimate=cost(2 * links * TILE * TILE * modes, 4 * surface * modes * 2),
        name="couple",
    )(coupling_rows[0], coupling_cols[0], incoming, coupling_blocks[0], tail, spread)
    coupling_left = passed_along(left, "slab", 1)

    onsite = pl.pallas_call(
        onsite_kernel,
        out_shape=struct((modes, modes), F32),
        in_specs=[INTO_SMEM, INTO_VMEM, INTO_VMEM, INTO_VMEM, INTO_VMEM, ANY],
        out_specs=INTO_VMEM,
        compiler_params=PARAMS,
        cost_estimate=cost(2 * orbitals * modes * modes, 2 * orbitals * modes * 2),
        name="onsite",
    )(place, u, spread, factor, steps, right)
    return (onsite[None], right[None], coupling_left[None])


def solution(mesh):
    return jax.shard_map(
        shards,
        mesh=mesh,
        in_specs=(
            P(("groups", "slab"), None, None),
            P(("groups", "slab"), None, None, None),
            P(("groups", "slab"), None),
            P(("groups", "slab"), None),
            P(("groups", "slab"), None, None, None),
            P(("groups", "slab"), None),
            P(("groups", "slab"), None),
            P(("groups", "slab")),
        ),
        out_specs=(
            P(("groups", "slab"), None, None),
            P(("groups", "slab"), None, None),
            P(("groups", "slab"), None, None),
        ),
        check_vma=False,
    )
```

profile of v0, /device:TPU:1, one launch (start us, length us, event | category | flops | bytes accessed | tf_op | source)
XLA Modules:
  0.0 71.8 jit_solution(8274702332107971887)
XLA Ops:
  0.6 18.9 %factor.1 = (bf16[384,384]{1,0:T(8,128)(2,1)}, bf16[512,384]{1,0:T(8,128)(2,1)}, bf16[512,384]{1,0:T(8,128)(2,1)}) custom-call(bf16[4096,384]{1,0:T(8,128)(2,1)} %bitcast.15), custom_call_target="tpu_custom_call" | custom-call | flops 1207959552 | bytes 3145728 | tf_op jit(solution)/shard_map/factor/pallas_call | solution.py:238
  19.6 2.0 %collective-permute-start = (bf16[512,384]{1,0:T(8,128)(2,1)}, bf16[512,384]{1,0:T(8,128)(2,1)S(1)}, u32[]{:S(2)}, u32[]{:S(2)}) collective-permute-start(bf16[512,384]{1,0:T(8,128)(2,1)} %get-tuple-element.9), channel_id=1, source_target_pairs={{1,0},{2,1},{3,2},{4,3},{5,4},{6,5},{7,6},{8,7},{9,8},{10,9},{11,1... | collective-permute-start | bytes 1179656 | tf_op jit(solution)/shard_map/ppermute | solution.py:209
  21.5 11.6 %spread.1.order_ref.spread_ref = bf16[4096,384]{1,0:T(8,128)(2,1)} custom-call(s32[96]{0:T(128)} %bitcast.24, s32[96]{0:T(128)} %bitcast.25, bf16[4096,384]{1,0:T(8,128)(2,1)} %bitcast.16, bf16[96,128,128]{2,1,0:T(8,128)(2,1)} %bitcast.18, bf16[384,384]{1,0:T(8,128)(2,1)} %get-tuple-element.8.order_ref.f_ref), custom_call_target="tpu_custom_call" | custom-call | flops 1207959552 | bytes 9437184 | tf_op jit(solution)/shard_map/spread/pallas_call | solution.py:260
  33.1 0.0 collective-permute-done.next_ref
  33.1 0.0 copy-start
  33.1 0.7 %copy-done = bf16[512,384]{1,0:T(8,128)(2,1)} copy-done((bf16[512,384]{1,0:T(8,128)(2,1)}, bf16[512,384]{1,0:T(8,128)(2,1)S(1)}, u32[]{:S(2)}) %copy-start) | copy-done | bytes 393240
  33.9 3.8 %couple.1 = (f32[384,384]{1,0:T(8,128)}, f32[384,384]{1,0:T(8,128)}) custom-call(s32[16]{0:T(128)} %bitcast.26, s32[16]{0:T(128)} %bitcast.27, bf16[512,384]{1,0:T(8,128)(2,1)} %copy-done, bf16[16,128,128]{2,1,0:T(8,128)(2,1)} %bitcast.22, bf16[512,384]{1,0:T(8,128)(2,1)} %get-tuple-element.10.tail_ref, bf16[4096,384]{1,0:T(8,128)(2,1)} %spread.1.order_ref.spread_ref), custom_call_target="tpu_custom_call" | custom-call | flops 201326592 | bytes 1572864 | tf_op jit(solution)/shard_map/couple/pallas_call | solution.py:271
  37.6 4.5 %collective-permute-start.1 = (f32[384,384]{1,0:T(8,128)}, f32[384,384]{1,0:T(8,128)S(1)}, u32[]{:S(2)}, u32[]{:S(2)}) collective-permute-start(f32[384,384]{1,0:T(8,128)} %get-tuple-element.12), channel_id=1, source_target_pairs={{0,1},{1,2},{2,3},{3,4},{4,5},{5,6},{6,7},{7,8},{8,9},{9,10},{10,1... | collective-permute-start | bytes 1769480 | tf_op jit(solution)/shard_map/ppermute | solution.py:209
  42.8 21.7 %all-gather = f32[16,1,128]{2,1,0:T(1,128)} all-gather(f32[1,1,128]{2,1,0:T(1,128)S(1)} %bitcast.28), channel_id=1, replica_groups=mesh['groups'=2,'slab'=16] {'slab'}, dimensions={0}, use_global_device_ids=true | all-gather | bytes 8704 | tf_op jit(solution)/shard_map/all_gather | solution.py:231
  64.5 6.5 %onsite.1 = f32[384,384]{1,0:T(8,128)} custom-call(s32[1]{0:T(128)} %bitcast.place_ref, bf16[4096,384]{1,0:T(8,128)(2,1)} %bitcast.17, bf16[4096,384]{1,0:T(8,128)(2,1)} %spread.1.order_ref.spread_ref, bf16[384,384]{1,0:T(8,128)(2,1)} %get-tuple-element.8.order_ref.f_ref, f32[16,128]{1,0:T(8,128)} %bitcast.23, f32[384,384]{1,0:T(8,128)} %get-tuple-element.11.order_ref), custom_call_target="tpu_custom_call" | custom-call | flops 1207959552 | bytes 6291456 | tf_op jit(solution)/shard_map/onsite/pallas_call | solution.py:283
  71.0 0.0 collective-permute-done.1
  71.0 0.8 %copy.14 = f32[1,384,384]{2,1,0:T(8,128)} copy(f32[1,384,384]{2,1,0:T(8,128)S(1)} %bitcast.21) | data formatting | bytes 1179648
  (1 shorter events, 0.0 us)
Async XLA Ops:
  19.6 13.5 %collective-permute-start = (bf16[512,384]{1,0:T(8,128)(2,1)}, bf16[512,384]{1,0:T(8,128)(2,1)S(1)}, u32[]{:S(2)}, u32[]{:S(2)}) collective-permute-start(bf16[512,384]{1,0:T(8,128)(2,1)} %get-tuple-element.9), channel_id=1, source_target_pairs={{1,0},{2,1},{3,2},{4,3},{5,4},{6,5},{7,6},{8,7},{9,8},{10,9},{11,1... | collective-permute-start | bytes 1179656 | tf_op jit(solution)/shard_map/ppermute | solution.py:209
  33.1 0.7 %copy-start = (bf16[512,384]{1,0:T(8,128)(2,1)}, bf16[512,384]{1,0:T(8,128)(2,1)S(1)}, u32[]{:S(2)}) copy-start(bf16[512,384]{1,0:T(8,128)(2,1)S(1)} %collective-permute-done.next_ref) | copy-start | bytes 1179652
  37.6 33.4 %collective-permute-start.1 = (f32[384,384]{1,0:T(8,128)}, f32[384,384]{1,0:T(8,128)S(1)}, u32[]{:S(2)}, u32[]{:S(2)}) collective-permute-start(f32[384,384]{1,0:T(8,128)} %get-tuple-element.12), channel_id=1, source_target_pairs={{0,1},{1,2},{2,3},{3,4},{4,5},{5,6},{6,7},{7,8},{8,9},{9,10},{10,1... | collective-permute-start | bytes 1769480 | tf_op jit(solution)/shard_map/ppermute | solution.py:209
where the time goes:
time: 72.2 us; the launch traced here: 71.8 us
  Pallas kernels  40.8 us (57%)
  blocking collectives  21.7 us (30%)
  starting transfers between devices  6.45 us (9%)
  local copies, waits for them, and re-layouts  1.56 us (2%)
  between operations  1.32 us (2%)
    all_gather x1, blocking collectives, shards(): lax.all_gather(lax.optimization_barrier(jnp.broadcast_to(potential_step[:...  21.7 us
    pallas_call x1, Pallas kernels, shards(): pl.pallas_call(factor_kernel, out_shape=(struct((modes, modes), BF16), st...  18.9 us
    pallas_call x1, Pallas kernels, shards(): pl.pallas_call(spread_kernel, out_shape=struct((orbitals, modes), BF16),...  11.6 us
    pallas_call x1, Pallas kernels, shards(): pl.pallas_call(onsite_kernel, out_shape=struct((modes, modes), F32), in_s...  6.53 us
    ppermute x2, starting transfers between devices, passed_along(): return lax.ppermute(block, axis, route)  6.45 us
    pallas_call x1, Pallas kernels, shards(): pl.pallas_call(functools.partial(couple_kernel, orbitals // TILE - SURFAC...  3.79 us
    unnamed x3, local copies, waits for them, and re-layouts  1.56 us
  transfers between devices with their start and end apart: 2, of which 0 were waited for; matrix products, arithmetic and copies ran while one was open for 0% of the time, Pallas kernels for 25%

commit v1 on v0

v1 whole, which is shorter than its diff:
```python
import functools

import jax
import jax.numpy as jnp
from jax import lax
from jax.experimental import pallas as pl
from jax.experimental.pallas import tpu as pltpu
from jax.sharding import PartitionSpec as P

F32 = jnp.float32
BF16 = jnp.bfloat16
VMEM_LIMIT = 56 * 1024 * 1024
SURFACE = 4
TILE = 128
ROWS = 8
COPIES = 64


def lane(value, k):
    return jnp.broadcast_to(value[:, k : k + 1], value.shape)


def row(value, k):
    return jnp.broadcast_to(value[k : k + 1, :], value.shape)


def exact_dot(a, b, dims):
    return lax.dot_general(
        a, b, (dims, ((), ())), precision=lax.Precision.HIGHEST, preferred_element_type=F32
    )


def bf_dot(a, b, dims):
    return lax.dot_general(a, b, (dims, ((), ())), preferred_element_type=F32)


NN = ((1,), (0,))
TN = ((0,), (0,))
NT = ((1,), (1,))


def factor_tile(a_rows, x_rows, between):
    panels = len(a_rows)
    for g in range(panels):
        here, here_x = a_rows[g], x_rows[g]
        columns = [lane(here, ROWS * g + j) for j in range(ROWS)]
        s = {(i, j): row(columns[j], i) for j in range(ROWS) for i in range(j, ROWS)}
        r = []
        for k in range(ROWS):
            r.append(lax.rsqrt(s[k, k]))
            for i in range(k + 1, ROWS):
                s[i, k] = s[i, k] * r[k]
            for j in range(k + 1, ROWS):
                for i in range(j, ROWS):
                    s[i, j] = s[i, j] - s[i, k] * s[j, k]
        z, zx = [], []
        for k in range(ROWS):
            top, top_x = row(here, k), row(here_x, k)
            for m in range(k):
                top = top - s[k, m] * z[m]
                top_x = top_x - s[k, m] * zx[m]
            z.append(top * r[k])
            zx.append(top_x * r[k])
        sub = lax.broadcasted_iota(jnp.int32, here.shape, 0)
        packed_x = zx[0]
        for k in range(1, ROWS):
            packed_x = jnp.where(sub == k, zx[k], packed_x)
        x_rows[g] = packed_x
        for i in range(g + 1, panels):
            below = []
            for k in range(ROWS):
                c = lane(a_rows[i], ROWS * g + k)
                for m in range(k):
                    c = c - below[m] * s[k, m]
                below.append(c * r[k])
            a_rows[i] = a_rows[i] - sum(below[k] * z[k] for k in range(ROWS))
            x_rows[i] = x_rows[i] - sum(below[k] * zx[k] for k in range(ROWS))
        between(g)
    return x_rows


def gram_kernel(u_hbm, gram_ref, u_ref, sems):
    chunks = sems.shape[0]
    step = u_ref.shape[0] // chunks
    copies = [
        pltpu.make_async_copy(
            u_hbm.at[pl.ds(c * step, step)], u_ref.at[pl.ds(c * step, step)], sems.at[c]
        )
        for c in range(chunks)
    ]
    for copy in copies:
        copy.start()
    for c, copy in enumerate(copies):
        copy.wait()
        part = u_ref[pl.ds(c * step, step), :]
        product = bf_dot(part, part, TN)
        gram_ref[...] = product if c == 0 else gram_ref[...] + product


def add_product(j, live, acc_ref, source_ref, blocks_ref, rows_ref, cols_ref, row_base):
    to = pl.multiple_of((rows_ref[j] - row_base) * TILE, TILE)
    at = pl.multiple_of(cols_ref[j] * TILE, TILE)
    product = bf_dot(blocks_ref[j], source_ref[pl.ds(at, TILE), :], NN)
    if live is not None:
        product = jnp.where(live, product, 0.0)
    acc_ref[pl.ds(to, TILE), :] = acc_ref[pl.ds(to, TILE), :] + product


def factor_kernel(
    rows_ref,
    cols_ref,
    crows_ref,
    ccols_ref,
    gram_in,
    next_ref,
    u_hbm,
    blocks_hbm,
    cblocks_hbm,
    f_ref,
    yt_ref,
    spread_hbm,
    gram_ref,
    inv_ref,
    x_ref,
    u_ref,
    blocks_ref,
    cblocks_ref,
    acc_ref,
    spread_ref,
    hop_ref,
    sems,
):
    orbitals, modes = u_ref.shape
    surface = hop_ref.shape[0]
    copies = [
        pltpu.make_async_copy(u_hbm, u_ref, sems.at[0]),
        pltpu.make_async_copy(blocks_hbm, blocks_ref, sems.at[1]),
        pltpu.make_async_copy(cblocks_hbm, cblocks_ref, sems.at[2]),
    ]
    for copy in copies:
        copy.start()
    acc_ref[...] = jnp.zeros_like(acc_ref)
    hop_ref[...] = jnp.zeros_like(hop_ref)
    inv_ref[...] = jnp.zeros_like(inv_ref)
    gram_ref[...] = gram_in[...]
    for copy in copies:
        copy.wait()

    tiles = modes // TILE
    panels = TILE // ROWS

    def onsite_product(j, live):
        add_product(j, live, acc_ref, u_ref, blocks_ref, rows_ref, cols_ref, 0)

    def coupling_product(j, live):
        base = (orbitals - surface) // TILE
        add_product(j, live, hop_ref, next_ref, cblocks_ref, crows_ref, ccols_ref, base)

    def one_tile(b, carry):
        here = pl.ds(pl.multiple_of(b * TILE, TILE), TILE)
        tile = gram_ref[here, here]
        sub = lax.broadcasted_iota(jnp.int32, (ROWS, TILE), 0)
        col = lax.broadcasted_iota(jnp.int32, (ROWS, TILE), 1)
        a_rows = [tile[ROWS * g : ROWS * (g + 1), :] for g in range(panels)]
        x_rows = [(col == sub + ROWS * g).astype(F32) for g in range(panels)]

        def between(g):
            for count, work in (
                (blocks_ref.shape[0], onsite_product),
                (cblocks_ref.shape[0], coupling_product),
            ):
                share = -(-count // tiles)
                for t in range(share):
                    if t * panels // share == g:
                        j = b * share + t
                        if share * tiles == count:
                            work(j, None)
                        else:
                            work(jnp.minimum(j, count - 1), j < count)

        x_rows = factor_tile(a_rows, x_rows, between)
        for g in range(panels):
            x_ref[ROWS * g : ROWS * (g + 1), :] = x_rows[g]
        for static_b in range(tiles):

            @pl.when(b == static_b)
            def _():
                lo, hi = static_b * TILE, (static_b + 1) * TILE
                x = x_ref[...]
                inv_ref[lo:hi, lo:hi] = x
                if static_b:
                    inv_ref[lo:hi, :lo] = exact_dot(x, inv_ref[lo:hi, :lo], NN)
                if static_b + 1 < tiles:
                    upper = exact_dot(x, gram_ref[lo:hi, hi:], NN)
                    gram_ref[hi:, hi:] = gram_ref[hi:, hi:] - exact_dot(upper, upper, TN)
                    inv_ref[hi:, :hi] = inv_ref[hi:, :hi] - exact_dot(
                        upper, inv_ref[lo:hi, :hi], TN
                    )

        return carry

    lax.fori_loop(0, tiles, one_tile, 0)
    spread_ref[...] = acc_ref[...].astype(BF16)
    out = pltpu.make_async_copy(spread_ref, spread_hbm, sems.at[3])
    out.start()
    factor = inv_ref[...].T.astype(BF16)
    f_ref[...] = factor
    high, low = split(bf_dot(u_ref[orbitals - surface :, :], hop_ref[...].astype(BF16), TN))
    yt_ref[...] = (bf_dot(high, factor, TN) + bf_dot(low, factor, TN)).astype(BF16)
    out.wait()


def couple_kernel(yt_ref, next_f_ref, f_ref, last_yt_ref, order_ref, right_ref, left_ref):
    right_ref[...] = bf_dot(yt_ref[...], next_f_ref[...], TN)
    left_ref[...] = bf_dot(f_ref[...], last_yt_ref[...], TN)


def split(value):
    high = value.astype(BF16)
    return high, (value - high.astype(F32)).astype(BF16)


def onsite_kernel(place_ref, u_hbm, spread_hbm, f_ref, steps_ref, out_ref, u_ref, spread_ref, w_ref, sems):
    modes = f_ref.shape[0]
    chunks = sems.shape[0]
    step = u_ref.shape[0] // chunks
    copies = []
    for c in range(chunks):
        part = pl.ds(c * step, step)
        copies.append(
            [
                pltpu.make_async_copy(u_hbm.at[part], u_ref.at[part], sems.at[c, 0]),
                pltpu.make_async_copy(spread_hbm.at[part], spread_ref.at[part], sems.at[c, 1]),
            ]
        )
    for pair in copies:
        for copy in pair:
            copy.start()
    for c, pair in enumerate(copies):
        for copy in pair:
            copy.wait()
        part = pl.ds(c * step, step)
        product = bf_dot(u_ref[part, :], spread_ref[part, :], TN)
        w_ref[...] = product if c == 0 else w_ref[...] + product
    w = w_ref[...]
    w = w + w.T
    f = f_ref[...]
    high, low = split(w)
    half = bf_dot(high, f, NN) + bf_dot(low, f, NN)
    high, low = split(half)
    full = bf_dot(f, high, TN) + bf_dot(f, low, TN)
    steps = steps_ref[...]
    index = lax.broadcasted_iota(jnp.int32, steps.shape, 0)
    used = (index <= place_ref[0] * COPIES) & (index % COPIES == 0)
    potential = jnp.sum(jnp.where(used, steps, 0.0), axis=0, keepdims=True)[:, :1]
    i = lax.broadcasted_iota(jnp.int32, (modes, modes), 0)
    j = lax.broadcasted_iota(jnp.int32, (modes, modes), 1)
    out_ref[...] = full + jnp.where(i == j, potential, 0.0)


def struct(shape, dtype):
    return jax.ShapeDtypeStruct(shape, dtype)


ANY = pl.BlockSpec(memory_space=pl.ANY)
INTO_VMEM = pl.BlockSpec(memory_space=pltpu.VMEM)
INTO_SMEM = pl.BlockSpec(memory_space=pltpu.SMEM)
PARAMS = pltpu.CompilerParams(vmem_limit_bytes=VMEM_LIMIT)


def passed_along(block, axis, distance):
    devices = range(lax.axis_size(axis))
    route = [(i - distance, i) for i in devices if i - distance in devices]
    return lax.ppermute(block, axis, route)


def cost(flops, moved):
    return pl.CostEstimate(flops=flops, bytes_accessed=moved, transcendentals=0)


def shards(
    trial_modes,
    onsite_blocks,
    onsite_rows,
    onsite_cols,
    coupling_blocks,
    coupling_rows,
    coupling_cols,
    potential_step,
):
    u = trial_modes[0]
    orbitals, modes = u.shape
    surface = SURFACE * TILE
    count = onsite_blocks.shape[1]
    links = coupling_blocks.shape[1]
    steps = lax.all_gather(
        lax.optimization_barrier(jnp.broadcast_to(potential_step[:, None], (COPIES, TILE))),
        "slab",
        tiled=True,
    )
    place = lax.axis_index("slab").astype(jnp.int32).reshape(1)
    next_head = passed_along(u[:surface], "slab", -1)

    gram = pl.pallas_call(
        gram_kernel,
        out_shape=struct((modes, modes), F32),
        in_specs=[ANY],
        out_specs=INTO_VMEM,
        scratch_shapes=[pltpu.VMEM((orbitals, modes), BF16), pltpu.SemaphoreType.DMA((8,))],
        compiler_params=PARAMS,
        cost_estimate=cost(2 * orbitals * modes * modes, orbitals * modes * 2),
        name="gram",
    )(u)

    factor, yt, spread = pl.pallas_call(
        factor_kernel,
        out_shape=(
            struct((modes, modes), BF16),
            struct((modes, modes), BF16),
            struct((orbitals, modes), BF16),
        ),
        in_specs=[INTO_SMEM] * 4 + [INTO_VMEM] * 2 + [ANY] * 3,
        out_specs=(INTO_VMEM, INTO_VMEM, ANY),
        scratch_shapes=[
            pltpu.VMEM((modes, modes), F32),
            pltpu.VMEM((modes, modes), F32),
            pltpu.VMEM((TILE, TILE), F32),
            pltpu.VMEM((orbitals, modes), BF16),
            pltpu.VMEM((count, TILE, TILE), BF16),
            pltpu.VMEM((links, TILE, TILE), BF16),
            pltpu.VMEM((orbitals, modes), F32),
            pltpu.VMEM((orbitals, modes), BF16),
            pltpu.VMEM((surface, modes), F32),
            pltpu.SemaphoreType.DMA((4,)),
        ],
        compiler_params=PARAMS,
        cost_estimate=cost(8 * orbitals * modes * modes, orbitals * modes * 2),
        name="factor",
    )(
        onsite_rows[0],
        onsite_cols[0],
        coupling_rows[0],
        coupling_cols[0],
        gram,
        next_head,
        u,
        onsite_blocks[0],
        coupling_blocks[0],
    )
    next_factor = passed_along(factor, "slab", -1)
    last_yt = passed_along(yt, "slab", 1)

    onsite = pl.pallas_call(
        onsite_kernel,
        out_shape=struct((modes, modes), F32),
        in_specs=[INTO_SMEM, ANY, ANY, INTO_VMEM, INTO_VMEM],
        out_specs=INTO_VMEM,
        scratch_shapes=[
            pltpu.VMEM((orbitals, modes), BF16),
            pltpu.VMEM((orbitals, modes), BF16),
            pltpu.VMEM((modes, modes), F32),
            pltpu.SemaphoreType.DMA((8, 2)),
        ],
        compiler_params=PARAMS,
        cost_estimate=cost(8 * modes * modes * modes, 8 * modes * modes * 2),
        name="onsite",
    )(place, u, spread, factor, steps)

    right, left = pl.pallas_call(
        couple_kernel,
        out_shape=(struct((modes, modes), F32),) * 2,
        in_specs=[INTO_VMEM] * 4 + [ANY],
        out_specs=(INTO_VMEM,) * 2,
        compiler_params=PARAMS,
        cost_estimate=cost(4 * modes * modes * modes, 8 * modes * modes * 2),
        name="couple",
    )(yt, next_factor, factor, last_yt, onsite)
    return (onsite[None], right[None], left[None])


def solution(mesh):
    return jax.shard_map(
        shards,
        mesh=mesh,
        in_specs=(
            P(("groups", "slab"), None, None),
            P(("groups", "slab"), None, None, None),
            P(("groups", "slab"), None),
            P(("groups", "slab"), None),
            P(("groups", "slab"), None, None, None),
            P(("groups", "slab"), None),
            P(("groups", "slab"), None),
            P(("groups", "slab")),
        ),
        out_specs=(
            P(("groups", "slab"), None, None),
            P(("groups", "slab"), None, None),
            P(("groups", "slab"), None, None),
        ),
        check_vma=False,
    )
```

time: 72.2 us -> 76.5 us (1.060)
  Pallas kernels: 40.8 us -> 37 us
  waiting for transfers between devices: 0.01 us -> 3.76 us
  local copies, waits for them, and re-layouts: 1.56 us -> 3.18 us
  blocking collectives: 21.7 us -> 23.3 us
  starting transfers between devices: 6.45 us -> 7.53 us
    pallas_call x2, Pallas kernels: 15.4 us -> 6.89 us  [the longest x1 4.26 us: shards(): pl.pallas_call(gram_kernel, out_shape=struct((modes, modes), F32), in_spe...]
    pallas_call x1, Pallas kernels: 18.9 us -> 23.5 us  [shards(): pl.pallas_call(factor_kernel, out_shape=(struct((modes, modes), BF16), st...]
    ppermute x2 -> x3, waiting for transfers between devices: 0.01 us -> 3.76 us  [passed_along(): return lax.ppermute(block, axis, route)]
    all_gather x1, blocking collectives: 21.7 us -> 23.3 us  [shards(): lax.all_gather(lax.optimization_barrier(jnp.broadcast_to(potential_step[:...]
    ppermute x2 -> x3, starting transfers between devices: 6.45 us -> 7.53 us  [passed_along(): return lax.ppermute(block, axis, route)]
    slice x0 -> x1, local copies, waits for them, and re-layouts: none -> 1.04 us  [shards(): next_head = passed_along(u[:surface], 'slab', -1)]
    unnamed x3 -> x6, local copies, waits for them, and re-layouts: 1.56 us -> 2.14 us
  transfers between devices with their start and end apart: 2 -> 3, of which waited for: 0 -> 1; matrix products, arithmetic and copies ran while one was open for 0% -> 0% of each run, Pallas kernels for 25% -> 14%
where the time goes in v1:
time: 76.5 us; the launch traced here: 76.1 us
  Pallas kernels  37 us (48%)
  blocking collectives  23.3 us (30%)
  starting transfers between devices  7.53 us (10%)
  waiting for transfers between devices  3.76 us (5%)
  local copies, waits for them, and re-layouts  3.18 us (4%)
  between operations  1.37 us (2%)
    pallas_call x1, Pallas kernels, shards(): pl.pallas_call(factor_kernel, out_shape=(struct((modes, modes), BF16), st...  23.5 us
    all_gather x1, blocking collectives, shards(): lax.all_gather(lax.optimization_barrier(jnp.broadcast_to(potential_step[:...  23.3 us
    ppermute x3, starting transfers between devices, passed_along(): return lax.ppermute(block, axis, route)  7.53 us
    pallas_call x1, Pallas kernels, shards(): pl.pallas_call(onsite_kernel, out_shape=struct((modes, modes), F32), in_s...  6.65 us
    pallas_call x1, Pallas kernels, shards(): pl.pallas_call(gram_kernel, out_shape=struct((modes, modes), F32), in_spe...  4.26 us
    ppermute x3, waiting for transfers between devices, passed_along(): return lax.ppermute(block, axis, route)  3.76 us
    pallas_call x1, Pallas kernels, shards(): pl.pallas_call(couple_kernel, out_shape=(struct((modes, modes), F32),) *...  2.63 us
    unnamed x6, local copies, waits for them, and re-layouts  2.14 us
  transfers between devices with their start and end apart: 3, of which 1 were waited for; matrix products, arithmetic and copies ran while one was open for 0% of the time, Pallas kernels for 14%

profile of v1, /device:TPU:1, one launch (start us, length us, event | category | flops | bytes accessed | tf_op | source)
XLA Modules:
  0.0 76.1 jit_solution(16727726964908426186)
XLA Ops:
  0.6 1.0 %slice_bitcast_fusion = bf16[512,384]{1,0:T(8,128)(2,1)S(1)} fusion(bf16[1,4096,384]{2,1,0:T(8,128)(2,1)} %param.8), kind=kLoop, calls=%fused_computation | loop fusion | bytes 786432 | tf_op jit(solution)/shard_map/slice | solution.py:302
  1.7 2.0 %collective-permute-start = (bf16[512,384]{1,0:T(8,128)(2,1)S(1)}, bf16[512,384]{1,0:T(8,128)(2,1)S(1)}, u32[]{:S(2)}, u32[]{:S(2)}) collective-permute-start(bf16[512,384]{1,0:T(8,128)(2,1)S(1)} %slice_bitcast_fusion), channel_id=1, source_target_pairs={{1,0},{2,1},{3,2},{4,3},{5,4},{6,5},{7,6},{8,7},{9,8},{10,9},{11,1... | collective-permute-start | bytes 1179656 | tf_op jit(solution)/shard_map/ppermute | solution.py:274
  3.6 4.3 %gram.1.gram_in = f32[384,384]{1,0:T(8,128)} custom-call(bf16[4096,384]{1,0:T(8,128)(2,1)} %bitcast.15), custom_call_target="tpu_custom_call" | custom-call | flops 1207959552 | bytes 3145728 | tf_op jit(solution)/shard_map/gram/pallas_call | solution.py:304
  7.9 3.8 %collective-permute-done.next_ref = bf16[512,384]{1,0:T(8,128)(2,1)S(1)} collective-permute-done((bf16[512,384]{1,0:T(8,128)(2,1)S(1)}, bf16[512,384]{1,0:T(8,128)(2,1)S(1)}, u32[]{:S(2)}, u32[]{:S(2)}) %collective-permute-start) | collective-permute-done | bytes 393248 | tf_op jit(solution)/shard_map/ppermute | solution.py:274
  11.7 0.0 copy-start.2
  11.7 0.7 copy-done.2
  12.4 23.5 %factor.1 = (bf16[384,384]{1,0:T(8,128)(2,1)}, bf16[384,384]{1,0:T(8,128)(2,1)}, bf16[4096,384]{1,0:T(8,128)(2,1)}) custom-call(s32[96]{0:T(128)} %bitcast.23, s32[96]{0:T(128)} %bitcast.24, s32[16]{0:T(128)} %bitcast.25, s32[16]{0:T(128)} %bitcast.26, f32[384,384]{1,0:T(8,128)} %gram.1.gram_in, bf16[512,384]{1,0:T(8,128)(2,1)} %copy-done.2, ...), custom_call_target="tpu_custom_call" | custom-call | flops 4831838208 | bytes 3145728 | tf_op jit(solution)/shard_map/factor/pallas_call | solution.py:315
  35.9 1.9 %collective-permute-start.1 = (bf16[384,384]{1,0:T(8,128)(2,1)}, bf16[384,384]{1,0:T(8,128)(2,1)S(1)}, u32[]{:S(2)}, u32[]{:S(2)}) collective-permute-start(bf16[384,384]{1,0:T(8,128)(2,1)} %get-tuple-element.9.f_ref), channel_id=1, source_target_pairs={{1,0},{2,1},{3,2},{4,3},{5,4},{6,5},{7,6},{8,7},{9,8},{10,9},{11,1... | collective-permute-start | bytes 884744 | tf_op jit(solution)/shard_map/ppermute | solution.py:274
  37.8 3.6 %collective-permute-start.2 = (bf16[384,384]{1,0:T(8,128)(2,1)}, bf16[384,384]{1,0:T(8,128)(2,1)S(1)}, u32[]{:S(2)}, u32[]{:S(2)}) collective-permute-start(bf16[384,384]{1,0:T(8,128)(2,1)} %get-tuple-element.10.yt_ref), channel_id=1, source_target_pairs={{0,1},{1,2},{2,3},{3,4},{4,5},{5,6},{6,7},{7,8},{8,9},{9,10},{10,1... | collective-permute-start | bytes 884744 | tf_op jit(solution)/shard_map/ppermute | solution.py:274
  42.1 23.3 %all_gather.3.steps_ref = f32[1024,128]{1,0:T(8,128)} all-gather(f32[64,128]{1,0:T(8,128)S(1)} %broadcast_in_dim.18), channel_id=1, replica_groups=mesh['groups'=2,'slab'=16] {'slab'}, dimensions={0}, use_global_device_ids=true | all-gather | bytes 557056 | tf_op jit(solution)/shard_map/all_gather | solution.py:296
  65.4 6.6 %onsite.1.order_ref = f32[384,384]{1,0:T(8,128)} custom-call(s32[1]{0:T(128)} %bitcast.place_ref, bf16[4096,384]{1,0:T(8,128)(2,1)} %bitcast.17, bf16[4096,384]{1,0:T(8,128)(2,1)} %get-tuple-element.8.spread_hbm, bf16[384,384]{1,0:T(8,128)(2,1)} %get-tuple-element.9.f_ref, f32[1024,128]{1,0:T(8,128)} %all_gather.3.steps_ref), custom_call_target="tpu_custom_call" | custom-call | flops 452984832 | bytes 2359296 | tf_op jit(solution)/shard_map/onsite/pallas_call | solution.py:353
  72.1 0.0 collective-permute-done.1.next_f_ref
  72.1 0.0 copy-start
  72.1 0.0 collective-permute-done.2.last_yt_ref
  72.1 0.7 copy-done
  72.8 0.0 copy-start.1
  72.8 0.7 copy-done.1
  73.5 2.6 %couple.1 = (f32[384,384]{1,0:T(8,128)}, f32[384,384]{1,0:T(8,128)}) custom-call(bf16[384,384]{1,0:T(8,128)(2,1)} %get-tuple-element.10.yt_ref, bf16[384,384]{1,0:T(8,128)(2,1)} %copy-done, bf16[384,384]{1,0:T(8,128)(2,1)} %get-tuple-element.9.f_ref, bf16[384,384]{1,0:T(8,128)(2,1)} %copy-done.1, f32[384,384]{1,0:T(8,128)} %onsite.1.order_ref), custom_call_target="tpu_custom_call" | custom-call | flops 226492416 | bytes 2359296 | tf_op jit(solution)/shard_map/couple/pallas_call | solution.py:369
  (1 shorter events, 0.0 us)
Async XLA Ops:
  1.7 10.0 %collective-permute-start = (bf16[512,384]{1,0:T(8,128)(2,1)S(1)}, bf16[512,384]{1,0:T(8,128)(2,1)S(1)}, u32[]{:S(2)}, u32[]{:S(2)}) collective-permute-start(bf16[512,384]{1,0:T(8,128)(2,1)S(1)} %slice_bitcast_fusion), channel_id=1, source_target_pairs={{1,0},{2,1},{3,2},{4,3},{5,4},{6,5},{7,6},{8,7},{9,8},{10,9},{11,1... | collective-permute-start | bytes 1179656 | tf_op jit(solution)/shard_map/ppermute | solution.py:274
  11.7 0.7 copy-start.2
  35.9 36.2 %collective-permute-start.1 = (bf16[384,384]{1,0:T(8,128)(2,1)}, bf16[384,384]{1,0:T(8,128)(2,1)S(1)}, u32[]{:S(2)}, u32[]{:S(2)}) collective-permute-start(bf16[384,384]{1,0:T(8,128)(2,1)} %get-tuple-element.9.f_ref), channel_id=1, source_target_pairs={{1,0},{2,1},{3,2},{4,3},{5,4},{6,5},{7,6},{8,7},{9,8},{10,9},{11,1... | collective-permute-start | bytes 884744 | tf_op jit(solution)/shard_map/ppermute | solution.py:274
  37.8 34.2 %collective-permute-start.2 = (bf16[384,384]{1,0:T(8,128)(2,1)}, bf16[384,384]{1,0:T(8,128)(2,1)S(1)}, u32[]{:S(2)}, u32[]{:S(2)}) collective-permute-start(bf16[384,384]{1,0:T(8,128)(2,1)} %get-tuple-element.10.yt_ref), channel_id=1, source_target_pairs={{0,1},{1,2},{2,3},{3,4},{4,5},{5,6},{6,7},{7,8},{8,9},{9,10},{10,1... | collective-permute-start | bytes 884744 | tf_op jit(solution)/shard_map/ppermute | solution.py:274
  72.1 0.7 copy-start
  72.8 0.7 copy-start.1

commit v2 on v1

v2 whole, which is shorter than its diff:
```python
import functools

import jax
import jax.numpy as jnp
from jax import lax
from jax.experimental import pallas as pl
from jax.experimental.pallas import tpu as pltpu
from jax.sharding import PartitionSpec as P

F32 = jnp.float32
BF16 = jnp.bfloat16
MIB = 1024 * 1024
SURFACE = 4
TILE = 128
ROWS = 8


def lane(value, k):
    return jnp.broadcast_to(value[:, k : k + 1], value.shape)


def row(value, k):
    return jnp.broadcast_to(value[k : k + 1, :], value.shape)


def exact_dot(a, b, dims):
    return lax.dot_general(
        a, b, (dims, ((), ())), precision=lax.Precision.HIGHEST, preferred_element_type=F32
    )


def bf_dot(a, b, dims):
    return lax.dot_general(a, b, (dims, ((), ())), preferred_element_type=F32)


NN = ((1,), (0,))
TN = ((0,), (0,))
NT = ((1,), (1,))


def factor_tile(a_rows, x_rows, between):
    panels = len(a_rows)
    for g in range(panels):
        here, here_x = a_rows[g], x_rows[g]
        columns = [lane(here, ROWS * g + j) for j in range(ROWS)]
        s = {(i, j): row(columns[j], i) for j in range(ROWS) for i in range(j, ROWS)}
        low, r = {}, []
        for p in range(0, ROWS, 2):
            q = p + 1
            a, b, c = s[p, p], s[q, p], s[q, q]
            root = lax.rsqrt(a * c - b * b)
            r_p = lax.rsqrt(a)
            r_q = a * r_p * root
            inverse = root * root
            r += [r_p, r_q]
            low[q, p] = b * r_p
            side = {}
            for i in range(q + 1, ROWS):
                first, second = s[i, p], s[i, q]
                low[i, p] = first * r_p
                low[i, q] = (second - low[i, p] * low[q, p]) * r_q
                side[i] = (c * first - b * second, a * second - b * first)
            for j in range(q + 1, ROWS):
                for i in range(j, ROWS):
                    both = side[j][0] * s[i, p] + side[j][1] * s[i, q]
                    s[i, j] = s[i, j] - both * inverse
        z, zx = [], []
        for k in range(ROWS):
            top, top_x = row(here, k), row(here_x, k)
            for m in range(k):
                top = top - low[k, m] * z[m]
                top_x = top_x - low[k, m] * zx[m]
            z.append(top * r[k])
            zx.append(top_x * r[k])
        sub = lax.broadcasted_iota(jnp.int32, here.shape, 0)
        packed, packed_x = z[0], zx[0]
        for k in range(1, ROWS):
            packed = jnp.where(sub == k, z[k], packed)
            packed_x = jnp.where(sub == k, zx[k], packed_x)
        x_rows[g] = packed_x
        if g + 2 < panels:
            turned = packed.T
        for i in range(g + 1, panels):
            below = []
            for k in range(ROWS):
                if i == g + 1:
                    column = lane(a_rows[i], ROWS * g + k)
                    for m in range(k):
                        column = column - below[m] * low[k, m]
                    below.append(column * r[k])
                else:
                    below.append(
                        jnp.broadcast_to(turned[ROWS * i : ROWS * (i + 1), k : k + 1], here.shape)
                    )
            for k in range(ROWS):
                a_rows[i] = a_rows[i] - below[k] * z[k]
                x_rows[i] = x_rows[i] - below[k] * zx[k]
        between(g)
    return x_rows


def add_product(j, live, acc_ref, source_ref, blocks_ref, rows_ref, cols_ref, row_base):
    to = pl.multiple_of((rows_ref[j] - row_base) * TILE, TILE)
    at = pl.multiple_of(cols_ref[j] * TILE, TILE)
    product = bf_dot(blocks_ref[j], source_ref[pl.ds(at, TILE), :], NN)
    if live is not None:
        product = jnp.where(live, product, 0.0)
    acc_ref[pl.ds(to, TILE), :] = acc_ref[pl.ds(to, TILE), :] + product


def factor_kernel(
    rows_ref,
    cols_ref,
    u_hbm,
    blocks_hbm,
    f_ref,
    turned_hbm,
    spread_hbm,
    gram_ref,
    inv_ref,
    x_ref,
    u_ref,
    turned_ref,
    blocks_ref,
    acc_ref,
    spread_ref,
    sems,
    u_sems,
):
    orbitals, modes = u_ref.shape
    chunks = u_sems.shape[0]
    step = orbitals // chunks
    copies = [
        pltpu.make_async_copy(
            u_hbm.at[pl.ds(c * step, step)], u_ref.at[pl.ds(c * step, step)], u_sems.at[c]
        )
        for c in range(chunks)
    ]
    blocks_copy = pltpu.make_async_copy(blocks_hbm, blocks_ref, sems.at[0])
    for copy in copies:
        copy.start()
    blocks_copy.start()
    acc_ref[...] = jnp.zeros_like(acc_ref)
    inv_ref[...] = jnp.zeros_like(inv_ref)
    for c, copy in enumerate(copies):
        copy.wait()
        part = u_ref[c * step : (c + 1) * step, :]
        turned = part.T
        turned_ref[:, c * step : (c + 1) * step] = turned
        product = bf_dot(turned, part, NN)
        gram_ref[...] = product if c == 0 else gram_ref[...] + product
    turned_copy = pltpu.make_async_copy(turned_ref, turned_hbm, sems.at[1])
    turned_copy.start()
    gram = gram_ref[...]
    on_diagonal = lax.broadcasted_iota(jnp.int32, gram.shape, 0) == lax.broadcasted_iota(
        jnp.int32, gram.shape, 1
    )
    diagonal = jnp.where(on_diagonal, gram, 0.0)
    across = lax.rsqrt(jnp.sum(diagonal, axis=0, keepdims=True))
    down = lax.rsqrt(jnp.sum(diagonal, axis=1, keepdims=True))
    gram_ref[...] = gram * across * down
    blocks_copy.wait()

    tiles = modes // TILE
    panels = TILE // ROWS
    count = blocks_ref.shape[0]
    share = -(-count // tiles)

    def one_tile(b, carry):
        here = pl.ds(pl.multiple_of(b * TILE, TILE), TILE)
        tile = gram_ref[here, here]
        sub = lax.broadcasted_iota(jnp.int32, (ROWS, TILE), 0)
        col = lax.broadcasted_iota(jnp.int32, (ROWS, TILE), 1)
        a_rows = [tile[ROWS * g : ROWS * (g + 1), :] for g in range(panels)]
        x_rows = [(col == sub + ROWS * g).astype(F32) for g in range(panels)]

        def between(g):
            for t in range(share):
                if t * panels // share == g:
                    j = b * share + t
                    live = None
                    if share * tiles != count:
                        live = j < count
                        j = jnp.minimum(j, count - 1)
                    add_product(j, live, acc_ref, u_ref, blocks_ref, rows_ref, cols_ref, 0)

        x_rows = factor_tile(a_rows, x_rows, between)
        for g in range(panels):
            x_ref[ROWS * g : ROWS * (g + 1), :] = x_rows[g]
        for static_b in range(tiles):

            @pl.when(b == static_b)
            def _():
                lo, hi = static_b * TILE, (static_b + 1) * TILE
                x = x_ref[...]
                inv_ref[lo:hi, lo:hi] = x
                if static_b:
                    inv_ref[lo:hi, :lo] = exact_dot(x, inv_ref[lo:hi, :lo], NN)
                if static_b + 1 < tiles:
                    upper = exact_dot(x, gram_ref[lo:hi, hi:], NN)
                    gram_ref[hi:, hi:] = gram_ref[hi:, hi:] - exact_dot(upper, upper, TN)
                    inv_ref[hi:, :hi] = inv_ref[hi:, :hi] - exact_dot(
                        upper, inv_ref[lo:hi, :hi], TN
                    )

        return carry

    lax.fori_loop(0, tiles, one_tile, 0)
    spread_ref[...] = acc_ref[...].astype(BF16)
    spread_copy = pltpu.make_async_copy(spread_ref, spread_hbm, sems.at[2])
    spread_copy.start()
    f_ref[...] = (inv_ref[...] * across).T.astype(BF16)
    turned_copy.wait()
    spread_copy.wait()


def link_kernel(
    rows_ref, cols_ref, next_ref, blocks_ref, u_hbm, f_ref, yt_ref, hop_ref, tail_ref, sem
):
    surface = tail_ref.shape[0]
    base = u_hbm.shape[0] - surface
    copy = pltpu.make_async_copy(u_hbm.at[pl.ds(base, surface)], tail_ref, sem.at[0])
    copy.start()
    hop_ref[...] = jnp.zeros_like(hop_ref)
    for j in range(blocks_ref.shape[0]):
        add_product(j, None, hop_ref, next_ref, blocks_ref, rows_ref, cols_ref, base // TILE)
    copy.wait()
    high, low = split(bf_dot(tail_ref[...], hop_ref[...].astype(BF16), TN))
    factor = f_ref[...]
    yt_ref[...] = (bf_dot(high, factor, TN) + bf_dot(low, factor, TN)).astype(BF16)


def couple_kernel(yt_ref, next_f_ref, f_ref, last_yt_ref, order_ref, right_ref, left_ref):
    right_ref[...] = bf_dot(yt_ref[...], next_f_ref[...], TN)
    left_ref[...] = bf_dot(f_ref[...], last_yt_ref[...], TN)


def split(value):
    high = value.astype(BF16)
    return high, (value - high.astype(F32)).astype(BF16)


def onsite_kernel(
    place_ref, turned_hbm, spread_hbm, f_ref, steps_ref, order_ref, out_ref, turned_ref, spread_ref, w_ref, sems
):
    modes = f_ref.shape[0]
    chunks = sems.shape[0]
    step = spread_ref.shape[0] // chunks
    copies = []
    for c in range(chunks):
        part = pl.ds(c * step, step)
        copies.append(
            [
                pltpu.make_async_copy(turned_hbm.at[:, part], turned_ref.at[:, part], sems.at[c, 0]),
                pltpu.make_async_copy(spread_hbm.at[part], spread_ref.at[part], sems.at[c, 1]),
            ]
        )
    for pair in copies:
        for copy in pair:
            copy.start()
    for c, pair in enumerate(copies):
        for copy in pair:
            copy.wait()
        part = slice(c * step, (c + 1) * step)
        product = bf_dot(turned_ref[:, part], spread_ref[part, :], NN)
        w_ref[...] = product if c == 0 else w_ref[...] + product
    w = w_ref[...]
    w = w + w.T
    f = f_ref[...]
    high, low = split(w)
    half = bf_dot(high, f, NN) + bf_dot(low, f, NN)
    high, low = split(half)
    full = bf_dot(f, high, TN) + bf_dot(f, low, TN)
    steps = steps_ref[...]
    reached = lax.broadcasted_iota(jnp.int32, steps.shape, 0) <= place_ref[0]
    potential = jnp.sum(jnp.where(reached, steps, 0.0), axis=0, keepdims=True)[:, :1]
    i = lax.broadcasted_iota(jnp.int32, (modes, modes), 0)
    j = lax.broadcasted_iota(jnp.int32, (modes, modes), 1)
    out_ref[...] = full + jnp.where(i == j, potential, 0.0)


def struct(shape, dtype):
    return jax.ShapeDtypeStruct(shape, dtype)


ANY = pl.BlockSpec(memory_space=pl.ANY)
INTO_VMEM = pl.BlockSpec(memory_space=pltpu.VMEM)
INTO_SMEM = pl.BlockSpec(memory_space=pltpu.SMEM)


def params(mebibytes):
    return pltpu.CompilerParams(vmem_limit_bytes=mebibytes * MIB)


def passed_along(block, axis, distance):
    devices = range(lax.axis_size(axis))
    route = [(i - distance, i) for i in devices if i - distance in devices]
    return lax.ppermute(block, axis, route)


def cost(flops, moved):
    return pl.CostEstimate(flops=flops, bytes_accessed=moved, transcendentals=0)


def shards(
    trial_modes,
    onsite_blocks,
    onsite_rows,
    onsite_cols,
    coupling_blocks,
    coupling_rows,
    coupling_cols,
    potential_step,
):
    u = trial_modes[0]
    orbitals, modes = u.shape
    surface = SURFACE * TILE
    count = onsite_blocks.shape[1]
    links = coupling_blocks.shape[1]
    place = lax.axis_index("slab").astype(jnp.int32).reshape(1)
    next_head = passed_along(u[:surface], "slab", -1)
    slabs = lax.axis_size("slab")
    steps = lax.all_to_all(
        jnp.broadcast_to(potential_step[:, None], (slabs, TILE)), "slab", 0, 0, tiled=True
    )

    factor, turned, spread = pl.pallas_call(
        factor_kernel,
        out_shape=(
            struct((modes, modes), BF16),
            struct((modes, orbitals), BF16),
            struct((orbitals, modes), BF16),
        ),
        in_specs=[INTO_SMEM] * 2 + [ANY] * 2,
        out_specs=(INTO_VMEM, ANY, ANY),
        scratch_shapes=[
            pltpu.VMEM((modes, modes), F32),
            pltpu.VMEM((modes, modes), F32),
            pltpu.VMEM((TILE, TILE), F32),
            pltpu.VMEM((orbitals, modes), BF16),
            pltpu.VMEM((modes, orbitals), BF16),
            pltpu.VMEM((count, TILE, TILE), BF16),
            pltpu.VMEM((orbitals, modes), F32),
            pltpu.VMEM((orbitals, modes), BF16),
            pltpu.SemaphoreType.DMA((3,)),
            pltpu.SemaphoreType.DMA((8,)),
        ],
        compiler_params=params(56),
        cost_estimate=cost(8 * orbitals * modes * modes, orbitals * modes * 2),
        name="factor",
    )(onsite_rows[0], onsite_cols[0], u, onsite_blocks[0])
    next_factor = passed_along(factor, "slab", -1)

    yt = pl.pallas_call(
        link_kernel,
        out_shape=struct((modes, modes), BF16),
        in_specs=[INTO_SMEM] * 2 + [INTO_VMEM] * 2 + [ANY, INTO_VMEM],
        out_specs=INTO_VMEM,
        scratch_shapes=[
            pltpu.VMEM((surface, modes), F32),
            pltpu.VMEM((surface, modes), BF16),
            pltpu.SemaphoreType.DMA((1,)),
        ],
        compiler_params=params(12),
        cost_estimate=cost(2 * links * TILE * TILE * modes, 4 * surface * modes * 2),
        name="link",
    )(coupling_rows[0], coupling_cols[0], next_head, coupling_blocks[0], u, factor)
    last_yt = passed_along(yt, "slab", 1)

    onsite = pl.pallas_call(
        onsite_kernel,
        out_shape=struct((modes, modes), F32),
        in_specs=[INTO_SMEM, ANY, ANY, INTO_VMEM, INTO_VMEM, ANY],
        out_specs=INTO_VMEM,
        scratch_shapes=[
            pltpu.VMEM((modes, orbitals), BF16),
            pltpu.VMEM((orbitals, modes), BF16),
            pltpu.VMEM((modes, modes), F32),
            pltpu.SemaphoreType.DMA((8, 2)),
        ],
        compiler_params=params(24),
        cost_estimate=cost(8 * orbitals * modes * modes, 4 * orbitals * modes),
        name="onsite",
    )(place, turned, spread, factor, steps, yt)

    right, left = pl.pallas_call(
        couple_kernel,
        out_shape=(struct((modes, modes), F32),) * 2,
        in_specs=[INTO_VMEM] * 4 + [ANY],
        out_specs=(INTO_VMEM,) * 2,
        compiler_params=params(8),
        cost_estimate=cost(4 * modes * modes * modes, 8 * modes * modes * 2),
        name="couple",
    )(yt, next_factor, factor, last_yt, onsite)
    return (onsite[None], right[None], left[None])


def solution(mesh):
    return jax.shard_map(
        shards,
        mesh=mesh,
        in_specs=(
            P(("groups", "slab"), None, None),
            P(("groups", "slab"), None, None, None),
            P(("groups", "slab"), None),
            P(("groups", "slab"), None),
            P(("groups", "slab"), None, None, None),
            P(("groups", "slab"), None),
            P(("groups", "slab"), None),
            P(("groups", "slab")),
        ),
        out_specs=(
            P(("groups", "slab"), None, None),
            P(("groups", "slab"), None, None),
            P(("groups", "slab"), None, None),
        ),
        check_vma=False,
    )
```

time: 76.5 us -> 67.7 us (0.88)
  blocking collectives: 23.3 us -> 0 us
  local copies, waits for them, and re-layouts: 3.18 us -> 11 us
  starting transfers between devices: 7.53 us -> 15.1 us
  waiting for transfers between devices: 3.76 us -> 0.01 us
  Pallas kernels: 37 us -> 39.2 us
    all_gather x1 -> x0, blocking collectives: 23.3 us -> none  [shards(): lax.all_gather(lax.optimization_barrier(jnp.broadcast_to(potential_step[:...]
    all_to_all x0 -> x1, starting transfers between devices: none -> 7.35 us  [shards(): lax.all_to_all(jnp.broadcast_to(potential_step[:, None], (slabs, TILE)),...]
    unnamed x6 -> x22, local copies, waits for them, and re-layouts: 2.14 us -> 8.59 us
    pallas_call x1, Pallas kernels: 23.5 us -> 27.8 us  [shards(): pl.pallas_call(factor_kernel, out_shape=(struct((modes, modes), BF16), st...]
    ppermute x3, waiting for transfers between devices: 3.76 us -> 0.01 us  [passed_along(): return lax.ppermute(block, axis, route)]
    pallas_call x1, Pallas kernels: 4.26 us -> 2.99 us  [shards(): pl.pallas_call(link_kernel, out_shape=struct((modes, modes), BF16), in_sp...]
  transfers between devices with their start and end apart: 3 -> 4, of which waited for: 1 -> 0; matrix products, arithmetic and copies ran while one was open for 0% -> 3% of each run, Pallas kernels for 14% -> 55%
where the time goes in v2:
time: 67.7 us; the launch traced here: 66.7 us
  Pallas kernels  39.2 us (58%)
  starting transfers between devices  15.1 us (22%)
  local copies, waits for them, and re-layouts  11 us (16%)
  between operations  1.43 us (2%)
    pallas_call x1, Pallas kernels, shards(): pl.pallas_call(factor_kernel, out_shape=(struct((modes, modes), BF16), st...  27.8 us
    unnamed x22, local copies, waits for them, and re-layouts  8.59 us
    ppermute x3, starting transfers between devices, passed_along(): return lax.ppermute(block, axis, route)  7.76 us
    all_to_all x1, starting transfers between devices, shards(): lax.all_to_all(jnp.broadcast_to(potential_step[:, None], (slabs, TILE)),...  7.35 us
    pallas_call x1, Pallas kernels, shards(): pl.pallas_call(onsite_kernel, out_shape=struct((modes, modes), F32), in_s...  5.98 us
    pallas_call x1, Pallas kernels, shards(): pl.pallas_call(link_kernel, out_shape=struct((modes, modes), BF16), in_sp...  2.99 us
    pallas_call x1, Pallas kernels, shards(): pl.pallas_call(couple_kernel, out_shape=(struct((modes, modes), F32),) *...  2.46 us
    slice x1, local copies, waits for them, and re-layouts, shards(): next_head = passed_along(u[:surface], 'slab', -1)  1.78 us
  transfers between devices with their start and end apart: 4, of which 0 were waited for; matrix products, arithmetic and copies ran while one was open for 3% of the time, Pallas kernels for 55%

profile of v2, /device:TPU:1, one launch (start us, length us, event | category | flops | bytes accessed | tf_op | source)
XLA Modules:
  0.0 66.7 jit_solution(12831708939835554881)
XLA Ops:
  1.3 0.6 broadcast_in_dim.18
  1.9 7.3 %all-to-all-start = ((f32[16,1,128]{2,1,0:T(1,128)}), f32[16,1,128]{2,1,0:T(1,128)S(1)}, u32[]{:S(2)}, u32[]{:S(2)}) async-start(f32[16,1,128]{2,1,0:T(1,128)} %broadcast_in_dim.18), calls=%async_computation | async-start | bytes 16384 | tf_op jit(solution)/shard_map/all_to_all | solution.py:323
  9.2 1.8 %slice_bitcast_fusion = bf16[512,384]{1,0:T(8,128)(2,1)} fusion(bf16[1,4096,384]{2,1,0:T(8,128)(2,1)} %param.8), kind=kLoop, calls=%fused_computation | loop fusion | bytes 786432 | tf_op jit(solution)/shard_map/slice | solution.py:321
  11.0 2.0 %collective-permute-start = (bf16[512,384]{1,0:T(8,128)(2,1)}, bf16[512,384]{1,0:T(8,128)(2,1)S(1)}, u32[]{:S(2)}, u32[]{:S(2)}) collective-permute-start(bf16[512,384]{1,0:T(8,128)(2,1)} %slice_bitcast_fusion), channel_id=1, source_target_pairs={{1,0},{2,1},{3,2},{4,3},{5,4},{6,5},{7,6},{8,7},{9,8},{10,9},{11,1... | collective-permute-start | bytes 1179656 | tf_op jit(solution)/shard_map/ppermute | solution.py:298
  13.0 0.0 copy-start
  13.0 0.0 copy-start.7
  13.0 0.0 copy-start.8
  13.1 27.8 %factor.1 = (bf16[384,384]{1,0:T(8,128)(2,1)}, bf16[384,4096]{1,0:T(8,128)(2,1)}, bf16[4096,384]{1,0:T(8,128)(2,1)}) custom-call(s32[96]{0:T(128)} %bitcast.26, s32[96]{0:T(128)} %bitcast.27, bf16[4096,384]{1,0:T(8,128)(2,1)} %bitcast.16, bf16[96,128,128]{2,1,0:T(8,128)(2,1)} %bitcast.23), custom_call_target="tpu_custom_call" | custom-call | flops 4831838208 | bytes 3145728 | tf_op jit(solution)/shard_map/factor/pallas_call | solution.py:327
  40.8 1.9 %collective-permute-start.1 = (bf16[384,384]{1,0:T(8,128)(2,1)}, bf16[384,384]{1,0:T(8,128)(2,1)}, u32[]{:S(2)}, u32[]{:S(2)}) collective-permute-start(bf16[384,384]{1,0:T(8,128)(2,1)} %get-tuple-element.10.f_ref), channel_id=1, source_target_pairs={{1,0},{2,1},{3,2},{4,3},{5,4},{6,5},{7,6},{8,7},{9,8},{10,9},{11,1... | collective-permute-start | bytes 884744 | tf_op jit(solution)/shard_map/ppermute | solution.py:298
  42.8 0.0 collective-permute-done.next_ref
  42.8 0.0 copy-start.5
  42.8 0.7 %copy-done.5 = bf16[512,384]{1,0:T(8,128)(2,1)} copy-done((bf16[512,384]{1,0:T(8,128)(2,1)}, bf16[512,384]{1,0:T(8,128)(2,1)S(1)}, u32[]{:S(2)}) %copy-start.5) | copy-done | bytes 393240
  43.6 1.0 %copy-done.1 = bf16[384,384]{1,0:T(8,128)(2,1)S(1)} copy-done((bf16[384,384]{1,0:T(8,128)(2,1)S(1)}, bf16[384,384]{1,0:T(8,128)(2,1)}, u32[]{:S(2)}) %copy-start.1) | copy-done | bytes 294936
  44.5 1.0 %copy-done.4 = bf16[1,16,128,128]{3,2,1,0:T(8,128)(2,1)S(1)} copy-done((bf16[1,16,128,128]{3,2,1,0:T(8,128)(2,1)S(1)}, bf16[1,16,128,128]{3,2,1,0:T(8,128)(2,1)}, u32[]{:S(2)}) %copy-start.4) | copy-done | bytes 524312
  45.6 1.0 %copy-done.6 = bf16[512,384]{1,0:T(8,128)(2,1)S(1)} copy-done((bf16[512,384]{1,0:T(8,128)(2,1)S(1)}, bf16[512,384]{1,0:T(8,128)(2,1)}, u32[]{:S(2)}) %copy-start.6) | copy-done | bytes 393240
  46.6 3.0 %link.1.order_ref.yt_ref = bf16[384,384]{1,0:T(8,128)(2,1)} custom-call(s32[16]{0:T(128)S(1)} %bitcast.21, s32[16]{0:T(128)S(1)} %bitcast.22, bf16[512,384]{1,0:T(8,128)(2,1)S(1)} %copy-done.6, bf16[16,128,128]{2,1,0:T(8,128)(2,1)S(1)} %bitcast.19, bf16[4096,384]{1,0:T(8,128)(2,1)S(1)} %bitcast.17, bf16[384,384]{1,0:T(8,128)(2,1)S(1)} %copy-done.1), custom_call_target="tpu_custom_call" | custom-call | flops 201326592 | bytes 1572864 | tf_op jit(solution)/shard_map/link/pallas_call | solution.py:354
  49.6 3.8 %collective-permute-start.2 = (bf16[384,384]{1,0:T(8,128)(2,1)}, bf16[384,384]{1,0:T(8,128)(2,1)S(1)}, u32[]{:S(2)}, u32[]{:S(2)}) collective-permute-start(bf16[384,384]{1,0:T(8,128)(2,1)} %link.1.order_ref.yt_ref), channel_id=1, source_target_pairs={{0,1},{1,2},{2,3},{3,4},{4,5},{5,6},{6,7},{7,8},{8,9},{9,10},{10,1... | collective-permute-start | bytes 884744 | tf_op jit(solution)/shard_map/ppermute | solution.py:298
  53.4 0.0 all-to-all-done
  53.4 1.9 %copy-done.9 = bf16[384,4096]{1,0:T(8,128)(2,1)S(1)} copy-done((bf16[384,4096]{1,0:T(8,128)(2,1)S(1)}, bf16[384,4096]{1,0:T(8,128)(2,1)}, u32[]{:S(2)}) %copy-start.9) | copy-done | bytes 3145752
  55.3 1.9 %copy-done.10 = bf16[4096,384]{1,0:T(8,128)(2,1)S(1)} copy-done((bf16[4096,384]{1,0:T(8,128)(2,1)S(1)}, bf16[4096,384]{1,0:T(8,128)(2,1)}, u32[]{:S(2)}) %copy-start.10) | copy-done | bytes 3145752
  57.2 6.0 %onsite.1.order_ref = f32[384,384]{1,0:T(8,128)} custom-call(s32[1]{0:T(128)} %bitcast.place_ref, bf16[384,4096]{1,0:T(8,128)(2,1)S(1)} %copy-done.9, bf16[4096,384]{1,0:T(8,128)(2,1)S(1)} %copy-done.10, bf16[384,384]{1,0:T(8,128)(2,1)S(1)} %copy-done.2, f32[16,128]{1,0:T(8,128)S(1)} %bitcast.20, bf16[384,384]{1,0:T(8,128)(2,1)} %link.1.order_ref.yt_ref), custom_call_target="tpu_custom_call" | custom-call | flops 4831838208 | bytes 6291456 | tf_op jit(solution)/shard_map/onsite/pallas_call | solution.py:370
  63.2 0.0 copy-start.3
  63.2 1.1 %copy-done.3 = f32[384,384]{1,0:T(8,128)S(1)} copy-done((f32[384,384]{1,0:T(8,128)S(1)}, f32[384,384]{1,0:T(8,128)}, u32[]{:S(2)}) %copy-start.3) | copy-done | bytes 589848
  64.3 2.5 %couple.1 = (f32[384,384]{1,0:T(8,128)}, f32[384,384]{1,0:T(8,128)}) custom-call(bf16[384,384]{1,0:T(8,128)(2,1)} %link.1.order_ref.yt_ref, bf16[384,384]{1,0:T(8,128)(2,1)} %collective-permute-done.1.next_f_ref, bf16[384,384]{1,0:T(8,128)(2,1)S(1)} %copy-done.2, bf16[384,384]{1,0:T(8,128)(2,1)S(1)} %collective-permute-done.2.last_yt_ref, ...), custom_call_target="tpu_custom_call" | custom-call | flops 226492416 | bytes 2359296 | tf_op jit(solution)/shard_map/couple/pallas_call | solution.py:386
  (12 shorter events, 0.0 us)
Async XLA Ops:
  1.9 51.5 %all-to-all-start = ((f32[16,1,128]{2,1,0:T(1,128)}), f32[16,1,128]{2,1,0:T(1,128)S(1)}, u32[]{:S(2)}, u32[]{:S(2)}) async-start(f32[16,1,128]{2,1,0:T(1,128)} %broadcast_in_dim.18), calls=%async_computation | async-start | bytes 16384 | tf_op jit(solution)/shard_map/all_to_all | solution.py:323
  11.0 31.8 %collective-permute-start = (bf16[512,384]{1,0:T(8,128)(2,1)}, bf16[512,384]{1,0:T(8,128)(2,1)S(1)}, u32[]{:S(2)}, u32[]{:S(2)}) collective-permute-start(bf16[512,384]{1,0:T(8,128)(2,1)} %slice_bitcast_fusion), channel_id=1, source_target_pairs={{1,0},{2,1},{3,2},{4,3},{5,4},{6,5},{7,6},{8,7},{9,8},{10,9},{11,1... | collective-permute-start | bytes 1179656 | tf_op jit(solution)/shard_map/ppermute | solution.py:298
  13.0 30.5 %copy-start = (bf16[1,4096,384]{2,1,0:T(8,128)(2,1)S(1)}, bf16[1,4096,384]{2,1,0:T(8,128)(2,1)}, u32[]{:S(2)}) copy-start(bf16[1,4096,384]{2,1,0:T(8,128)(2,1)} %param.8) | copy-start | bytes 9437188
  13.0 30.5 %copy-start.7 = (s32[1,16]{1,0:T(1,128)S(1)}, s32[1,16]{1,0:T(1,128)}, u32[]{:S(2)}) copy-start(s32[1,16]{1,0:T(1,128)} %param.13) | copy-start | bytes 196
  13.0 30.5 %copy-start.8 = (s32[1,16]{1,0:T(1,128)S(1)}, s32[1,16]{1,0:T(1,128)}, u32[]{:S(2)}) copy-start(s32[1,16]{1,0:T(1,128)} %param.14) | copy-start | bytes 196
  40.8 22.3 %collective-permute-start.1 = (bf16[384,384]{1,0:T(8,128)(2,1)}, bf16[384,384]{1,0:T(8,128)(2,1)}, u32[]{:S(2)}, u32[]{:S(2)}) collective-permute-start(bf16[384,384]{1,0:T(8,128)(2,1)} %get-tuple-element.10.f_ref), channel_id=1, source_target_pairs={{1,0},{2,1},{3,2},{4,3},{5,4},{6,5},{7,6},{8,7},{9,8},{10,9},{11,1... | collective-permute-start | bytes 884744 | tf_op jit(solution)/shard_map/ppermute | solution.py:298
  42.8 0.7 %copy-start.5 = (bf16[512,384]{1,0:T(8,128)(2,1)}, bf16[512,384]{1,0:T(8,128)(2,1)S(1)}, u32[]{:S(2)}) copy-start(bf16[512,384]{1,0:T(8,128)(2,1)S(1)} %collective-permute-done.next_ref) | copy-start | bytes 1179652
  43.5 1.0 %copy-start.1 = (bf16[384,384]{1,0:T(8,128)(2,1)S(1)}, bf16[384,384]{1,0:T(8,128)(2,1)}, u32[]{:S(2)}) copy-start(bf16[384,384]{1,0:T(8,128)(2,1)} %get-tuple-element.10.f_ref) | copy-start | bytes 884740
  44.5 1.0 %copy-start.4 = (bf16[1,16,128,128]{3,2,1,0:T(8,128)(2,1)S(1)}, bf16[1,16,128,128]{3,2,1,0:T(8,128)(2,1)}, u32[]{:S(2)}) copy-start(bf16[1,16,128,128]{3,2,1,0:T(8,128)(2,1)} %param.12) | copy-start | bytes 1572868
  45.6 1.0 %copy-start.6 = (bf16[512,384]{1,0:T(8,128)(2,1)S(1)}, bf16[512,384]{1,0:T(8,128)(2,1)}, u32[]{:S(2)}) copy-start(bf16[512,384]{1,0:T(8,128)(2,1)} %copy-done.5) | copy-start | bytes 1179652
  46.6 6.9 %copy-start.2 = (bf16[384,384]{1,0:T(8,128)(2,1)S(1)}, bf16[384,384]{1,0:T(8,128)(2,1)}, u32[]{:S(2)}) copy-start(bf16[384,384]{1,0:T(8,128)(2,1)} %get-tuple-element.10.f_ref) | copy-start | bytes 884740
  49.6 13.6 %collective-permute-start.2 = (bf16[384,384]{1,0:T(8,128)(2,1)}, bf16[384,384]{1,0:T(8,128)(2,1)S(1)}, u32[]{:S(2)}, u32[]{:S(2)}) collective-permute-start(bf16[384,384]{1,0:T(8,128)(2,1)} %link.1.order_ref.yt_ref), channel_id=1, source_target_pairs={{0,1},{1,2},{2,3},{3,4},{4,5},{5,6},{6,7},{7,8},{8,9},{9,10},{10,1... | collective-permute-start | bytes 884744 | tf_op jit(solution)/shard_map/ppermute | solution.py:298
  53.4 1.9 %copy-start.9 = (bf16[384,4096]{1,0:T(8,128)(2,1)S(1)}, bf16[384,4096]{1,0:T(8,128)(2,1)}, u32[]{:S(2)}) copy-start(bf16[384,4096]{1,0:T(8,128)(2,1)} %get-tuple-element.8.turned_hbm) | copy-start | bytes 9437188
  55.3 1.9 %copy-start.10 = (bf16[4096,384]{1,0:T(8,128)(2,1)S(1)}, bf16[4096,384]{1,0:T(8,128)(2,1)}, u32[]{:S(2)}) copy-start(bf16[4096,384]{1,0:T(8,128)(2,1)} %get-tuple-element.9.spread_hbm) | copy-start | bytes 9437188
  63.2 1.1 %copy-start.3 = (f32[384,384]{1,0:T(8,128)S(1)}, f32[384,384]{1,0:T(8,128)}, u32[]{:S(2)}) copy-start(f32[384,384]{1,0:T(8,128)} %onsite.1.order_ref) | copy-start | bytes 1769476

commit v3 on v2

v3 whole, which is shorter than its diff:
```python
import functools

import jax
import jax.numpy as jnp
from jax import lax
from jax.experimental import pallas as pl
from jax.experimental.pallas import tpu as pltpu
from jax.sharding import PartitionSpec as P

F32 = jnp.float32
BF16 = jnp.bfloat16
VMEM_LIMIT = 63900000
SURFACE = 4
TILE = 128
ROWS = 8


def lane(value, k):
    return jnp.broadcast_to(value[:, k : k + 1], value.shape)


def row(ref, k, width):
    return jnp.broadcast_to(ref[k : k + 1, :], (ROWS, width))


def exact_dot(a, b, dims):
    return lax.dot_general(
        a, b, (dims, ((), ())), precision=lax.Precision.HIGHEST, preferred_element_type=F32
    )


def bf_dot(a, b, dims):
    return lax.dot_general(a, b, (dims, ((), ())), preferred_element_type=F32)


NN = ((1,), (0,))
TN = ((0,), (0,))
NT = ((1,), (1,))


def three_parts(value):
    a = value.astype(BF16).astype(F32)
    b = (value - a).astype(BF16).astype(F32)
    return a, b, value - a - b


def factor_tile(ax_ref, col_ref, between):
    width = ax_ref.shape[1]
    panels = ax_ref.shape[0] // ROWS
    near = 2
    for g in range(panels):
        base = ROWS * g
        here = ax_ref[base : base + ROWS, :TILE]
        for j in range(ROWS):
            col_ref[j] = lane(here, base + j)
        s = {(i, j): row(col_ref.at[j], i, TILE) for j in range(ROWS) for i in range(j, ROWS)}
        low, r = {}, []
        for p in range(0, ROWS, 2):
            q = p + 1
            a, b, c = s[p, p], s[q, p], s[q, q]
            root = lax.rsqrt(a * c - b * b)
            r_p = lax.rsqrt(a)
            r_q = a * r_p * root
            inverse = root * root
            r += [r_p, r_q]
            low[q, p] = b * r_p
            side = {}
            for i in range(q + 1, ROWS):
                first, second = s[i, p], s[i, q]
                low[i, p] = first * r_p
                low[i, q] = (second - low[i, p] * low[q, p]) * r_q
                side[i] = (c * first - b * second, a * second - b * first)
            for j in range(q + 1, ROWS):
                for i in range(j, ROWS):
                    both = side[j][0] * s[i, p] + side[j][1] * s[i, q]
                    s[i, j] = s[i, j] - both * inverse
        r2 = [jnp.concatenate([v, v], axis=1) for v in r]
        low2 = {key: jnp.concatenate([v, v], axis=1) for key, v in low.items()}
        z = []
        for k in range(ROWS):
            top = row(ax_ref, base + k, width)
            for m in range(k):
                top = top - low2[k, m] * z[m]
            z.append(top * r2[k])
        sub = lax.broadcasted_iota(jnp.int32, z[0].shape, 0)
        packed = z[0]
        for k in range(1, ROWS):
            packed = jnp.where(sub == k, z[k], packed)
        for i in range(g + 1, min(g + 1 + near, panels)):
            at = ROWS * i
            block = ax_ref[at : at + ROWS, :]
            below = []
            for k in range(ROWS):
                column = lane(block[:, :TILE], base + k)
                for m in range(k):
                    column = column - below[m] * low[k, m]
                below.append(column * r[k])
            for k in range(ROWS):
                block = block - jnp.concatenate([below[k], below[k]], axis=1) * z[k]
            ax_ref[at : at + ROWS, :] = block
        ax_ref[base : base + ROWS, TILE:] = packed[:, TILE:]
        far = ROWS * (g + 1 + near)
        if far < ax_ref.shape[0]:
            a, b, c = three_parts(packed)
            left = jnp.concatenate([v[:, :TILE] for v in (a, a, b, b, a, c)], axis=0).astype(BF16)
            right = jnp.concatenate([a, b, a, b, c, a], axis=0).astype(BF16)
            product = bf_dot(left, right, TN)
            ax_ref[far:, :] = ax_ref[far:, :] - product[far:, :]
        between(g)


def add_product(j, live, acc_ref, source_ref, blocks_ref, rows_ref, cols_ref, row_base):
    to = pl.multiple_of((rows_ref[j] - row_base) * TILE, TILE)
    at = pl.multiple_of(cols_ref[j] * TILE, TILE)
    product = bf_dot(blocks_ref[j], source_ref[pl.ds(at, TILE), :], NN)
    if live is not None:
        product = jnp.where(live, product, 0.0)
    acc_ref[pl.ds(to, TILE), :] = acc_ref[pl.ds(to, TILE), :] + product


def factor_kernel(
    rows_ref,
    cols_ref,
    u_hbm,
    blocks_hbm,
    f_ref,
    w_ref,
    gram_ref,
    upper_ref,
    inv_ref,
    ax_ref,
    col_ref,
    u_ref,
    turned_ref,
    blocks_ref,
    acc_ref,
    sems,
    u_sems,
):
    orbitals, modes = u_ref.shape
    tiles = modes // TILE
    panels = TILE // ROWS
    step = orbitals // panels
    chunks = u_sems.shape[0]
    long_step = orbitals // chunks
    copies = [
        pltpu.make_async_copy(
            u_hbm.at[pl.ds(c * long_step, long_step)],
            u_ref.at[pl.ds(c * long_step, long_step)],
            u_sems.at[c],
        )
        for c in range(chunks)
    ]
    blocks_copy = pltpu.make_async_copy(blocks_hbm, blocks_ref, sems.at[0])
    for copy in copies:
        copy.start()
    blocks_copy.start()
    acc_ref[...] = jnp.zeros_like(acc_ref)
    inv_ref[...] = jnp.zeros_like(inv_ref)
    upper_ref[...] = jnp.zeros_like(upper_ref)

    def gram_part(of, store, first, size):
        turned = u_ref[first : first + size, of].T
        turned_ref[store, first : first + size] = turned
        return bf_dot(turned, u_ref[first : first + size, :], NN)

    block0 = pl.ds(0, TILE)
    for c, copy in enumerate(copies):
        copy.wait()
        product = gram_part(block0, block0, c * long_step, long_step)
        gram_ref[0] = product if c == 0 else gram_ref[0] + product
    blocks_copy.wait()

    count = blocks_ref.shape[0]
    share = -(-count // tiles)

    def one_tile(b, carry):
        here = pl.ds(pl.multiple_of(b * TILE, TILE), TILE)
        later = pl.ds(pl.multiple_of(jnp.minimum(b + 1, tiles - 1) * TILE, TILE), TILE)
        store = pl.ds(pl.multiple_of((b + 1) * TILE, TILE), TILE)
        tile = gram_ref[0, :, here]
        on_diagonal = lax.broadcasted_iota(jnp.int32, tile.shape, 0) == lax.broadcasted_iota(
            jnp.int32, tile.shape, 1
        )
        diagonal = jnp.where(on_diagonal, tile, 0.0)
        across = lax.rsqrt(jnp.sum(diagonal, axis=0, keepdims=True))
        down = lax.rsqrt(jnp.sum(diagonal, axis=1, keepdims=True))
        ax_ref[:, :TILE] = tile * across * down
        ax_ref[:, TILE:] = on_diagonal.astype(F32)

        def between(g):
            product = gram_part(later, store, g * step, step)
            gram_ref[1] = product if g == 0 else gram_ref[1] + product
            for t in range(share):
                if t * panels // share == g:
                    j = b * share + t
                    live = None
                    if share * tiles != count:
                        live = j < count
                        j = jnp.minimum(j, count - 1)
                    add_product(j, live, acc_ref, u_ref, blocks_ref, rows_ref, cols_ref, 0)

        factor_tile(ax_ref, col_ref, between)
        x = ax_ref[:, TILE:] * across
        inv_part = exact_dot(upper_ref[:, here], inv_ref[...], TN)
        inv_ref[here, :] = -exact_dot(x, inv_part, NN)
        inv_ref[here, here] = x
        upper_ref[here, :] = exact_dot(x, gram_ref[0], NN)
        gram_ref[0] = gram_ref[1] - exact_dot(upper_ref[:, later], upper_ref[...], TN)
        return carry

    lax.fori_loop(0, tiles, one_tile, 0)
    f_ref[...] = inv_ref[...].T.astype(BF16)
    for c in range(chunks):
        part = slice(c * long_step, (c + 1) * long_step)
        product = bf_dot(turned_ref[:modes, part], acc_ref[part, :].astype(BF16), NN)
        w_ref[...] = product if c == 0 else w_ref[...] + product


def link_kernel(
    rows_ref,
    cols_ref,
    next_hbm,
    blocks_hbm,
    u_hbm,
    f_hbm,
    yt_ref,
    hop_ref,
    next_ref,
    blocks_ref,
    tail_ref,
    f_ref,
    sems,
):
    surface = tail_ref.shape[0]
    base = u_hbm.shape[0] - surface
    pairs = [
        (next_hbm, next_ref),
        (blocks_hbm, blocks_ref),
        (u_hbm.at[pl.ds(base, surface)], tail_ref),
        (f_hbm, f_ref),
    ]
    copies = [pltpu.make_async_copy(a, b, sems.at[n]) for n, (a, b) in enumerate(pairs)]
    for copy in copies:
        copy.start()
    hop_ref[...] = jnp.zeros_like(hop_ref)
    for copy in copies:
        copy.wait()
    for j in range(blocks_ref.shape[0]):
        add_product(j, None, hop_ref, next_ref, blocks_ref, rows_ref, cols_ref, base // TILE)
    high, low = split(bf_dot(tail_ref[...], hop_ref[...].astype(BF16), TN))
    factor = f_ref[...]
    yt_ref[...] = (bf_dot(high, factor, TN) + bf_dot(low, factor, TN)).astype(BF16)


def couple_kernel(yt_ref, next_f_ref, f_ref, last_yt_ref, order_ref, right_ref, left_ref):
    right_ref[...] = bf_dot(yt_ref[...], next_f_ref[...], TN)
    left_ref[...] = bf_dot(f_ref[...], last_yt_ref[...], TN)


def split(value):
    high = value.astype(BF16)
    return high, (value - high.astype(F32)).astype(BF16)


def onsite_kernel(place_ref, w_ref, f_ref, steps_ref, order_ref, out_ref, done_ref):
    modes = f_ref.shape[0]
    w = w_ref[...]
    w = w + w.T
    f = f_ref[...]
    high, low = split(w)
    half = bf_dot(high, f, NN) + bf_dot(low, f, NN)
    high, low = split(half)
    full = bf_dot(f, high, TN) + bf_dot(f, low, TN)
    steps = steps_ref[...]
    reached = lax.broadcasted_iota(jnp.int32, steps.shape, 0) <= place_ref[0]
    potential = jnp.sum(jnp.where(reached, steps, 0.0), axis=0, keepdims=True)[:, :1]
    i = lax.broadcasted_iota(jnp.int32, (modes, modes), 0)
    j = lax.broadcasted_iota(jnp.int32, (modes, modes), 1)
    out_ref[...] = full + jnp.where(i == j, potential, 0.0)
    done_ref[...] = jnp.zeros_like(done_ref)


def struct(shape, dtype):
    return jax.ShapeDtypeStruct(shape, dtype)


ANY = pl.BlockSpec(memory_space=pl.ANY)
INTO_VMEM = pl.BlockSpec(memory_space=pltpu.VMEM)
INTO_SMEM = pl.BlockSpec(memory_space=pltpu.SMEM)


PARAMS = pltpu.CompilerParams(vmem_limit_bytes=VMEM_LIMIT)
SMALL = pltpu.CompilerParams(vmem_limit_bytes=8 * 1024 * 1024)


def passed_along(block, axis, distance):
    devices = range(lax.axis_size(axis))
    route = [(i - distance, i) for i in devices if i - distance in devices]
    return lax.ppermute(block, axis, route)


def cost(flops, moved):
    return pl.CostEstimate(flops=flops, bytes_accessed=moved, transcendentals=0)


def shards(
    trial_modes,
    onsite_blocks,
    onsite_rows,
    onsite_cols,
    coupling_blocks,
    coupling_rows,
    coupling_cols,
    potential_step,
):
    u = trial_modes[0]
    orbitals, modes = u.shape
    surface = SURFACE * TILE
    count = onsite_blocks.shape[1]
    links = coupling_blocks.shape[1]
    place = lax.axis_index("slab").astype(jnp.int32).reshape(1)
    next_head = passed_along(u[:surface], "slab", -1)
    slabs = lax.axis_size("slab")
    steps = lax.all_to_all(
        jnp.broadcast_to(potential_step[:, None], (slabs, TILE)), "slab", 0, 0, tiled=True
    )

    factor, w = pl.pallas_call(
        factor_kernel,
        out_shape=(struct((modes, modes), BF16), struct((modes, modes), F32)),
        in_specs=[INTO_SMEM] * 2 + [ANY] * 2,
        out_specs=(INTO_VMEM,) * 2,
        scratch_shapes=[
            pltpu.VMEM((2, TILE, modes), F32),
            pltpu.VMEM((modes, modes), F32),
            pltpu.VMEM((modes, modes), F32),
            pltpu.VMEM((TILE, 2 * TILE), F32),
            pltpu.VMEM((ROWS, ROWS, TILE), F32),
            pltpu.VMEM((orbitals, modes), BF16),
            pltpu.VMEM((modes + TILE, orbitals), BF16),
            pltpu.VMEM((count, TILE, TILE), BF16),
            pltpu.VMEM((orbitals, modes), F32),
            pltpu.SemaphoreType.DMA((1,)),
            pltpu.SemaphoreType.DMA((8,)),
        ],
        compiler_params=PARAMS,
        cost_estimate=cost(8 * orbitals * modes * modes, orbitals * modes * 2),
        name="factor",
    )(onsite_rows[0], onsite_cols[0], u, onsite_blocks[0])
    next_factor = passed_along(factor, "slab", -1)

    yt = pl.pallas_call(
        link_kernel,
        out_shape=struct((modes, modes), BF16),
        in_specs=[INTO_SMEM] * 2 + [ANY] * 4,
        out_specs=INTO_VMEM,
        scratch_shapes=[
            pltpu.VMEM((surface, modes), F32),
            pltpu.VMEM((surface, modes), BF16),
            pltpu.VMEM((links, TILE, TILE), BF16),
            pltpu.VMEM((surface, modes), BF16),
            pltpu.VMEM((modes, modes), BF16),
            pltpu.SemaphoreType.DMA((4,)),
        ],
        compiler_params=PARAMS,
        cost_estimate=cost(2 * links * TILE * TILE * modes, 4 * surface * modes * 2),
        name="link",
    )(coupling_rows[0], coupling_cols[0], next_head, coupling_blocks[0], u, factor)
    last_yt = passed_along(yt, "slab", 1)

    onsite, done = pl.pallas_call(
        onsite_kernel,
        out_shape=(struct((modes, modes), F32), struct((ROWS, TILE), F32)),
        in_specs=[INTO_SMEM] + [INTO_VMEM] * 3 + [ANY],
        out_specs=(INTO_VMEM,) * 2,
        compiler_params=PARAMS,
        cost_estimate=cost(8 * orbitals * modes * modes, 4 * orbitals * modes),
        name="onsite",
    )(place, w, factor, steps, yt)

    right, left = pl.pallas_call(
        couple_kernel,
        out_shape=(struct((modes, modes), F32),) * 2,
        in_specs=[INTO_VMEM] * 4 + [ANY],
        out_specs=(INTO_VMEM,) * 2,
        compiler_params=SMALL,
        cost_estimate=cost(4 * modes * modes * modes, 8 * modes * modes * 2),
        name="couple",
    )(yt, next_factor, factor, last_yt, done)
    return (onsite[None], right[None], left[None])


def solution(mesh):
    return jax.shard_map(
        shards,
        mesh=mesh,
        in_specs=(
            P(("groups", "slab"), None, None),
            P(("groups", "slab"), None, None, None),
            P(("groups", "slab"), None),
            P(("groups", "slab"), None),
            P(("groups", "slab"), None, None, None),
            P(("groups", "slab"), None),
            P(("groups", "slab"), None),
            P(("groups", "slab")),
        ),
        out_specs=(
            P(("groups", "slab"), None, None),
            P(("groups", "slab"), None, None),
            P(("groups", "slab"), None, None),
        ),
        check_vma=False,
    )
```

time: 67.7 us -> 54.7 us (0.81)
  the two profiles are of different devices: /device:TPU:1 before, /device:TPU:8 now
where the time goes in v3:
time: 54.7 us; the launch traced here: 54.3 us
  Pallas kernels  32.2 us (59%)
  starting transfers between devices  13.8 us (25%)
  local copies, waits for them, and re-layouts  3.66 us (7%)
  waiting for transfers between devices  3.32 us (6%)
  between operations  1.36 us (2%)
    pallas_call x1, Pallas kernels, shards(): pl.pallas_call(factor_kernel, out_shape=(struct((modes, modes), BF16), st...  23.4 us
    ppermute x3, starting transfers between devices, passed_along(): return lax.ppermute(block, axis, route)  7.46 us
    all_to_all x1, starting transfers between devices, shards(): lax.all_to_all(jnp.broadcast_to(potential_step[:, None], (slabs, TILE)),...  6.3 us
    pallas_call x1, Pallas kernels, shards(): pl.pallas_call(link_kernel, out_shape=struct((modes, modes), BF16), in_sp...  4.28 us
    ppermute x3, waiting for transfers between devices, passed_along(): return lax.ppermute(block, axis, route)  3.31 us
    pallas_call x1, Pallas kernels, shards(): pl.pallas_call(onsite_kernel, out_shape=(struct((modes, modes), F32), str...  3.15 us
    unnamed x10, local copies, waits for them, and re-layouts  2.02 us
    pallas_call x1, Pallas kernels, shards(): pl.pallas_call(couple_kernel, out_shape=(struct((modes, modes), F32),) *...  1.4 us
  transfers between devices with their start and end apart: 4, of which 1 were waited for; matrix products, arithmetic and copies ran while one was open for 2% of the time, Pallas kernels for 57%

profile of v3, /device:TPU:8, one launch (start us, length us, event | category | flops | bytes accessed | tf_op | source)
XLA Modules:
  0.0 54.3 jit_solution(7891409679236392274)
XLA Ops:
  1.3 0.6 %broadcast_in_dim.18 = f32[16,1,128]{2,1,0:T(1,128)} broadcast(f32[]{:T(128)} %bitcast.15), dimensions={} | broadcast | bytes 8196 | tf_op jit(solution)/shard_map/broadcast_in_dim | solution.py:326
  1.9 6.3 %all-to-all-start = ((f32[16,1,128]{2,1,0:T(1,128)}), f32[16,1,128]{2,1,0:T(1,128)S(1)}, u32[]{:S(2)}, u32[]{:S(2)}) async-start(f32[16,1,128]{2,1,0:T(1,128)} %broadcast_in_dim.18), calls=%async_computation | async-start | bytes 16384 | tf_op jit(solution)/shard_map/all_to_all | solution.py:325
  8.2 1.0 %slice_bitcast_fusion = bf16[512,384]{1,0:T(8,128)(2,1)S(1)} fusion(bf16[1,4096,384]{2,1,0:T(8,128)(2,1)} %param.8), kind=kLoop, calls=%fused_computation | loop fusion | bytes 786432 | tf_op jit(solution)/shard_map/slice | solution.py:323
  9.2 3.1 %collective-permute-start = (bf16[512,384]{1,0:T(8,128)(2,1)S(1)}, bf16[512,384]{1,0:T(8,128)(2,1)S(1)}, u32[]{:S(2)}, u32[]{:S(2)}) collective-permute-start(bf16[512,384]{1,0:T(8,128)(2,1)S(1)} %slice_bitcast_fusion), channel_id=1, source_target_pairs={{1,0},{2,1},{3,2},{4,3},{5,4},{6,5},{7,6},{8,7},{9,8},{10,9},{11,1... | collective-permute-start | bytes 1179656 | tf_op jit(solution)/shard_map/ppermute | solution.py:300
  12.3 23.4 %factor.1 = (bf16[384,384]{1,0:T(8,128)(2,1)}, f32[384,384]{1,0:T(8,128)}) custom-call(s32[96]{0:T(128)} %bitcast.25, s32[96]{0:T(128)} %bitcast.26, bf16[4096,384]{1,0:T(8,128)(2,1)} %bitcast.16, bf16[96,128,128]{2,1,0:T(8,128)(2,1)} %bitcast.22), custom_call_target="tpu_custom_call" | custom-call | flops 4831838208 | bytes 3145728 | tf_op jit(solution)/shard_map/factor/pallas_call | solution.py:329
  35.7 2.3 %collective-permute-start.1 = (bf16[384,384]{1,0:T(8,128)(2,1)}, bf16[384,384]{1,0:T(8,128)(2,1)S(1)}, u32[]{:S(2)}, u32[]{:S(2)}) collective-permute-start(bf16[384,384]{1,0:T(8,128)(2,1)} %get-tuple-element.10.f_hbm.f_ref), channel_id=1, source_target_pairs={{1,0},{2,1},{3,2},{4,3},{5,4},{6,5},{7,6},{8,7},{9,8},{10,9},{11,1... | collective-permute-start | bytes 884744 | tf_op jit(solution)/shard_map/ppermute | solution.py:300
  38.0 0.0 collective-permute-done.next_hbm
  38.0 0.0 copy-start.3
  38.1 0.7 %copy-done.3 = bf16[512,384]{1,0:T(8,128)(2,1)} copy-done((bf16[512,384]{1,0:T(8,128)(2,1)}, bf16[512,384]{1,0:T(8,128)(2,1)S(1)}, u32[]{:S(2)}) %copy-start.3) | copy-done | bytes 393240
  38.8 4.3 %link.1.order_ref.yt_ref = bf16[384,384]{1,0:T(8,128)(2,1)} custom-call(s32[16]{0:T(128)} %bitcast.20, s32[16]{0:T(128)} %bitcast.21, bf16[512,384]{1,0:T(8,128)(2,1)} %copy-done.3, bf16[16,128,128]{2,1,0:T(8,128)(2,1)} %bitcast.18, bf16[4096,384]{1,0:T(8,128)(2,1)} %bitcast.17, bf16[384,384]{1,0:T(8,128)(2,1)} %get-tuple-element.10.f_hbm.f_ref), custom_call_target="tpu_custom_call" | custom-call | flops 201326592 | bytes 1572864 | tf_op jit(solution)/shard_map/link/pallas_call | solution.py:353
  43.1 2.1 %collective-permute-start.2 = (bf16[384,384]{1,0:T(8,128)(2,1)}, bf16[384,384]{1,0:T(8,128)(2,1)S(1)}, u32[]{:S(2)}, u32[]{:S(2)}) collective-permute-start(bf16[384,384]{1,0:T(8,128)(2,1)} %link.1.order_ref.yt_ref), channel_id=1, source_target_pairs={{0,1},{1,2},{2,3},{3,4},{4,5},{5,6},{6,7},{7,8},{8,9},{9,10},{10,1... | collective-permute-start | bytes 884744 | tf_op jit(solution)/shard_map/ppermute | solution.py:300
  45.1 0.0 all-to-all-done
  45.2 0.0 copy-start.4
  45.2 0.6 %copy-done.4 = f32[16,1,128]{2,1,0:T(1,128)} copy-done((f32[16,1,128]{2,1,0:T(1,128)}, f32[16,1,128]{2,1,0:T(1,128)S(1)}, u32[]{:S(2)}) %copy-start.4) | copy-done | bytes 8216
  45.8 0.0 copy-start
  45.8 0.0 copy-start.1
  45.8 3.2 %onsite.1 = (f32[384,384]{1,0:T(8,128)}, f32[8,128]{1,0:T(8,128)}) custom-call(s32[1]{0:T(128)} %bitcast.place_ref, f32[384,384]{1,0:T(8,128)} %get-tuple-element.9.w_ref, bf16[384,384]{1,0:T(8,128)(2,1)} %get-tuple-element.10.f_hbm.f_ref, f32[16,128]{1,0:T(8,128)} %bitcast.19, bf16[384,384]{1,0:T(8,128)(2,1)} %link.1.order_ref.yt_ref), custom_call_target="tpu_custom_call" | custom-call | flops 4831838208 | bytes 6291456 | tf_op jit(solution)/shard_map/onsite/pallas_call | solution.py:372
  48.9 0.0 collective-permute-done.1.next_f_ref
  48.9 3.3 %collective-permute-done.2.last_yt_ref = bf16[384,384]{1,0:T(8,128)(2,1)S(1)} collective-permute-done((bf16[384,384]{1,0:T(8,128)(2,1)}, bf16[384,384]{1,0:T(8,128)(2,1)S(1)}, u32[]{:S(2)}, u32[]{:S(2)}) %collective-permute-start.2) | collective-permute-done | bytes 294944 | tf_op jit(solution)/shard_map/ppermute | solution.py:300
  52.2 0.0 copy-done
  52.2 0.0 copy-done.1
  52.2 0.0 copy-start.2
  52.2 0.7 %copy-done.2 = f32[8,128]{1,0:T(8,128)S(1)} copy-done((f32[8,128]{1,0:T(8,128)S(1)}, f32[8,128]{1,0:T(8,128)}, u32[]{:S(2)}) %copy-start.2) | copy-done | bytes 4120
  52.9 1.4 %couple.1 = (f32[384,384]{1,0:T(8,128)}, f32[384,384]{1,0:T(8,128)}) custom-call(bf16[384,384]{1,0:T(8,128)(2,1)S(1)} %copy-done.1, bf16[384,384]{1,0:T(8,128)(2,1)S(1)} %collective-permute-done.1.next_f_ref, bf16[384,384]{1,0:T(8,128)(2,1)S(1)} %copy-done, bf16[384,384]{1,0:T(8,128)(2,1)S(1)} %collective-permute-done.2.last_yt_ref, f32[8,128]{1,0:T(8,128)S(1)} %copy-done.2), custom_call_target="tpu_custom_call" | custom-call | flops 226492416 | bytes 2359296 | tf_op jit(solution)/shard_map/couple/pallas_call | solution.py:382
Async XLA Ops:
  1.9 43.3 %all-to-all-start = ((f32[16,1,128]{2,1,0:T(1,128)}), f32[16,1,128]{2,1,0:T(1,128)S(1)}, u32[]{:S(2)}, u32[]{:S(2)}) async-start(f32[16,1,128]{2,1,0:T(1,128)} %broadcast_in_dim.18), calls=%async_computation | async-start | bytes 16384 | tf_op jit(solution)/shard_map/all_to_all | solution.py:325
  9.2 28.8 %collective-permute-start = (bf16[512,384]{1,0:T(8,128)(2,1)S(1)}, bf16[512,384]{1,0:T(8,128)(2,1)S(1)}, u32[]{:S(2)}, u32[]{:S(2)}) collective-permute-start(bf16[512,384]{1,0:T(8,128)(2,1)S(1)} %slice_bitcast_fusion), channel_id=1, source_target_pairs={{1,0},{2,1},{3,2},{4,3},{5,4},{6,5},{7,6},{8,7},{9,8},{10,9},{11,1... | collective-permute-start | bytes 1179656 | tf_op jit(solution)/shard_map/ppermute | solution.py:300
  35.7 13.2 %collective-permute-start.1 = (bf16[384,384]{1,0:T(8,128)(2,1)}, bf16[384,384]{1,0:T(8,128)(2,1)S(1)}, u32[]{:S(2)}, u32[]{:S(2)}) collective-permute-start(bf16[384,384]{1,0:T(8,128)(2,1)} %get-tuple-element.10.f_hbm.f_ref), channel_id=1, source_target_pairs={{1,0},{2,1},{3,2},{4,3},{5,4},{6,5},{7,6},{8,7},{9,8},{10,9},{11,1... | collective-permute-start | bytes 884744 | tf_op jit(solution)/shard_map/ppermute | solution.py:300
  38.0 0.7 %copy-start.3 = (bf16[512,384]{1,0:T(8,128)(2,1)}, bf16[512,384]{1,0:T(8,128)(2,1)S(1)}, u32[]{:S(2)}) copy-start(bf16[512,384]{1,0:T(8,128)(2,1)S(1)} %collective-permute-done.next_hbm) | copy-start | bytes 1179652
  43.1 9.2 %collective-permute-start.2 = (bf16[384,384]{1,0:T(8,128)(2,1)}, bf16[384,384]{1,0:T(8,128)(2,1)S(1)}, u32[]{:S(2)}, u32[]{:S(2)}) collective-permute-start(bf16[384,384]{1,0:T(8,128)(2,1)} %link.1.order_ref.yt_ref), channel_id=1, source_target_pairs={{0,1},{1,2},{2,3},{3,4},{4,5},{5,6},{6,7},{7,8},{8,9},{9,10},{10,1... | collective-permute-start | bytes 884744 | tf_op jit(solution)/shard_map/ppermute | solution.py:300
  45.2 0.6 %copy-start.4 = (f32[16,1,128]{2,1,0:T(1,128)}, f32[16,1,128]{2,1,0:T(1,128)S(1)}, u32[]{:S(2)}) copy-start(f32[16,1,128]{2,1,0:T(1,128)S(1)} %all-to-all-done) | copy-start | bytes 24580
  45.8 6.5 %copy-start = (bf16[384,384]{1,0:T(8,128)(2,1)S(1)}, bf16[384,384]{1,0:T(8,128)(2,1)}, u32[]{:S(2)}) copy-start(bf16[384,384]{1,0:T(8,128)(2,1)} %get-tuple-element.10.f_hbm.f_ref) | copy-start | bytes 884740
  45.8 6.5 %copy-start.1 = (bf16[384,384]{1,0:T(8,128)(2,1)S(1)}, bf16[384,384]{1,0:T(8,128)(2,1)}, u32[]{:S(2)}) copy-start(bf16[384,384]{1,0:T(8,128)(2,1)} %link.1.order_ref.yt_ref) | copy-start | bytes 884740
  52.2 0.7 %copy-start.2 = (f32[8,128]{1,0:T(8,128)S(1)}, f32[8,128]{1,0:T(8,128)}, u32[]{:S(2)}) copy-start(f32[8,128]{1,0:T(8,128)} %get-tuple-element.12.order_ref) | copy-start | bytes 12292

commit v4 on v3

--- a/solution.py
+++ b/solution.py
@@ -121,9 +121,14 @@
 def factor_kernel(
     rows_ref,
     cols_ref,
+    crows_ref,
+    ccols_ref,
+    next_hbm,
     u_hbm,
     blocks_hbm,
+    cblocks_hbm,
     f_ref,
+    yt_ref,
     w_ref,
     gram_ref,
     upper_ref,
@@ -134,10 +139,15 @@
     turned_ref,
     blocks_ref,
     acc_ref,
+    next_ref,
+    cblocks_ref,
+    hop_ref,
+    m_ref,
     sems,
     u_sems,
 ):
     orbitals, modes = u_ref.shape
+    surface = hop_ref.shape[0]
     tiles = modes // TILE
     panels = TILE // ROWS
     step = orbitals // panels
@@ -151,34 +161,93 @@
         )
         for c in range(chunks)
     ]
-    blocks_copy = pltpu.make_async_copy(blocks_hbm, blocks_ref, sems.at[0])
-    for copy in copies:
+    more = [
+        pltpu.make_async_copy(blocks_hbm, blocks_ref, sems.at[0]),
+        pltpu.make_async_copy(cblocks_hbm, cblocks_ref, sems.at[1]),
+        pltpu.make_async_copy(next_hbm, next_ref, sems.at[2]),
+    ]
+    for copy in copies + more:
         copy.start()
-    blocks_copy.start()
     acc_ref[...] = jnp.zeros_like(acc_ref)
+    hop_ref[...] = jnp.zeros_like(hop_ref)
     inv_ref[...] = jnp.zeros_like(inv_ref)
-    upper_ref[...] = jnp.zeros_like(upper_ref)
-
-    def gram_part(of, store, first, size):
-        turned = u_ref[first : first + size, of].T
-        turned_ref[store, first : first + size] = turned
-        return bf_dot(turned, u_ref[first : first + size, :], NN)
-
-    block0 = pl.ds(0, TILE)
+
+    def tile_of(t):
+        return slice(t * TILE, (t + 1) * TILE)
+
+    def gram_part(lo, hi, first, size):
+        piece = slice(first, first + size)
+        turned = u_ref[piece, lo:hi].T
+        turned_ref[lo:hi, piece] = turned
+        product = bf_dot(turned, u_ref[piece, lo:], NN)
+        if first == 0:
+            gram_ref[lo:hi, lo:] = product
+        else:
+            gram_ref[lo:hi, lo:] = gram_ref[lo:hi, lo:] + product
+
     for c, copy in enumerate(copies):
         copy.wait()
-        product = gram_part(block0, block0, c * long_step, long_step)
-        gram_ref[0] = product if c == 0 else gram_ref[0] + product
-    blocks_copy.wait()
-
-    count = blocks_ref.shape[0]
-    share = -(-count // tiles)
-
-    def one_tile(b, carry):
-        here = pl.ds(pl.multiple_of(b * TILE, TILE), TILE)
-        later = pl.ds(pl.multiple_of(jnp.minimum(b + 1, tiles - 1) * TILE, TILE), TILE)
-        store = pl.ds(pl.multiple_of((b + 1) * TILE, TILE), TILE)
-        tile = gram_ref[0, :, here]
+        gram_part(0, TILE, c * long_step, long_step)
+    for copy in more:
+        copy.wait()
+
+    def onsite_product(j):
+        add_product(j, None, acc_ref, u_ref, blocks_ref, rows_ref, cols_ref, 0)
+
+    def coupling_product(j):
+        base = (orbitals - surface) // TILE
+        add_product(j, None, hop_ref, next_ref, cblocks_ref, crows_ref, ccols_ref, base)
+
+    def reduce_part(out_ref, base, source_ref, first):
+        left = turned_ref[:, base + first : base + first + step]
+        product = bf_dot(left, source_ref[first : first + step, :].astype(BF16), NN)
+        out_ref[...] = product if first == 0 else out_ref[...] + product
+
+    def schur(i, j, t):
+        gram_ref[tile_of(i), tile_of(j)] = gram_ref[tile_of(i), tile_of(j)] - exact_dot(
+            upper_ref[tile_of(t), tile_of(i)], upper_ref[tile_of(t), tile_of(j)], TN
+        )
+
+    def inverse_sum(i, t):
+        width = slice(0, (t + 1) * TILE)
+        inv_ref[tile_of(i), width] = inv_ref[tile_of(i), width] - exact_dot(
+            upper_ref[tile_of(t), tile_of(i)], inv_ref[tile_of(t), width], TN
+        )
+
+    def inverse_row(i):
+        width = slice(0, i * TILE)
+        inv_ref[tile_of(i), width] = exact_dot(
+            inv_ref[tile_of(i), tile_of(i)], inv_ref[tile_of(i), width], NN
+        )
+
+    call = functools.partial
+    products = [call(onsite_product, j) for j in range(blocks_ref.shape[0])]
+    products += [call(coupling_product, j) for j in range(cblocks_ref.shape[0])]
+    reductions = [call(reduce_part, w_ref, 0, acc_ref, c * step) for c in range(panels)]
+    reductions += [
+        call(reduce_part, m_ref, orbitals - surface, hop_ref, first)
+        for first in range(0, surface, step)
+    ]
+    plan = {(t, g): [] for t in range(tiles) for g in range(panels)}
+    for g in range(panels):
+        plan[0, g].append(call(gram_part, TILE, modes, g * step, step))
+    room = [(t, g) for t in range(tiles - 1) for g in range(panels)]
+    for n, work in enumerate(products):
+        plan[room[n * len(room) // len(products)]].append(work)
+    for n, work in enumerate(reductions):
+        plan[tiles - 1, n * panels // len(reductions)].append(work)
+    for t in range(1, tiles):
+        late = []
+        if t > 1:
+            late.append(call(inverse_row, t - 1))
+        late += [call(schur, i, j, t - 1) for i in range(t, tiles) for j in range(i, tiles)][1:]
+        late += [call(inverse_sum, i, t - 1) for i in range(t, tiles)]
+        for n, work in enumerate(late):
+            plan[t, n * (panels - 2) // len(late)].insert(0, work)
+
+    def one_tile(t):
+        here = tile_of(t)
+        tile = gram_ref[here, here]
         on_diagonal = lax.broadcasted_iota(jnp.int32, tile.shape, 0) == lax.broadcasted_iota(
             jnp.int32, tile.shape, 1
         )
@@ -189,67 +258,27 @@
         ax_ref[:, TILE:] = on_diagonal.astype(F32)
 
         def between(g):
-            product = gram_part(later, store, g * step, step)
-            gram_ref[1] = product if g == 0 else gram_ref[1] + product
-            for t in range(share):
-                if t * panels // share == g:
-                    j = b * share + t
-                    live = None
-                    if share * tiles != count:
-                        live = j < count
-                        j = jnp.minimum(j, count - 1)
-                    add_product(j, live, acc_ref, u_ref, blocks_ref, rows_ref, cols_ref, 0)
+            for work in plan[t, g]:
+                work()
 
         factor_tile(ax_ref, col_ref, between)
         x = ax_ref[:, TILE:] * across
-        inv_part = exact_dot(upper_ref[:, here], inv_ref[...], TN)
-        inv_ref[here, :] = -exact_dot(x, inv_part, NN)
         inv_ref[here, here] = x
-        upper_ref[here, :] = exact_dot(x, gram_ref[0], NN)
-        gram_ref[0] = gram_ref[1] - exact_dot(upper_ref[:, later], upper_ref[...], TN)
+        if t + 1 < tiles:
+            upper_ref[here, (t + 1) * TILE :] = exact_dot(x, gram_ref[here, (t + 1) * TILE :], NN)
+            schur(t + 1, t + 1, t)
+        else:
+            inverse_row(t)
+
+    def step_of(b, carry):
+        for t in range(tiles):
+            pl.when(b == t)(call(one_tile, t))
         return carry
 
-    lax.fori_loop(0, tiles, one_tile, 0)
-    f_ref[...] = inv_ref[...].T.astype(BF16)
-    for c in range(chunks):
-        part = slice(c * long_step, (c + 1) * long_step)
-        product = bf_dot(turned_ref[:modes, part], acc_ref[part, :].astype(BF16), NN)
-        w_ref[...] = product if c == 0 else w_ref[...] + product
-
-
-def link_kernel(
-    rows_ref,
-    cols_ref,
-    next_hbm,
-    blocks_hbm,
-    u_hbm,
-    f_hbm,
-    yt_ref,
-    hop_ref,
-    next_ref,
-    blocks_ref,
-    tail_ref,
-    f_ref,
-    sems,
-):
-    surface = tail_ref.shape[0]
-    base = u_hbm.shape[0] - surface
-    pairs = [
-        (next_hbm, next_ref),
-        (blocks_hbm, blocks_ref),
-        (u_hbm.at[pl.ds(base, surface)], tail_ref),
-        (f_hbm, f_ref),
-    ]
-    copies = [pltpu.make_async_copy(a, b, sems.at[n]) for n, (a, b) in enumerate(pairs)]
-    for copy in copies:
-        copy.start()
-    hop_ref[...] = jnp.zeros_like(hop_ref)
-    for copy in copies:
-        copy.wait()
-    for j in range(blocks_ref.shape[0]):
-        add_product(j, None, hop_ref, next_ref, blocks_ref, rows_ref, cols_ref, base // TILE)
-    high, low = split(bf_dot(tail_ref[...], hop_ref[...].astype(BF16), TN))
-    factor = f_ref[...]
+    lax.fori_loop(0, tiles, step_of, 0)
+    factor = inv_ref[...].T.astype(BF16)
+    f_ref[...] = factor
+    high, low = split(m_ref[...])
     yt_ref[...] = (bf_dot(high, factor, TN) + bf_dot(low, factor, TN)).astype(BF16)
 
 
@@ -320,53 +349,52 @@
     count = onsite_blocks.shape[1]
     links = coupling_blocks.shape[1]
     place = lax.axis_index("slab").astype(jnp.int32).reshape(1)
+    slabs = lax.axis_size("slab")
     next_head = passed_along(u[:surface], "slab", -1)
-    slabs = lax.axis_size("slab")
     steps = lax.all_to_all(
         jnp.broadcast_to(potential_step[:, None], (slabs, TILE)), "slab", 0, 0, tiled=True
     )
 
-    factor, w = pl.pallas_call(
+    factor, yt, w = pl.pallas_call(
         factor_kernel,
-        out_shape=(struct((modes, modes), BF16), struct((modes, modes), F32)),
-        in_specs=[INTO_SMEM] * 2 + [ANY] * 2,
-        out_specs=(INTO_VMEM,) * 2,
+        out_shape=(
+            struct((modes, modes), BF16),
+            struct((modes, modes), BF16),
+            struct((modes, modes), F32),
+        ),
+        in_specs=[INTO_SMEM] * 4 + [ANY] * 4,
+        out_specs=(INTO_VMEM,) * 3,
         scratch_shapes=[
-            pltpu.VMEM((2, TILE, modes), F32),
+            pltpu.VMEM((modes, modes), F32),
             pltpu.VMEM((modes, modes), F32),
             pltpu.VMEM((modes, modes), F32),
             pltpu.VMEM((TILE, 2 * TILE), F32),
             pltpu.VMEM((ROWS, ROWS, TILE), F32),
             pltpu.VMEM((orbitals, modes), BF16),
-            pltpu.VMEM((modes + TILE, orbitals), BF16),
+            pltpu.VMEM((modes, orbitals), BF16),
             pltpu.VMEM((count, TILE, TILE), BF16),
             pltpu.VMEM((orbitals, modes), F32),
-            pltpu.SemaphoreType.DMA((1,)),
+            pltpu.VMEM((surface, modes), BF16),
+            pltpu.VMEM((links, TILE, TILE), BF16),
+            pltpu.VMEM((surface, modes), F32),
+            pltpu.VMEM((modes, modes), F32),
+            pltpu.SemaphoreType.DMA((3,)),
             pltpu.SemaphoreType.DMA((8,)),
         ],
         compiler_params=PARAMS,
         cost_estimate=cost(8 * orbitals * modes * modes, orbitals * modes * 2),
         name="factor",
-    )(onsite_rows[0], onsite_cols[0], u, onsite_blocks[0])
+    )(
+        onsite_rows[0],
+        onsite_cols[0],
+        coupling_rows[0],
+        coupling_cols[0],
+        next_head,
+        u,
+        onsite_blocks[0],
+        coupling_blocks[0],
+    )
     next_factor = passed_along(factor, "slab", -1)
-
-    yt = pl.pallas_call(
-        link_kernel,
-        out_shape=struct((modes, modes), BF16),
-        in_specs=[INTO_SMEM] * 2 + [ANY] * 4,
-        out_specs=INTO_VMEM,
-        scratch_shapes=[
-            pltpu.VMEM((surface, modes), F32),
-            pltpu.VMEM((surface, modes), BF16),
-            pltpu.VMEM((links, TILE, TILE), BF16),
-            pltpu.VMEM((surface, modes), BF16),
-            pltpu.VMEM((modes, modes), BF16),
-            pltpu.SemaphoreType.DMA((4,)),
-        ],
-        compiler_params=PARAMS,
-        cost_estimate=cost(2 * links * TILE * TILE * modes, 4 * surface * modes * 2),
-        name="link",
-    )(coupling_rows[0], coupling_cols[0], next_head, coupling_blocks[0], u, factor)
     last_yt = passed_along(yt, "slab", 1)
 
     onsite, done = pl.pallas_call(

time: 54.7 us -> 46.3 us (0.85)
  the two profiles are of different devices: /device:TPU:8 before, /device:TPU:1 now
where the time goes in v4:
time: 46.3 us; the launch traced here: 46 us
  Pallas kernels  23.4 us (51%)
  starting transfers between devices  15 us (32%)
  local copies, waits for them, and re-layouts  3.66 us (8%)
  waiting for transfers between devices  2.57 us (6%)
  between operations  1.34 us (3%)
    pallas_call x1, Pallas kernels, shards(): pl.pallas_call(factor_kernel, out_shape=(struct((modes, modes), BF16), st...  18.9 us
    ppermute x3, starting transfers between devices, passed_along(): return lax.ppermute(block, axis, route)  7.53 us
    all_to_all x1, starting transfers between devices, shards(): lax.all_to_all(jnp.broadcast_to(potential_step[:, None], (slabs, TILE)),...  7.43 us
    pallas_call x1, Pallas kernels, shards(): pl.pallas_call(onsite_kernel, out_shape=(struct((modes, modes), F32), str...  3.15 us
    ppermute x3, waiting for transfers between devices, passed_along(): return lax.ppermute(block, axis, route)  2.57 us
    unnamed x10, local copies, waits for them, and re-layouts  2.02 us
    pallas_call x1, Pallas kernels, shards(): pl.pallas_call(couple_kernel, out_shape=(struct((modes, modes), F32),) *...  1.4 us
    slice x1, local copies, waits for them, and re-layouts, shards(): next_head = passed_along(u[:surface], 'slab', -1)  1.04 us
  transfers between devices with their start and end apart: 4, of which 1 were waited for; matrix products, arithmetic and copies ran while one was open for 1% of the time, Pallas kernels for 48%

profile of v4, /device:TPU:1, one launch (start us, length us, event | category | flops | bytes accessed | tf_op | source)
XLA Modules:
  0.0 46.0 jit_solution(8758176224209764693)
XLA Ops:
  0.6 1.0 %slice_bitcast_fusion = bf16[512,384]{1,0:T(8,128)(2,1)S(1)} fusion(bf16[1,4096,384]{2,1,0:T(8,128)(2,1)} %param.8), kind=kLoop, calls=%fused_computation | loop fusion | bytes 786432 | tf_op jit(solution)/shard_map/slice | solution.py:353
  1.7 2.0 %collective-permute-start = (bf16[512,384]{1,0:T(8,128)(2,1)S(1)}, bf16[512,384]{1,0:T(8,128)(2,1)S(1)}, u32[]{:S(2)}, u32[]{:S(2)}) collective-permute-start(bf16[512,384]{1,0:T(8,128)(2,1)S(1)} %slice_bitcast_fusion), channel_id=1, source_target_pairs={{1,0},{2,1},{3,2},{4,3},{5,4},{6,5},{7,6},{8,7},{9,8},{10,9},{11,1... | collective-permute-start | bytes 1179656 | tf_op jit(solution)/shard_map/ppermute | solution.py:329
  4.3 0.6 %broadcast_in_dim.18 = f32[16,1,128]{2,1,0:T(1,128)} broadcast(f32[]{:T(128)} %bitcast.15), dimensions={} | broadcast | bytes 8196 | tf_op jit(solution)/shard_map/broadcast_in_dim | solution.py:355
  4.9 7.4 %all-to-all-start = ((f32[16,1,128]{2,1,0:T(1,128)}), f32[16,1,128]{2,1,0:T(1,128)S(1)}, u32[]{:S(2)}, u32[]{:S(2)}) async-start(f32[16,1,128]{2,1,0:T(1,128)} %broadcast_in_dim.18), calls=%async_computation | async-start | bytes 16384 | tf_op jit(solution)/shard_map/all_to_all | solution.py:354
  12.3 0.0 collective-permute-done.next_hbm
  12.3 0.0 copy-start.4
  12.3 0.7 %copy-done.4 = bf16[512,384]{1,0:T(8,128)(2,1)} copy-done((bf16[512,384]{1,0:T(8,128)(2,1)}, bf16[512,384]{1,0:T(8,128)(2,1)S(1)}, u32[]{:S(2)}) %copy-start.4) | copy-done | bytes 393240
  13.1 18.9 %factor.1 = (bf16[384,384]{1,0:T(8,128)(2,1)}, bf16[384,384]{1,0:T(8,128)(2,1)}, f32[384,384]{1,0:T(8,128)}) custom-call(s32[96]{0:T(128)} %bitcast.22, s32[96]{0:T(128)} %bitcast.23, s32[16]{0:T(128)} %bitcast.24, s32[16]{0:T(128)} %bitcast.25, bf16[512,384]{1,0:T(8,128)(2,1)} %copy-done.4, bf16[4096,384]{1,0:T(8,128)(2,1)} %bitcast.16, ...), custom_call_target="tpu_custom_call" | custom-call | flops 4831838208 | bytes 3145728 | tf_op jit(solution)/shard_map/factor/pallas_call | solution.py:358
  32.0 2.0 %collective-permute-start.1 = (bf16[384,384]{1,0:T(8,128)(2,1)}, bf16[384,384]{1,0:T(8,128)(2,1)S(1)}, u32[]{:S(2)}, u32[]{:S(2)}) collective-permute-start(bf16[384,384]{1,0:T(8,128)(2,1)} %get-tuple-element.11.f_ref), channel_id=1, source_target_pairs={{1,0},{2,1},{3,2},{4,3},{5,4},{6,5},{7,6},{8,7},{9,8},{10,9},{11,1... | collective-permute-start | bytes 884744 | tf_op jit(solution)/shard_map/ppermute | solution.py:329
  34.0 3.5 %collective-permute-start.2 = (bf16[384,384]{1,0:T(8,128)(2,1)}, bf16[384,384]{1,0:T(8,128)(2,1)S(1)}, u32[]{:S(2)}, u32[]{:S(2)}) collective-permute-start(bf16[384,384]{1,0:T(8,128)(2,1)} %get-tuple-element.12.order_ref.yt_ref), channel_id=1, source_target_pairs={{0,1},{1,2},{2,3},{3,4},{4,5},{5,6},{6,7},{7,8},{8,9},{9,10},{10,1... | collective-permute-start | bytes 884744 | tf_op jit(solution)/shard_map/ppermute | solution.py:329
  37.5 0.0 all-to-all-done
  37.6 0.0 copy-start.3
  37.6 0.6 %copy-done.3 = f32[16,1,128]{2,1,0:T(1,128)} copy-done((f32[16,1,128]{2,1,0:T(1,128)}, f32[16,1,128]{2,1,0:T(1,128)S(1)}, u32[]{:S(2)}) %copy-start.3) | copy-done | bytes 8216
  38.2 0.0 copy-start
  38.2 0.0 copy-start.1
  38.2 3.2 %onsite.1 = (f32[384,384]{1,0:T(8,128)}, f32[8,128]{1,0:T(8,128)}) custom-call(s32[1]{0:T(128)} %bitcast.place_ref, f32[384,384]{1,0:T(8,128)} %get-tuple-element.10.w_ref, bf16[384,384]{1,0:T(8,128)(2,1)} %get-tuple-element.11.f_ref, f32[16,128]{1,0:T(8,128)} %bitcast.17, bf16[384,384]{1,0:T(8,128)(2,1)} %get-tuple-element.12.order_ref.yt_ref), custom_call_target="tpu_custom_call" | custom-call | flops 4831838208 | bytes 6291456 | tf_op jit(solution)/shard_map/onsite/pallas_call | solution.py:400
  41.3 0.0 collective-permute-done.1.next_f_ref
  41.3 2.6 %collective-permute-done.2.last_yt_ref = bf16[384,384]{1,0:T(8,128)(2,1)S(1)} collective-permute-done((bf16[384,384]{1,0:T(8,128)(2,1)}, bf16[384,384]{1,0:T(8,128)(2,1)S(1)}, u32[]{:S(2)}, u32[]{:S(2)}) %collective-permute-start.2) | collective-permute-done | bytes 294944 | tf_op jit(solution)/shard_map/ppermute | solution.py:329
  43.9 0.0 copy-done
  43.9 0.0 copy-done.1
  43.9 0.0 copy-start.2
  43.9 0.7 %copy-done.2 = f32[8,128]{1,0:T(8,128)S(1)} copy-done((f32[8,128]{1,0:T(8,128)S(1)}, f32[8,128]{1,0:T(8,128)}, u32[]{:S(2)}) %copy-start.2) | copy-done | bytes 4120
  44.6 1.4 %couple.1 = (f32[384,384]{1,0:T(8,128)}, f32[384,384]{1,0:T(8,128)}) custom-call(bf16[384,384]{1,0:T(8,128)(2,1)S(1)} %copy-done.1, bf16[384,384]{1,0:T(8,128)(2,1)S(1)} %collective-permute-done.1.next_f_ref, bf16[384,384]{1,0:T(8,128)(2,1)S(1)} %copy-done, bf16[384,384]{1,0:T(8,128)(2,1)S(1)} %collective-permute-done.2.last_yt_ref, f32[8,128]{1,0:T(8,128)S(1)} %copy-done.2), custom_call_target="tpu_custom_call" | custom-call | flops 226492416 | bytes 2359296 | tf_op jit(solution)/shard_map/couple/pallas_call | solution.py:410
Async XLA Ops:
  1.7 10.7 %collective-permute-start = (bf16[512,384]{1,0:T(8,128)(2,1)S(1)}, bf16[512,384]{1,0:T(8,128)(2,1)S(1)}, u32[]{:S(2)}, u32[]{:S(2)}) collective-permute-start(bf16[512,384]{1,0:T(8,128)(2,1)S(1)} %slice_bitcast_fusion), channel_id=1, source_target_pairs={{1,0},{2,1},{3,2},{4,3},{5,4},{6,5},{7,6},{8,7},{9,8},{10,9},{11,1... | collective-permute-start | bytes 1179656 | tf_op jit(solution)/shard_map/ppermute | solution.py:329
  4.9 32.7 %all-to-all-start = ((f32[16,1,128]{2,1,0:T(1,128)}), f32[16,1,128]{2,1,0:T(1,128)S(1)}, u32[]{:S(2)}, u32[]{:S(2)}) async-start(f32[16,1,128]{2,1,0:T(1,128)} %broadcast_in_dim.18), calls=%async_computation | async-start | bytes 16384 | tf_op jit(solution)/shard_map/all_to_all | solution.py:354
  12.3 0.7 %copy-start.4 = (bf16[512,384]{1,0:T(8,128)(2,1)}, bf16[512,384]{1,0:T(8,128)(2,1)S(1)}, u32[]{:S(2)}) copy-start(bf16[512,384]{1,0:T(8,128)(2,1)S(1)} %collective-permute-done.next_hbm) | copy-start | bytes 1179652
  32.0 9.4 %collective-permute-start.1 = (bf16[384,384]{1,0:T(8,128)(2,1)}, bf16[384,384]{1,0:T(8,128)(2,1)S(1)}, u32[]{:S(2)}, u32[]{:S(2)}) collective-permute-start(bf16[384,384]{1,0:T(8,128)(2,1)} %get-tuple-element.11.f_ref), channel_id=1, source_target_pairs={{1,0},{2,1},{3,2},{4,3},{5,4},{6,5},{7,6},{8,7},{9,8},{10,9},{11,1... | collective-permute-start | bytes 884744 | tf_op jit(solution)/shard_map/ppermute | solution.py:329
  34.0 9.9 %collective-permute-start.2 = (bf16[384,384]{1,0:T(8,128)(2,1)}, bf16[384,384]{1,0:T(8,128)(2,1)S(1)}, u32[]{:S(2)}, u32[]{:S(2)}) collective-permute-start(bf16[384,384]{1,0:T(8,128)(2,1)} %get-tuple-element.12.order_ref.yt_ref), channel_id=1, source_target_pairs={{0,1},{1,2},{2,3},{3,4},{4,5},{5,6},{6,7},{7,8},{8,9},{9,10},{10,1... | collective-permute-start | bytes 884744 | tf_op jit(solution)/shard_map/ppermute | solution.py:329
  37.6 0.6 %copy-start.3 = (f32[16,1,128]{2,1,0:T(1,128)}, f32[16,1,128]{2,1,0:T(1,128)S(1)}, u32[]{:S(2)}) copy-start(f32[16,1,128]{2,1,0:T(1,128)S(1)} %all-to-all-done) | copy-start | bytes 24580
  38.2 5.7 %copy-start = (bf16[384,384]{1,0:T(8,128)(2,1)S(1)}, bf16[384,384]{1,0:T(8,128)(2,1)}, u32[]{:S(2)}) copy-start(bf16[384,384]{1,0:T(8,128)(2,1)} %get-tuple-element.11.f_ref) | copy-start | bytes 884740
  38.2 5.7 %copy-start.1 = (bf16[384,384]{1,0:T(8,128)(2,1)S(1)}, bf16[384,384]{1,0:T(8,128)(2,1)}, u32[]{:S(2)}) copy-start(bf16[384,384]{1,0:T(8,128)(2,1)} %get-tuple-element.12.order_ref.yt_ref) | copy-start | bytes 884740
  43.9 0.7 %copy-start.2 = (f32[8,128]{1,0:T(8,128)S(1)}, f32[8,128]{1,0:T(8,128)}, u32[]{:S(2)}) copy-start(f32[8,128]{1,0:T(8,128)} %get-tuple-element.14.order_ref) | copy-start | bytes 12292

commit v5 on v4

--- a/solution.py
+++ b/solution.py
@@ -9,7 +9,6 @@
 
 F32 = jnp.float32
 BF16 = jnp.bfloat16
-VMEM_LIMIT = 63900000
 SURFACE = 4
 TILE = 128
 ROWS = 8
@@ -21,21 +20,6 @@
 
 def row(ref, k, width):
     return jnp.broadcast_to(ref[k : k + 1, :], (ROWS, width))
-
-
-def exact_dot(a, b, dims):
-    return lax.dot_general(
-        a, b, (dims, ((), ())), precision=lax.Precision.HIGHEST, preferred_element_type=F32
-    )
-
-
-def bf_dot(a, b, dims):
-    return lax.dot_general(a, b, (dims, ((), ())), preferred_element_type=F32)
-
-
-NN = ((1,), (0,))
-TN = ((0,), (0,))
-NT = ((1,), (1,))
 
 
 def three_parts(value):
@@ -44,16 +28,40 @@
     return a, b, value - a - b
 
 
-def factor_tile(ax_ref, col_ref, between):
+def exact_dot(a, b):
+    a0, a1, a2 = (part.astype(BF16) for part in three_parts(a))
+    b0, b1, b2 = (part.astype(BF16) for part in three_parts(b))
+    return bf_dot(
+        jnp.concatenate([a0, a0, a1, a1, a0, a2], axis=1),
+        jnp.concatenate([b0, b1, b0, b1, b2, b0], axis=0),
+        NN,
+    )
+
+
+def bf_dot(a, b, dims):
+    return lax.dot_general(a, b, (dims, ((), ())), preferred_element_type=F32)
+
+
+NN = ((1,), (0,))
+TN = ((0,), (0,))
+NT = ((1,), (1,))
+
+
+def factor_tile(ax_ref, col_ref, below_ref, between):
     width = ax_ref.shape[1]
     panels = ax_ref.shape[0] // ROWS
     near = 2
+    first_rows = ax_ref[:ROWS, :TILE]
+    columns = [lane(first_rows, j) for j in range(ROWS)]
     for g in range(panels):
         base = ROWS * g
-        here = ax_ref[base : base + ROWS, :TILE]
         for j in range(ROWS):
-            col_ref[j] = lane(here, base + j)
-        s = {(i, j): row(col_ref.at[j], i, TILE) for j in range(ROWS) for i in range(j, ROWS)}
+            col_ref[g % 2, j] = columns[j]
+        s = {
+            (i, j): row(col_ref.at[g % 2, j], i, TILE)
+            for j in range(ROWS)
+            for i in range(j, ROWS)
+        }
         low, r = {}, []
         for p in range(0, ROWS, 2):
             q = p + 1
@@ -74,6 +82,23 @@
                 for i in range(j, ROWS):
                     both = side[j][0] * s[i, p] + side[j][1] * s[i, q]
                     s[i, j] = s[i, j] - both * inverse
+        blocks, belows = {}, {}
+        for i in range(g + 1, min(g + 1 + near, panels)):
+            block = ax_ref[ROWS * i : ROWS * (i + 1), :]
+            below = []
+            for k in range(ROWS):
+                column = lane(block[:, :TILE], base + k)
+                for m in range(k):
+                    column = column - below[m] * low[k, m]
+                below.append(column * r[k])
+            blocks[i], belows[i] = block, below
+        if g + 1 < panels:
+            below = belows[g + 1]
+            columns = [lane(blocks[g + 1][:, :TILE], base + ROWS + j) for j in range(ROWS)]
+            for k in range(ROWS):
+                below_ref[g % 2, k] = below[k]
+                for j in range(ROWS):
+                    columns[j] = columns[j] - below[k] * row(below_ref.at[g % 2, k], j, TILE)
         r2 = [jnp.concatenate([v, v], axis=1) for v in r]
         low2 = {key: jnp.concatenate([v, v], axis=1) for key, v in low.items()}
         z = []
@@ -86,18 +111,10 @@
         packed = z[0]
         for k in range(1, ROWS):
             packed = jnp.where(sub == k, z[k], packed)
-        for i in range(g + 1, min(g + 1 + near, panels)):
-            at = ROWS * i
-            block = ax_ref[at : at + ROWS, :]
-            below = []
+        for i, block in blocks.items():
             for k in range(ROWS):
-                column = lane(block[:, :TILE], base + k)
-                for m in range(k):
-                    column = column - below[m] * low[k, m]
-                below.append(column * r[k])
-            for k in range(ROWS):
-                block = block - jnp.concatenate([below[k], below[k]], axis=1) * z[k]
-            ax_ref[at : at + ROWS, :] = block
+                block = block - jnp.concatenate([belows[i][k], belows[i][k]], axis=1) * z[k]
+            ax_ref[ROWS * i : ROWS * (i + 1), :] = block
         ax_ref[base : base + ROWS, TILE:] = packed[:, TILE:]
         far = ROWS * (g + 1 + near)
         if far < ax_ref.shape[0]:
@@ -128,6 +145,7 @@
     blocks_hbm,
     cblocks_hbm,
     f_ref,
+    packed_ref,
     yt_ref,
     w_ref,
     gram_ref,
@@ -135,6 +153,7 @@
     inv_ref,
     ax_ref,
     col_ref,
+    below_ref,
     u_ref,
     turned_ref,
     blocks_ref,
@@ -188,8 +207,10 @@
     for c, copy in enumerate(copies):
         copy.wait()
         gram_part(0, TILE, c * long_step, long_step)
-    for copy in more:
-        copy.wait()
+
+    def wait_more():
+        for copy in more:
+            copy.wait()
 
     def onsite_product(j):
         add_product(j, None, acc_ref, u_ref, blocks_ref, rows_ref, cols_ref, 0)
@@ -205,19 +226,19 @@
 
     def schur(i, j, t):
         gram_ref[tile_of(i), tile_of(j)] = gram_ref[tile_of(i), tile_of(j)] - exact_dot(
-            upper_ref[tile_of(t), tile_of(i)], upper_ref[tile_of(t), tile_of(j)], TN
+            upper_ref[tile_of(t), tile_of(i)].T, upper_ref[tile_of(t), tile_of(j)]
         )
 
     def inverse_sum(i, t):
         width = slice(0, (t + 1) * TILE)
         inv_ref[tile_of(i), width] = inv_ref[tile_of(i), width] - exact_dot(
-            upper_ref[tile_of(t), tile_of(i)], inv_ref[tile_of(t), width], TN
+            upper_ref[tile_of(t), tile_of(i)].T, inv_ref[tile_of(t), width]
         )
 
     def inverse_row(i):
         width = slice(0, i * TILE)
         inv_ref[tile_of(i), width] = exact_dot(
-            inv_ref[tile_of(i), tile_of(i)], inv_ref[tile_of(i), width], NN
+            inv_ref[tile_of(i), tile_of(i)], inv_ref[tile_of(i), width]
         )
 
     call = functools.partial
@@ -231,7 +252,8 @@
     plan = {(t, g): [] for t in range(tiles) for g in range(panels)}
     for g in range(panels):
         plan[0, g].append(call(gram_part, TILE, modes, g * step, step))
-    room = [(t, g) for t in range(tiles - 1) for g in range(panels)]
+    plan[0, 3].append(wait_more)
+    room = [(t, g) for t in range(tiles - 1) for g in range(panels)][4:]
     for n, work in enumerate(products):
         plan[room[n * len(room) // len(products)]].append(work)
     for n, work in enumerate(reductions):
@@ -261,11 +283,11 @@
             for work in plan[t, g]:
                 work()
 
-        factor_tile(ax_ref, col_ref, between)
+        factor_tile(ax_ref, col_ref, below_ref, between)
         x = ax_ref[:, TILE:] * across
         inv_ref[here, here] = x
         if t + 1 < tiles:
-            upper_ref[here, (t + 1) * TILE :] = exact_dot(x, gram_ref[here, (t + 1) * TILE :], NN)
+            upper_ref[here, (t + 1) * TILE :] = exact_dot(x, gram_ref[here, (t + 1) * TILE :])
             schur(t + 1, t + 1, t)
         else:
             inverse_row(t)
@@ -278,13 +300,22 @@
     lax.fori_loop(0, tiles, step_of, 0)
     factor = inv_ref[...].T.astype(BF16)
     f_ref[...] = factor
+    packed_ref[...] = factor[: 2 * TILE, :]
+    packed_ref[TILE:, :TILE] = factor[2 * TILE :, 2 * TILE :]
     high, low = split(m_ref[...])
     yt_ref[...] = (bf_dot(high, factor, TN) + bf_dot(low, factor, TN)).astype(BF16)
 
 
-def couple_kernel(yt_ref, next_f_ref, f_ref, last_yt_ref, order_ref, right_ref, left_ref):
-    right_ref[...] = bf_dot(yt_ref[...], next_f_ref[...], TN)
+def left_kernel(f_ref, last_yt_ref, left_ref):
     left_ref[...] = bf_dot(f_ref[...], last_yt_ref[...], TN)
+
+
+def first_kernel(step_ref, u_hbm, head_hbm, steps_ref, sem):
+    surface = head_hbm.shape[0]
+    copy = pltpu.make_async_copy(u_hbm.at[pl.ds(0, surface)], head_hbm, sem.at[0])
+    copy.start()
+    steps_ref[...] = jnp.full(steps_ref.shape, step_ref[0], F32)
+    copy.wait()
 
 
 def split(value):
@@ -292,7 +323,9 @@
     return high, (value - high.astype(F32)).astype(BF16)
 
 
-def onsite_kernel(place_ref, w_ref, f_ref, steps_ref, order_ref, out_ref, done_ref):
+def onsite_kernel(
+    place_ref, w_ref, f_ref, steps_ref, yt_ref, next_ref, out_ref, right_ref, full_ref
+):
     modes = f_ref.shape[0]
     w = w_ref[...]
     w = w + w.T
@@ -307,7 +340,11 @@
     i = lax.broadcasted_iota(jnp.int32, (modes, modes), 0)
     j = lax.broadcasted_iota(jnp.int32, (modes, modes), 1)
     out_ref[...] = full + jnp.where(i == j, potential, 0.0)
-    done_ref[...] = jnp.zeros_like(done_ref)
+    full_ref[...] = jnp.zeros_like(full_ref)
+    full_ref[:TILE, :] = next_ref[:TILE, :]
+    full_ref[TILE : 2 * TILE, TILE:] = next_ref[TILE:, TILE:]
+    full_ref[2 * TILE :, 2 * TILE :] = next_ref[TILE:, :TILE]
+    right_ref[...] = bf_dot(yt_ref[...], full_ref[...], TN)
 
 
 def struct(shape, dtype):
@@ -319,8 +356,8 @@
 INTO_SMEM = pl.BlockSpec(memory_space=pltpu.SMEM)
 
 
-PARAMS = pltpu.CompilerParams(vmem_limit_bytes=VMEM_LIMIT)
-SMALL = pltpu.CompilerParams(vmem_limit_bytes=8 * 1024 * 1024)
+def params(mebibytes):
+    return pltpu.CompilerParams(vmem_limit_bytes=mebibytes * 1024 * 1024)
 
 
 def passed_along(block, axis, distance):
@@ -350,26 +387,36 @@
     links = coupling_blocks.shape[1]
     place = lax.axis_index("slab").astype(jnp.int32).reshape(1)
     slabs = lax.axis_size("slab")
-    next_head = passed_along(u[:surface], "slab", -1)
-    steps = lax.all_to_all(
-        jnp.broadcast_to(potential_step[:, None], (slabs, TILE)), "slab", 0, 0, tiled=True
-    )
-
-    factor, yt, w = pl.pallas_call(
+    head, step_rows = pl.pallas_call(
+        first_kernel,
+        out_shape=(struct((surface, modes), BF16), struct((slabs, TILE), F32)),
+        in_specs=[INTO_SMEM, ANY],
+        out_specs=(ANY, INTO_VMEM),
+        scratch_shapes=[pltpu.SemaphoreType.DMA((1,))],
+        compiler_params=params(59),
+        cost_estimate=cost(0, 4 * surface * modes),
+        name="first",
+    )(potential_step, u)
+    next_head = passed_along(head, "slab", -1)
+    steps = lax.all_to_all(step_rows, "slab", 0, 0, tiled=True)
+
+    factor, packed, yt, w = pl.pallas_call(
         factor_kernel,
         out_shape=(
             struct((modes, modes), BF16),
+            struct((modes - TILE, modes), BF16),
             struct((modes, modes), BF16),
             struct((modes, modes), F32),
         ),
         in_specs=[INTO_SMEM] * 4 + [ANY] * 4,
-        out_specs=(INTO_VMEM,) * 3,
+        out_specs=(INTO_VMEM,) * 4,
         scratch_shapes=[
             pltpu.VMEM((modes, modes), F32),
             pltpu.VMEM((modes, modes), F32),
             pltpu.VMEM((modes, modes), F32),
             pltpu.VMEM((TILE, 2 * TILE), F32),
-            pltpu.VMEM((ROWS, ROWS, TILE), F32),
+            pltpu.VMEM((2, ROWS, ROWS, TILE), F32),
+            pltpu.VMEM((2, ROWS, ROWS, TILE), F32),
             pltpu.VMEM((orbitals, modes), BF16),
             pltpu.VMEM((modes, orbitals), BF16),
             pltpu.VMEM((count, TILE, TILE), BF16),
@@ -381,7 +428,7 @@
             pltpu.SemaphoreType.DMA((3,)),
             pltpu.SemaphoreType.DMA((8,)),
         ],
-        compiler_params=PARAMS,
+        compiler_params=params(59),
         cost_estimate=cost(8 * orbitals * modes * modes, orbitals * modes * 2),
         name="factor",
     )(
@@ -394,28 +441,29 @@
         onsite_blocks[0],
         coupling_blocks[0],
     )
-    next_factor = passed_along(factor, "slab", -1)
+    next_packed = passed_along(packed, "slab", -1)
     last_yt = passed_along(yt, "slab", 1)
 
-    onsite, done = pl.pallas_call(
+    onsite, right = pl.pallas_call(
         onsite_kernel,
-        out_shape=(struct((modes, modes), F32), struct((ROWS, TILE), F32)),
-        in_specs=[INTO_SMEM] + [INTO_VMEM] * 3 + [ANY],
+        out_shape=(struct((modes, modes), F32),) * 2,
+        in_specs=[INTO_SMEM] + [INTO_VMEM] * 5,
         out_specs=(INTO_VMEM,) * 2,
-        compiler_params=PARAMS,
+        scratch_shapes=[pltpu.VMEM((modes, modes), BF16)],
+        compiler_params=params(16),
         cost_estimate=cost(8 * orbitals * modes * modes, 4 * orbitals * modes),
         name="onsite",
-    )(place, w, factor, steps, yt)
-
-    right, left = pl.pallas_call(
-        couple_kernel,
-        out_shape=(struct((modes, modes), F32),) * 2,
-        in_specs=[INTO_VMEM] * 4 + [ANY],
-        out_specs=(INTO_VMEM,) * 2,
-        compiler_params=SMALL,
-        cost_estimate=cost(4 * modes * modes * modes, 8 * modes * modes * 2),
-        name="couple",
-    )(yt, next_factor, factor, last_yt, done)
+    )(place, w, factor, steps, yt, next_packed)
+
+    left = pl.pallas_call(
+        left_kernel,
+        out_shape=struct((modes, modes), F32),
+        in_specs=[INTO_VMEM] * 2,
+        out_specs=INTO_VMEM,
+        compiler_params=params(8),
+        cost_estimate=cost(2 * modes * modes * modes, 8 * modes * modes),
+        name="left",
+    )(factor, last_yt)
     return (onsite[None], right[None], left[None])
 
 

time: 46.3 us -> 66.5 us (1.44)
  Pallas kernels: 23.4 us -> 35.3 us
  waiting for transfers between devices: 2.57 us -> 10.5 us
    pallas_call x2 -> x3, Pallas kernels: 4.56 us -> 16.9 us  [the longest x1 13.6 us: shards(): pl.pallas_call(first_kernel, out_shape=(struct((surface, modes), BF16), s...]
    ppermute x3, waiting for transfers between devices: 2.57 us -> 8.23 us  [passed_along(): return lax.ppermute(block, axis, route)]
    all_to_all x1, waiting for transfers between devices: 0.01 us -> 2.25 us  [shards(): steps = lax.all_to_all(step_rows, 'slab', 0, 0, tiled=True)]
    unnamed x10 -> x8, local copies, waits for them, and re-layouts: 2.02 us -> 3.73 us
    slice x1 -> x0, local copies, waits for them, and re-layouts: 1.04 us -> none  [shards(): next_head = passed_along(u[:surface], 'slab', -1)]
  transfers between devices with their start and end apart: 4 -> 4, of which waited for: 1 -> 2; matrix products, arithmetic and copies ran while one was open for 1% -> 0% of each run, Pallas kernels for 48% -> 3%
where the time goes in v5:
time: 66.5 us; the launch traced here: 65.5 us
  Pallas kernels  35.3 us (53%)
  starting transfers between devices  14.7 us (22%)
  waiting for transfers between devices  10.5 us (16%)
  local copies, waits for them, and re-layouts  3.73 us (6%)
  between operations  1.32 us (2%)
    pallas_call x1, Pallas kernels, shards(): pl.pallas_call(factor_kernel, out_shape=(struct((modes, modes), BF16), st...  18.4 us
    pallas_call x1, Pallas kernels, shards(): pl.pallas_call(first_kernel, out_shape=(struct((surface, modes), BF16), s...  13.6 us
    ppermute x3, waiting for transfers between devices, passed_along(): return lax.ppermute(block, axis, route)  8.23 us
    ppermute x3, starting transfers between devices, passed_along(): return lax.ppermute(block, axis, route)  7.41 us
    all_to_all x1, starting transfers between devices, shards(): steps = lax.all_to_all(step_rows, 'slab', 0, 0, tiled=True)  7.24 us
    unnamed x8, local copies, waits for them, and re-layouts  3.73 us
    all_to_all x1, waiting for transfers between devices, shards(): steps = lax.all_to_all(step_rows, 'slab', 0, 0, tiled=True)  2.25 us
    pallas_call x1, Pallas kernels, shards(): pl.pallas_call(onsite_kernel, out_shape=(struct((modes, modes), F32),) *...  2.12 us
  transfers between devices with their start and end apart: 4, of which 2 were waited for; matrix products, arithmetic and copies ran while one was open for 0% of the time, Pallas kernels for 3%

profile of v5, /device:TPU:1, one launch (start us, length us, event | category | flops | bytes accessed | tf_op | source)
XLA Modules:
  0.0 65.5 jit_solution(12499244486988197120)
XLA Ops:
  1.3 13.6 %first.1 = (bf16[512,384]{1,0:T(8,128)(2,1)}, f32[16,128]{1,0:T(8,128)}) custom-call(f32[1]{0:T(128)S(6)} %copy.12.step_ref, bf16[4096,384]{1,0:T(8,128)(2,1)} %bitcast.16), custom_call_target="tpu_custom_call" | custom-call | bytes 786432 | tf_op jit(solution)/shard_map/first/pallas_call | solution.py:390
  14.9 2.0 %collective-permute-start = (bf16[512,384]{1,0:T(8,128)(2,1)}, bf16[512,384]{1,0:T(8,128)(2,1)S(1)}, u32[]{:S(2)}, u32[]{:S(2)}) collective-permute-start(bf16[512,384]{1,0:T(8,128)(2,1)} %get-tuple-element.11), channel_id=1, source_target_pairs={{1,0},{2,1},{3,2},{4,3},{5,4},{6,5},{7,6},{8,7},{9,8},{10,9},{11,1... | collective-permute-start | bytes 1179656 | tf_op jit(solution)/shard_map/ppermute | solution.py:366
  16.9 8.2 %collective-permute-done.next_hbm = bf16[512,384]{1,0:T(8,128)(2,1)S(1)} collective-permute-done((bf16[512,384]{1,0:T(8,128)(2,1)}, bf16[512,384]{1,0:T(8,128)(2,1)S(1)}, u32[]{:S(2)}, u32[]{:S(2)}) %collective-permute-start) | collective-permute-done | bytes 393248 | tf_op jit(solution)/shard_map/ppermute | solution.py:366
  25.1 0.0 copy-start.3
  25.1 0.7 %copy-done.3 = bf16[512,384]{1,0:T(8,128)(2,1)} copy-done((bf16[512,384]{1,0:T(8,128)(2,1)}, bf16[512,384]{1,0:T(8,128)(2,1)S(1)}, u32[]{:S(2)}) %copy-start.3) | copy-done | bytes 393240
  25.8 18.4 %factor.1 = (bf16[384,384]{1,0:T(8,128)(2,1)}, bf16[256,384]{1,0:T(8,128)(2,1)}, bf16[384,384]{1,0:T(8,128)(2,1)}, f32[384,384]{1,0:T(8,128)}) custom-call(s32[96]{0:T(128)} %bitcast.21, s32[96]{0:T(128)} %bitcast.22, s32[16]{0:T(128)} %bitcast.23, s32[16]{0:T(128)} %bitcast.24, bf16[512,384]{1,0:T(8,128)(2,1)} %copy-done.3, bf16[4096,384]{1,0:T(8,128)(2,1)} %bitcast.17, ...), custom_call_target="tpu_custom_call" | custom-call | flops 4831838208 | bytes 3145728 | tf_op jit(solution)/shard_map/factor/pallas_call | solution.py:403
  44.2 1.9 %collective-permute-start.1 = (bf16[256,384]{1,0:T(8,128)(2,1)}, bf16[256,384]{1,0:T(8,128)(2,1)S(1)}, u32[]{:S(2)}, u32[]{:S(2)}) collective-permute-start(bf16[256,384]{1,0:T(8,128)(2,1)} %get-tuple-element.16), channel_id=1, source_target_pairs={{1,0},{2,1},{3,2},{4,3},{5,4},{6,5},{7,6},{8,7},{9,8},{10,9},{11,1... | collective-permute-start | bytes 589832 | tf_op jit(solution)/shard_map/ppermute | solution.py:366
  46.2 7.2 %all-to-all-start = ((f32[16,1,128]{2,1,0:T(1,128)}), f32[16,1,128]{2,1,0:T(1,128)S(1)}, u32[]{:S(2)}, u32[]{:S(2)}) async-start(f32[16,1,128]{2,1,0:T(1,128)} %bitcast.9), calls=%async_computation | async-start | bytes 16384 | tf_op jit(solution)/shard_map/all_to_all | solution.py:401
  53.4 3.5 %collective-permute-start.2 = (bf16[384,384]{1,0:T(8,128)(2,1)}, bf16[384,384]{1,0:T(8,128)(2,1)S(1)}, u32[]{:S(2)}, u32[]{:S(2)}) collective-permute-start(bf16[384,384]{1,0:T(8,128)(2,1)} %get-tuple-element.15.yt_ref), channel_id=1, source_target_pairs={{0,1},{1,2},{2,3},{3,4},{4,5},{5,6},{6,7},{7,8},{8,9},{9,10},{10,1... | collective-permute-start | bytes 884744 | tf_op jit(solution)/shard_map/ppermute | solution.py:366
  56.9 2.2 %all-to-all-done = f32[16,1,128]{2,1,0:T(1,128)S(1)} async-done(((f32[16,1,128]{2,1,0:T(1,128)}), f32[16,1,128]{2,1,0:T(1,128)S(1)}, u32[]{:S(2)}, u32[]{:S(2)}) %all-to-all-start) | async-done | bytes 8224 | tf_op jit(solution)/shard_map/all_to_all | solution.py:401
  59.2 0.0 collective-permute-done.1.next_ref
  59.2 0.0 copy-start
  59.2 1.0 %copy-done = bf16[384,384]{1,0:T(8,128)(2,1)S(1)} copy-done((bf16[384,384]{1,0:T(8,128)(2,1)S(1)}, bf16[384,384]{1,0:T(8,128)(2,1)}, u32[]{:S(2)}) %copy-start) | copy-done | bytes 294936
  60.2 0.0 copy-start.1
  60.2 1.0 %copy-done.1 = bf16[384,384]{1,0:T(8,128)(2,1)S(1)} copy-done((bf16[384,384]{1,0:T(8,128)(2,1)S(1)}, bf16[384,384]{1,0:T(8,128)(2,1)}, u32[]{:S(2)}) %copy-start.1) | copy-done | bytes 294936
  61.1 0.0 copy-start.2
  61.1 1.1 %copy-done.2 = f32[384,384]{1,0:T(8,128)S(1)} copy-done((f32[384,384]{1,0:T(8,128)S(1)}, f32[384,384]{1,0:T(8,128)}, u32[]{:S(2)}) %copy-start.2) | copy-done | bytes 589848
  62.2 2.1 %onsite.1 = (f32[384,384]{1,0:T(8,128)}, f32[384,384]{1,0:T(8,128)}) custom-call(s32[1]{0:T(128)} %bitcast.place_ref, f32[384,384]{1,0:T(8,128)S(1)} %copy-done.2, bf16[384,384]{1,0:T(8,128)(2,1)S(1)} %copy-done, f32[16,128]{1,0:T(8,128)S(1)} %bitcast.15, bf16[384,384]{1,0:T(8,128)(2,1)S(1)} %copy-done.1, bf16[256,384]{1,0:T(8,128)(2,1)S(1)} %collective-permute-done.1.next_ref), custom_call_target="tpu_custom_call" | custom-call | flops 4831838208 | bytes 6291456 | tf_op jit(solution)/shard_map/onsite/pallas_call | solution.py:447
  64.3 0.0 collective-permute-done.2.last_yt_ref
  64.3 1.2 %left.1 = f32[384,384]{1,0:T(8,128)} custom-call(bf16[384,384]{1,0:T(8,128)(2,1)S(1)} %copy-done, bf16[384,384]{1,0:T(8,128)(2,1)S(1)} %collective-permute-done.2.last_yt_ref), custom_call_target="tpu_custom_call" | custom-call | flops 113246208 | bytes 1179648 | tf_op jit(solution)/shard_map/left/pallas_call | solution.py:458
Async XLA Ops:
  14.9 10.2 %collective-permute-start = (bf16[512,384]{1,0:T(8,128)(2,1)}, bf16[512,384]{1,0:T(8,128)(2,1)S(1)}, u32[]{:S(2)}, u32[]{:S(2)}) collective-permute-start(bf16[512,384]{1,0:T(8,128)(2,1)} %get-tuple-element.11), channel_id=1, source_target_pairs={{1,0},{2,1},{3,2},{4,3},{5,4},{6,5},{7,6},{8,7},{9,8},{10,9},{11,1... | collective-permute-start | bytes 1179656 | tf_op jit(solution)/shard_map/ppermute | solution.py:366
  25.1 0.7 %copy-start.3 = (bf16[512,384]{1,0:T(8,128)(2,1)}, bf16[512,384]{1,0:T(8,128)(2,1)S(1)}, u32[]{:S(2)}) copy-start(bf16[512,384]{1,0:T(8,128)(2,1)S(1)} %collective-permute-done.next_hbm) | copy-start | bytes 1179652
  44.2 15.0 %collective-permute-start.1 = (bf16[256,384]{1,0:T(8,128)(2,1)}, bf16[256,384]{1,0:T(8,128)(2,1)S(1)}, u32[]{:S(2)}, u32[]{:S(2)}) collective-permute-start(bf16[256,384]{1,0:T(8,128)(2,1)} %get-tuple-element.16), channel_id=1, source_target_pairs={{1,0},{2,1},{3,2},{4,3},{5,4},{6,5},{7,6},{8,7},{9,8},{10,9},{11,1... | collective-permute-start | bytes 589832 | tf_op jit(solution)/shard_map/ppermute | solution.py:366
  46.2 13.0 %all-to-all-start = ((f32[16,1,128]{2,1,0:T(1,128)}), f32[16,1,128]{2,1,0:T(1,128)S(1)}, u32[]{:S(2)}, u32[]{:S(2)}) async-start(f32[16,1,128]{2,1,0:T(1,128)} %bitcast.9), calls=%async_computation | async-start | bytes 16384 | tf_op jit(solution)/shard_map/all_to_all | solution.py:401
  53.4 10.9 %collective-permute-start.2 = (bf16[384,384]{1,0:T(8,128)(2,1)}, bf16[384,384]{1,0:T(8,128)(2,1)S(1)}, u32[]{:S(2)}, u32[]{:S(2)}) collective-permute-start(bf16[384,384]{1,0:T(8,128)(2,1)} %get-tuple-element.15.yt_ref), channel_id=1, source_target_pairs={{0,1},{1,2},{2,3},{3,4},{4,5},{5,6},{6,7},{7,8},{8,9},{9,10},{10,1... | collective-permute-start | bytes 884744 | tf_op jit(solution)/shard_map/ppermute | solution.py:366
  59.2 1.0 %copy-start = (bf16[384,384]{1,0:T(8,128)(2,1)S(1)}, bf16[384,384]{1,0:T(8,128)(2,1)}, u32[]{:S(2)}) copy-start(bf16[384,384]{1,0:T(8,128)(2,1)} %get-tuple-element.13.f_ref) | copy-start | bytes 884740
  60.2 1.0 %copy-start.1 = (bf16[384,384]{1,0:T(8,128)(2,1)S(1)}, bf16[384,384]{1,0:T(8,128)(2,1)}, u32[]{:S(2)}) copy-start(bf16[384,384]{1,0:T(8,128)(2,1)} %get-tuple-element.15.yt_ref) | copy-start | bytes 884740
  61.1 1.1 %copy-start.2 = (f32[384,384]{1,0:T(8,128)S(1)}, f32[384,384]{1,0:T(8,128)}, u32[]{:S(2)}) copy-start(f32[384,384]{1,0:T(8,128)} %get-tuple-element.12.w_ref) | copy-start | bytes 1769476

commit v6 on v5

--- a/solution.py
+++ b/solution.py
@@ -306,16 +306,13 @@
     yt_ref[...] = (bf_dot(high, factor, TN) + bf_dot(low, factor, TN)).astype(BF16)
 
 
-def left_kernel(f_ref, last_yt_ref, left_ref):
+def couple_kernel(yt_ref, next_ref, f_ref, last_yt_ref, right_ref, left_ref, full_ref):
+    full_ref[...] = jnp.zeros_like(full_ref)
+    full_ref[:TILE, :] = next_ref[:TILE, :]
+    full_ref[TILE : 2 * TILE, TILE:] = next_ref[TILE:, TILE:]
+    full_ref[2 * TILE :, 2 * TILE :] = next_ref[TILE:, :TILE]
+    right_ref[...] = bf_dot(yt_ref[...], full_ref[...], TN)
     left_ref[...] = bf_dot(f_ref[...], last_yt_ref[...], TN)
-
-
-def first_kernel(step_ref, u_hbm, head_hbm, steps_ref, sem):
-    surface = head_hbm.shape[0]
-    copy = pltpu.make_async_copy(u_hbm.at[pl.ds(0, surface)], head_hbm, sem.at[0])
-    copy.start()
-    steps_ref[...] = jnp.full(steps_ref.shape, step_ref[0], F32)
-    copy.wait()
 
 
 def split(value):
@@ -323,9 +320,7 @@
     return high, (value - high.astype(F32)).astype(BF16)
 
 
-def onsite_kernel(
-    place_ref, w_ref, f_ref, steps_ref, yt_ref, next_ref, out_ref, right_ref, full_ref
-):
+def onsite_kernel(place_ref, w_ref, f_ref, steps_ref, out_ref):
     modes = f_ref.shape[0]
     w = w_ref[...]
     w = w + w.T
@@ -340,11 +335,6 @@
     i = lax.broadcasted_iota(jnp.int32, (modes, modes), 0)
     j = lax.broadcasted_iota(jnp.int32, (modes, modes), 1)
     out_ref[...] = full + jnp.where(i == j, potential, 0.0)
-    full_ref[...] = jnp.zeros_like(full_ref)
-    full_ref[:TILE, :] = next_ref[:TILE, :]
-    full_ref[TILE : 2 * TILE, TILE:] = next_ref[TILE:, TILE:]
-    full_ref[2 * TILE :, 2 * TILE :] = next_ref[TILE:, :TILE]
-    right_ref[...] = bf_dot(yt_ref[...], full_ref[...], TN)
 
 
 def struct(shape, dtype):
@@ -387,18 +377,10 @@
     links = coupling_blocks.shape[1]
     place = lax.axis_index("slab").astype(jnp.int32).reshape(1)
     slabs = lax.axis_size("slab")
-    head, step_rows = pl.pallas_call(
-        first_kernel,
-        out_shape=(struct((surface, modes), BF16), struct((slabs, TILE), F32)),
-        in_specs=[INTO_SMEM, ANY],
-        out_specs=(ANY, INTO_VMEM),
-        scratch_shapes=[pltpu.SemaphoreType.DMA((1,))],
-        compiler_params=params(59),
-        cost_estimate=cost(0, 4 * surface * modes),
-        name="first",
-    )(potential_step, u)
-    next_head = passed_along(head, "slab", -1)
-    steps = lax.all_to_all(step_rows, "slab", 0, 0, tiled=True)
+    next_head = passed_along(u[:surface], "slab", -1)
+    steps = lax.all_to_all(
+        jnp.broadcast_to(potential_step[:, None], (slabs, TILE)), "slab", 0, 0, tiled=True
+    )
 
     factor, packed, yt, w = pl.pallas_call(
         factor_kernel,
@@ -428,7 +410,7 @@
             pltpu.SemaphoreType.DMA((3,)),
             pltpu.SemaphoreType.DMA((8,)),
         ],
-        compiler_params=params(59),
+        compiler_params=params(40),
         cost_estimate=cost(8 * orbitals * modes * modes, orbitals * modes * 2),
         name="factor",
     )(
@@ -444,26 +426,26 @@
     next_packed = passed_along(packed, "slab", -1)
     last_yt = passed_along(yt, "slab", 1)
 
-    onsite, right = pl.pallas_call(
+    onsite = pl.pallas_call(
         onsite_kernel,
+        out_shape=struct((modes, modes), F32),
+        in_specs=[INTO_SMEM] + [INTO_VMEM] * 3,
+        out_specs=INTO_VMEM,
+        compiler_params=params(40),
+        cost_estimate=cost(8 * orbitals * modes * modes, 4 * orbitals * modes),
+        name="onsite",
+    )(place, w, factor, steps)
+
+    right, left = pl.pallas_call(
+        couple_kernel,
         out_shape=(struct((modes, modes), F32),) * 2,
-        in_specs=[INTO_SMEM] + [INTO_VMEM] * 5,
+        in_specs=[INTO_VMEM] * 4,
         out_specs=(INTO_VMEM,) * 2,
         scratch_shapes=[pltpu.VMEM((modes, modes), BF16)],
-        compiler_params=params(16),
-        cost_estimate=cost(8 * orbitals * modes * modes, 4 * orbitals * modes),
-        name="onsite",
-    )(place, w, factor, steps, yt, next_packed)
-
-    left = pl.pallas_call(
-        left_kernel,
-        out_shape=struct((modes, modes), F32),
-        in_specs=[INTO_VMEM] * 2,
-        out_specs=INTO_VMEM,
-        compiler_params=params(8),
-        cost_estimate=cost(2 * modes * modes * modes, 8 * modes * modes),
-        name="left",
-    )(factor, last_yt)
+        compiler_params=params(40),
+        cost_estimate=cost(4 * modes * modes * modes, 8 * modes * modes),
+        name="couple",
+    )(yt, next_packed, factor, last_yt)
     return (onsite[None], right[None], left[None])
 
 

time: 66.5 us -> 51.7 us (0.78)
  Pallas kernels: 35.3 us -> 22.4 us
  waiting for transfers between devices: 10.5 us -> 3.02 us
  local copies, waits for them, and re-layouts: 3.73 us -> 9.08 us
    pallas_call x3 -> x2, Pallas kernels: 16.9 us -> 3.35 us  [the longest x1 1.94 us: shards(): pl.pallas_call(onsite_kernel, out_shape=struct((modes, modes), F32), in_s...]
    ppermute x3, waiting for transfers between devices: 8.23 us -> 3.02 us  [passed_along(): return lax.ppermute(block, axis, route)]
    unnamed x8 -> x14, local copies, waits for them, and re-layouts: 3.73 us -> 7.43 us
    all_to_all x1, waiting for transfers between devices: 2.25 us -> 0.01 us  [shards(): lax.all_to_all(jnp.broadcast_to(potential_step[:, None], (slabs, TILE)),...]
    slice x0 -> x1, local copies, waits for them, and re-layouts: none -> 1.04 us  [shards(): next_head = passed_along(u[:surface], 'slab', -1)]
    pallas_call x1, Pallas kernels: 18.4 us -> 19.1 us  [shards(): pl.pallas_call(factor_kernel, out_shape=(struct((modes, modes), BF16), st...]
  transfers between devices with their start and end apart: 4 -> 4, of which waited for: 2 -> 1; matrix products, arithmetic and copies ran while one was open for 0% -> 1% of each run, Pallas kernels for 3% -> 41%
where the time goes in v6:
time: 51.7 us; the launch traced here: 50.8 us
  Pallas kernels  22.4 us (43%)
  starting transfers between devices  15 us (29%)
  local copies, waits for them, and re-layouts  9.08 us (18%)
  waiting for transfers between devices  3.02 us (6%)
  between operations  1.34 us (3%)
    pallas_call x1, Pallas kernels, shards(): pl.pallas_call(factor_kernel, out_shape=(struct((modes, modes), BF16), st...  19.1 us
    ppermute x3, starting transfers between devices, passed_along(): return lax.ppermute(block, axis, route)  7.53 us
    unnamed x14, local copies, waits for them, and re-layouts  7.43 us
    all_to_all x1, starting transfers between devices, shards(): lax.all_to_all(jnp.broadcast_to(potential_step[:, None], (slabs, TILE)),...  7.43 us
    ppermute x3, waiting for transfers between devices, passed_along(): return lax.ppermute(block, axis, route)  3.02 us
    pallas_call x1, Pallas kernels, shards(): pl.pallas_call(onsite_kernel, out_shape=struct((modes, modes), F32), in_s...  1.94 us
    pallas_call x1, Pallas kernels, shards(): pl.pallas_call(couple_kernel, out_shape=(struct((modes, modes), F32),) *...  1.41 us
    slice x1, local copies, waits for them, and re-layouts, shards(): next_head = passed_along(u[:surface], 'slab', -1)  1.04 us
  transfers between devices with their start and end apart: 4, of which 1 were waited for; matrix products, arithmetic and copies ran while one was open for 1% of the time, Pallas kernels for 41%

profile of v6, /device:TPU:1, one launch (start us, length us, event | category | flops | bytes accessed | tf_op | source)
XLA Modules:
  0.0 50.8 jit_solution(1313344228255956982)
XLA Ops:
  0.6 1.0 %slice_bitcast_fusion = bf16[512,384]{1,0:T(8,128)(2,1)S(1)} fusion(bf16[1,4096,384]{2,1,0:T(8,128)(2,1)} %param.8), kind=kLoop, calls=%fused_computation | loop fusion | bytes 786432 | tf_op jit(solution)/shard_map/slice | solution.py:380
  1.7 2.0 %collective-permute-start = (bf16[512,384]{1,0:T(8,128)(2,1)S(1)}, bf16[512,384]{1,0:T(8,128)(2,1)S(1)}, u32[]{:S(2)}, u32[]{:S(2)}) collective-permute-start(bf16[512,384]{1,0:T(8,128)(2,1)S(1)} %slice_bitcast_fusion), channel_id=1, source_target_pairs={{1,0},{2,1},{3,2},{4,3},{5,4},{6,5},{7,6},{8,7},{9,8},{10,9},{11,1... | collective-permute-start | bytes 1179656 | tf_op jit(solution)/shard_map/ppermute | solution.py:356
  4.3 0.6 %broadcast_in_dim.18 = f32[16,1,128]{2,1,0:T(1,128)} broadcast(f32[]{:T(128)} %bitcast.15), dimensions={} | broadcast | bytes 8196 | tf_op jit(solution)/shard_map/broadcast_in_dim | solution.py:382
  4.9 7.4 %all-to-all-start = ((f32[16,1,128]{2,1,0:T(1,128)}), f32[16,1,128]{2,1,0:T(1,128)S(1)}, u32[]{:S(2)}, u32[]{:S(2)}) async-start(f32[16,1,128]{2,1,0:T(1,128)} %broadcast_in_dim.18), calls=%async_computation | async-start | bytes 16384 | tf_op jit(solution)/shard_map/all_to_all | solution.py:381
  12.3 0.0 collective-permute-done.next_hbm
  12.3 0.0 copy-start
  12.3 1.9 %copy-done = bf16[1,4096,384]{2,1,0:T(8,128)(2,1)S(1)} copy-done((bf16[1,4096,384]{2,1,0:T(8,128)(2,1)S(1)}, bf16[1,4096,384]{2,1,0:T(8,128)(2,1)}, u32[]{:S(2)}) %copy-start) | copy-done | bytes 3145752
  14.2 0.0 copy-start.1
  14.2 1.9 %copy-done.1 = bf16[1,96,128,128]{3,2,1,0:T(8,128)(2,1)S(1)} copy-done((bf16[1,96,128,128]{3,2,1,0:T(8,128)(2,1)S(1)}, bf16[1,96,128,128]{3,2,1,0:T(8,128)(2,1)}, u32[]{:S(2)}) %copy-start.1) | copy-done | bytes 3145752
  16.1 0.0 copy-start.2
  16.1 1.0 %copy-done.2 = bf16[1,16,128,128]{3,2,1,0:T(8,128)(2,1)S(1)} copy-done((bf16[1,16,128,128]{3,2,1,0:T(8,128)(2,1)S(1)}, bf16[1,16,128,128]{3,2,1,0:T(8,128)(2,1)}, u32[]{:S(2)}) %copy-start.2) | copy-done | bytes 524312
  17.2 0.0 copy-start.3
  17.2 0.7 %copy-done.3 = s32[1,96]{1,0:T(1,128)S(1)} copy-done((s32[1,96]{1,0:T(1,128)S(1)}, s32[1,96]{1,0:T(1,128)}, u32[]{:S(2)}) %copy-start.3) | copy-done | bytes 408
  17.8 0.7 %copy-done.4 = s32[1,96]{1,0:T(1,128)S(1)} copy-done((s32[1,96]{1,0:T(1,128)S(1)}, s32[1,96]{1,0:T(1,128)}, u32[]{:S(2)}) %copy-start.4) | copy-done | bytes 408
  18.5 0.7 %copy-done.5 = s32[1,16]{1,0:T(1,128)S(1)} copy-done((s32[1,16]{1,0:T(1,128)S(1)}, s32[1,16]{1,0:T(1,128)}, u32[]{:S(2)}) %copy-start.5) | copy-done | bytes 88
  19.1 0.7 %copy-done.6 = s32[1,16]{1,0:T(1,128)S(1)} copy-done((s32[1,16]{1,0:T(1,128)S(1)}, s32[1,16]{1,0:T(1,128)}, u32[]{:S(2)}) %copy-start.6) | copy-done | bytes 88
  19.8 19.1 %factor.1 = (bf16[384,384]{1,0:T(8,128)(2,1)S(1)}, bf16[256,384]{1,0:T(8,128)(2,1)S(1)}, bf16[384,384]{1,0:T(8,128)(2,1)S(1)}, f32[384,384]{1,0:T(8,128)S(1)}) custom-call(s32[96]{0:T(128)S(1)} %bitcast.20, s32[96]{0:T(128)S(1)} %bitcast.21, s32[16]{0:T(128)S(1)} %bitcast.22, s32[16]{0:T(128)S(1)} %bitcast.23, ...), custom_call_target="tpu_custom_call" | custom-call | flops 4831838208 | bytes 3145728 | tf_op jit(solution)/shard_map/factor/pallas_call | solution.py:385
  38.9 2.0 %collective-permute-start.1 = (bf16[256,384]{1,0:T(8,128)(2,1)S(1)}, bf16[256,384]{1,0:T(8,128)(2,1)S(1)}, u32[]{:S(2)}, u32[]{:S(2)}) collective-permute-start(bf16[256,384]{1,0:T(8,128)(2,1)S(1)} %get-tuple-element.12), channel_id=1, source_target_pairs={{1,0},{2,1},{3,2},{4,3},{5,4},{6,5},{7,6},{8,7},{9,8},{10,9},{11,1... | collective-permute-start | bytes 589832 | tf_op jit(solution)/shard_map/ppermute | solution.py:356
  40.9 3.5 %collective-permute-start.2 = (bf16[384,384]{1,0:T(8,128)(2,1)S(1)}, bf16[384,384]{1,0:T(8,128)(2,1)S(1)}, u32[]{:S(2)}, u32[]{:S(2)}) collective-permute-start(bf16[384,384]{1,0:T(8,128)(2,1)S(1)} %get-tuple-element.11.yt_ref), channel_id=1, source_target_pairs={{0,1},{1,2},{2,3},{3,4},{4,5},{5,6},{6,7},{7,8},{8,9},{9,10},{10,1... | collective-permute-start | bytes 884744 | tf_op jit(solution)/shard_map/ppermute | solution.py:356
  44.4 0.0 all-to-all-done
  44.4 1.9 %onsite.1 = f32[384,384]{1,0:T(8,128)} custom-call(s32[1]{0:T(128)} %bitcast.place_ref, f32[384,384]{1,0:T(8,128)S(1)} %get-tuple-element.9.w_ref, bf16[384,384]{1,0:T(8,128)(2,1)S(1)} %get-tuple-element.10.f_ref, f32[16,128]{1,0:T(8,128)S(1)} %bitcast.17), custom_call_target="tpu_custom_call" | custom-call | flops 4831838208 | bytes 6291456 | tf_op jit(solution)/shard_map/onsite/pallas_call | solution.py:429
  46.4 0.0 collective-permute-done.1.next_ref
  46.4 3.0 %collective-permute-done.2.last_yt_ref = bf16[384,384]{1,0:T(8,128)(2,1)S(1)} collective-permute-done((bf16[384,384]{1,0:T(8,128)(2,1)S(1)}, bf16[384,384]{1,0:T(8,128)(2,1)S(1)}, u32[]{:S(2)}, u32[]{:S(2)}) %collective-permute-start.2) | collective-permute-done | bytes 294944 | tf_op jit(solution)/shard_map/ppermute | solution.py:356
  49.4 1.4 %couple.1 = (f32[384,384]{1,0:T(8,128)}, f32[384,384]{1,0:T(8,128)}) custom-call(bf16[384,384]{1,0:T(8,128)(2,1)S(1)} %get-tuple-element.11.yt_ref, bf16[256,384]{1,0:T(8,128)(2,1)S(1)} %collective-permute-done.1.next_ref, bf16[384,384]{1,0:T(8,128)(2,1)S(1)} %get-tuple-element.10.f_ref, bf16[384,384]{1,0:T(8,128)(2,1)S(1)} %collective-permute-done.2.last_yt_ref), custom_call_target="tpu_custom_call" | custom-call | flops 226492416 | bytes 1179648 | tf_op jit(solution)/shard_map/couple/pallas_call | solution.py:439
  (3 shorter events, 0.0 us)
Async XLA Ops:
  1.7 10.7 %collective-permute-start = (bf16[512,384]{1,0:T(8,128)(2,1)S(1)}, bf16[512,384]{1,0:T(8,128)(2,1)S(1)}, u32[]{:S(2)}, u32[]{:S(2)}) collective-permute-start(bf16[512,384]{1,0:T(8,128)(2,1)S(1)} %slice_bitcast_fusion), channel_id=1, source_target_pairs={{1,0},{2,1},{3,2},{4,3},{5,4},{6,5},{7,6},{8,7},{9,8},{10,9},{11,1... | collective-permute-start | bytes 1179656 | tf_op jit(solution)/shard_map/ppermute | solution.py:356
  4.9 39.5 %all-to-all-start = ((f32[16,1,128]{2,1,0:T(1,128)}), f32[16,1,128]{2,1,0:T(1,128)S(1)}, u32[]{:S(2)}, u32[]{:S(2)}) async-start(f32[16,1,128]{2,1,0:T(1,128)} %broadcast_in_dim.18), calls=%async_computation | async-start | bytes 16384 | tf_op jit(solution)/shard_map/all_to_all | solution.py:381
  12.3 1.9 %copy-start = (bf16[1,4096,384]{2,1,0:T(8,128)(2,1)S(1)}, bf16[1,4096,384]{2,1,0:T(8,128)(2,1)}, u32[]{:S(2)}) copy-start(bf16[1,4096,384]{2,1,0:T(8,128)(2,1)} %param.8) | copy-start | bytes 9437188
  14.2 1.9 %copy-start.1 = (bf16[1,96,128,128]{3,2,1,0:T(8,128)(2,1)S(1)}, bf16[1,96,128,128]{3,2,1,0:T(8,128)(2,1)}, u32[]{:S(2)}) copy-start(bf16[1,96,128,128]{3,2,1,0:T(8,128)(2,1)} %param.9) | copy-start | bytes 9437188
  16.1 1.0 %copy-start.2 = (bf16[1,16,128,128]{3,2,1,0:T(8,128)(2,1)S(1)}, bf16[1,16,128,128]{3,2,1,0:T(8,128)(2,1)}, u32[]{:S(2)}) copy-start(bf16[1,16,128,128]{3,2,1,0:T(8,128)(2,1)} %param.12) | copy-start | bytes 1572868
  17.2 0.7 %copy-start.3 = (s32[1,96]{1,0:T(1,128)S(1)}, s32[1,96]{1,0:T(1,128)}, u32[]{:S(2)}) copy-start(s32[1,96]{1,0:T(1,128)} %param.10) | copy-start | bytes 1156
  17.8 0.7 %copy-start.4 = (s32[1,96]{1,0:T(1,128)S(1)}, s32[1,96]{1,0:T(1,128)}, u32[]{:S(2)}) copy-start(s32[1,96]{1,0:T(1,128)} %param.11) | copy-start | bytes 1156
  18.5 0.7 %copy-start.5 = (s32[1,16]{1,0:T(1,128)S(1)}, s32[1,16]{1,0:T(1,128)}, u32[]{:S(2)}) copy-start(s32[1,16]{1,0:T(1,128)} %param.13) | copy-start | bytes 196
  19.1 0.7 %copy-start.6 = (s32[1,16]{1,0:T(1,128)S(1)}, s32[1,16]{1,0:T(1,128)}, u32[]{:S(2)}) copy-start(s32[1,16]{1,0:T(1,128)} %param.14) | copy-start | bytes 196
  38.9 7.5 %collective-permute-start.1 = (bf16[256,384]{1,0:T(8,128)(2,1)S(1)}, bf16[256,384]{1,0:T(8,128)(2,1)S(1)}, u32[]{:S(2)}, u32[]{:S(2)}) collective-permute-start(bf16[256,384]{1,0:T(8,128)(2,1)S(1)} %get-tuple-element.12), channel_id=1, source_target_pairs={{1,0},{2,1},{3,2},{4,3},{5,4},{6,5},{7,6},{8,7},{9,8},{10,9},{11,1... | collective-permute-start | bytes 589832 | tf_op jit(solution)/shard_map/ppermute | solution.py:356
  40.9 8.5 %collective-permute-start.2 = (bf16[384,384]{1,0:T(8,128)(2,1)S(1)}, bf16[384,384]{1,0:T(8,128)(2,1)S(1)}, u32[]{:S(2)}, u32[]{:S(2)}) collective-permute-start(bf16[384,384]{1,0:T(8,128)(2,1)S(1)} %get-tuple-element.11.yt_ref), channel_id=1, source_target_pairs={{0,1},{1,2},{2,3},{3,4},{4,5},{5,6},{6,7},{7,8},{8,9},{9,10},{10,1... | collective-permute-start | bytes 884744 | tf_op jit(solution)/shard_map/ppermute | solution.py:356

commit v7 on v6

--- a/solution.py
+++ b/solution.py
@@ -147,7 +147,8 @@
     f_ref,
     packed_ref,
     yt_ref,
-    w_ref,
+    turned_hbm,
+    spread_hbm,
     gram_ref,
     upper_ref,
     inv_ref,
@@ -158,12 +159,14 @@
     turned_ref,
     blocks_ref,
     acc_ref,
+    spread_ref,
     next_ref,
     cblocks_ref,
     hop_ref,
     m_ref,
     sems,
     u_sems,
+    out_sems,
 ):
     orbitals, modes = u_ref.shape
     surface = hop_ref.shape[0]
@@ -241,11 +244,27 @@
             inv_ref[tile_of(i), tile_of(i)], inv_ref[tile_of(i), width]
         )
 
+    outs = out_sems.shape[0] - 1
+    out_step = orbitals // outs
+    turned_copy = pltpu.make_async_copy(turned_ref, turned_hbm, out_sems.at[outs])
+    spread_copies = [
+        pltpu.make_async_copy(
+            spread_ref.at[pl.ds(c * out_step, out_step)],
+            spread_hbm.at[pl.ds(c * out_step, out_step)],
+            out_sems.at[c],
+        )
+        for c in range(outs)
+    ]
+
+    def round_part(c):
+        part = slice(c * out_step, (c + 1) * out_step)
+        spread_ref[part, :] = acc_ref[part, :].astype(BF16)
+        spread_copies[c].start()
+
     call = functools.partial
     products = [call(onsite_product, j) for j in range(blocks_ref.shape[0])]
     products += [call(coupling_product, j) for j in range(cblocks_ref.shape[0])]
-    reductions = [call(reduce_part, w_ref, 0, acc_ref, c * step) for c in range(panels)]
-    reductions += [
+    reductions = [
         call(reduce_part, m_ref, orbitals - surface, hop_ref, first)
         for first in range(0, surface, step)
     ]
@@ -256,6 +275,9 @@
     room = [(t, g) for t in range(tiles - 1) for g in range(panels)][4:]
     for n, work in enumerate(products):
         plan[room[n * len(room) // len(products)]].append(work)
+    plan[1, 0].append(turned_copy.start)
+    for c in range(outs):
+        plan[tiles - 1, c * (panels - 4) // outs].append(call(round_part, c))
     for n, work in enumerate(reductions):
         plan[tiles - 1, n * panels // len(reductions)].append(work)
     for t in range(1, tiles):
@@ -304,6 +326,8 @@
     packed_ref[TILE:, :TILE] = factor[2 * TILE :, 2 * TILE :]
     high, low = split(m_ref[...])
     yt_ref[...] = (bf_dot(high, factor, TN) + bf_dot(low, factor, TN)).astype(BF16)
+    for copy in spread_copies + [turned_copy]:
+        copy.wait()
 
 
 def couple_kernel(yt_ref, next_ref, f_ref, last_yt_ref, right_ref, left_ref, full_ref):
@@ -320,8 +344,30 @@
     return high, (value - high.astype(F32)).astype(BF16)
 
 
-def onsite_kernel(place_ref, w_ref, f_ref, steps_ref, out_ref):
+def onsite_kernel(
+    place_ref, turned_hbm, spread_hbm, f_ref, steps_ref, out_ref, turned_ref, spread_ref, w_ref, sems
+):
     modes = f_ref.shape[0]
+    chunks = sems.shape[0]
+    step = spread_ref.shape[0] // chunks
+    copies = []
+    for c in range(chunks):
+        part = pl.ds(c * step, step)
+        copies.append(
+            [
+                pltpu.make_async_copy(turned_hbm.at[:, part], turned_ref.at[:, part], sems.at[c, 0]),
+                pltpu.make_async_copy(spread_hbm.at[part], spread_ref.at[part], sems.at[c, 1]),
+            ]
+        )
+    for pair in copies:
+        for copy in pair:
+            copy.start()
+    for c, pair in enumerate(copies):
+        for copy in pair:
+            copy.wait()
+        part = slice(c * step, (c + 1) * step)
+        product = bf_dot(turned_ref[:, part], spread_ref[part, :], NN)
+        w_ref[...] = product if c == 0 else w_ref[...] + product
     w = w_ref[...]
     w = w + w.T
     f = f_ref[...]
@@ -382,16 +428,17 @@
         jnp.broadcast_to(potential_step[:, None], (slabs, TILE)), "slab", 0, 0, tiled=True
     )
 
-    factor, packed, yt, w = pl.pallas_call(
+    factor, packed, yt, turned, spread = pl.pallas_call(
         factor_kernel,
         out_shape=(
             struct((modes, modes), BF16),
             struct((modes - TILE, modes), BF16),
             struct((modes, modes), BF16),
-            struct((modes, modes), F32),
+            struct((modes, orbitals), BF16),
+            struct((orbitals, modes), BF16),
         ),
         in_specs=[INTO_SMEM] * 4 + [ANY] * 4,
-        out_specs=(INTO_VMEM,) * 4,
+        out_specs=(INTO_VMEM,) * 3 + (ANY,) * 2,
         scratch_shapes=[
             pltpu.VMEM((modes, modes), F32),
             pltpu.VMEM((modes, modes), F32),
@@ -403,14 +450,16 @@
             pltpu.VMEM((modes, orbitals), BF16),
             pltpu.VMEM((count, TILE, TILE), BF16),
             pltpu.VMEM((orbitals, modes), F32),
+            pltpu.VMEM((orbitals, modes), BF16),
             pltpu.VMEM((surface, modes), BF16),
             pltpu.VMEM((links, TILE, TILE), BF16),
             pltpu.VMEM((surface, modes), F32),
             pltpu.VMEM((modes, modes), F32),
             pltpu.SemaphoreType.DMA((3,)),
             pltpu.SemaphoreType.DMA((8,)),
+            pltpu.SemaphoreType.DMA((5,)),
         ],
-        compiler_params=params(40),
+        compiler_params=params(59),
         cost_estimate=cost(8 * orbitals * modes * modes, orbitals * modes * 2),
         name="factor",
     )(
@@ -429,12 +478,18 @@
     onsite = pl.pallas_call(
         onsite_kernel,
         out_shape=struct((modes, modes), F32),
-        in_specs=[INTO_SMEM] + [INTO_VMEM] * 3,
+        in_specs=[INTO_SMEM, ANY, ANY, INTO_VMEM, INTO_VMEM],
         out_specs=INTO_VMEM,
-        compiler_params=params(40),
+        scratch_shapes=[
+            pltpu.VMEM((modes, orbitals), BF16),
+            pltpu.VMEM((orbitals, modes), BF16),
+            pltpu.VMEM((modes, modes), F32),
+            pltpu.SemaphoreType.DMA((8, 2)),
+        ],
+        compiler_params=params(59),
         cost_estimate=cost(8 * orbitals * modes * modes, 4 * orbitals * modes),
         name="onsite",
-    )(place, w, factor, steps)
+    )(place, turned, spread, factor, steps)
 
     right, left = pl.pallas_call(
         couple_kernel,
@@ -442,7 +497,7 @@
         in_specs=[INTO_VMEM] * 4,
         out_specs=(INTO_VMEM,) * 2,
         scratch_shapes=[pltpu.VMEM((modes, modes), BF16)],
-        compiler_params=params(40),
+        compiler_params=params(8),
         cost_estimate=cost(4 * modes * modes * modes, 8 * modes * modes),
         name="couple",
     )(yt, next_packed, factor, last_yt)

time: 51.7 us -> 46.9 us (0.907)
  local copies, waits for them, and re-layouts: 9.08 us -> 2.98 us
  Pallas kernels: 22.4 us -> 26.9 us
  waiting for transfers between devices: 3.02 us -> 0.01 us
    unnamed x14 -> x8, local copies, waits for them, and re-layouts: 7.43 us -> 1.34 us
    pallas_call x1, Pallas kernels: 1.94 us -> 6.32 us  [shards(): pl.pallas_call(onsite_kernel, out_shape=struct((modes, modes), F32), in_s...]
    ppermute x3, waiting for transfers between devices: 3.02 us -> 0.01 us  [passed_along(): return lax.ppermute(block, axis, route)]
  transfers between devices with their start and end apart: 4 -> 4, of which waited for: 1 -> 0; matrix products, arithmetic and copies ran while one was open for 1% -> 1% of each run, Pallas kernels for 41% -> 55%
where the time goes in v7:
time: 46.9 us; the launch traced here: 46.4 us
  Pallas kernels  26.9 us (57%)
  starting transfers between devices  15.1 us (32%)
  local copies, waits for them, and re-layouts  2.98 us (6%)
  between operations  1.38 us (3%)
    pallas_call x1, Pallas kernels, shards(): pl.pallas_call(factor_kernel, out_shape=(struct((modes, modes), BF16), st...  19.1 us
    ppermute x3, starting transfers between devices, passed_along(): return lax.ppermute(block, axis, route)  7.71 us
    all_to_all x1, starting transfers between devices, shards(): lax.all_to_all(jnp.broadcast_to(potential_step[:, None], (slabs, TILE)),...  7.43 us
    pallas_call x1, Pallas kernels, shards(): pl.pallas_call(onsite_kernel, out_shape=struct((modes, modes), F32), in_s...  6.32 us
    pallas_call x1, Pallas kernels, shards(): pl.pallas_call(couple_kernel, out_shape=(struct((modes, modes), F32),) *...  1.42 us
    unnamed x8, local copies, waits for them, and re-layouts  1.34 us
    slice x1, local copies, waits for them, and re-layouts, shards(): next_head = passed_along(u[:surface], 'slab', -1)  1.04 us
  transfers between devices with their start and end apart: 4, of which 0 were waited for; matrix products, arithmetic and copies ran while one was open for 1% of the time, Pallas kernels for 55%

profile of v7, /device:TPU:1, one launch (start us, length us, event | category | flops | bytes accessed | tf_op | source)
XLA Modules:
  0.0 46.4 jit_solution(17090233593746130446)
XLA Ops:
  0.6 1.0 %slice_bitcast_fusion = bf16[512,384]{1,0:T(8,128)(2,1)S(1)} fusion(bf16[1,4096,384]{2,1,0:T(8,128)(2,1)} %param.8), kind=kLoop, calls=%fused_computation | loop fusion | bytes 786432 | tf_op jit(solution)/shard_map/slice | solution.py:426
  1.7 2.0 %collective-permute-start = (bf16[512,384]{1,0:T(8,128)(2,1)S(1)}, bf16[512,384]{1,0:T(8,128)(2,1)S(1)}, u32[]{:S(2)}, u32[]{:S(2)}) collective-permute-start(bf16[512,384]{1,0:T(8,128)(2,1)S(1)} %slice_bitcast_fusion), channel_id=1, source_target_pairs={{1,0},{2,1},{3,2},{4,3},{5,4},{6,5},{7,6},{8,7},{9,8},{10,9},{11,1... | collective-permute-start | bytes 1179656 | tf_op jit(solution)/shard_map/ppermute | solution.py:402
  4.3 0.6 %broadcast_in_dim.18 = f32[16,1,128]{2,1,0:T(1,128)} broadcast(f32[]{:T(128)} %bitcast.15), dimensions={} | broadcast | bytes 8196 | tf_op jit(solution)/shard_map/broadcast_in_dim | solution.py:428
  4.9 7.4 %all-to-all-start = ((f32[16,1,128]{2,1,0:T(1,128)}), f32[16,1,128]{2,1,0:T(1,128)S(1)}, u32[]{:S(2)}, u32[]{:S(2)}) async-start(f32[16,1,128]{2,1,0:T(1,128)} %broadcast_in_dim.18), calls=%async_computation | async-start | bytes 16384 | tf_op jit(solution)/shard_map/all_to_all | solution.py:427
  12.3 0.0 collective-permute-done.next_hbm
  12.3 0.0 copy-start.3
  12.3 0.7 %copy-done.3 = bf16[512,384]{1,0:T(8,128)(2,1)} copy-done((bf16[512,384]{1,0:T(8,128)(2,1)}, bf16[512,384]{1,0:T(8,128)(2,1)S(1)}, u32[]{:S(2)}) %copy-start.3) | copy-done | bytes 393240
  13.1 19.1 %factor.1 = (bf16[384,384]{1,0:T(8,128)(2,1)}, bf16[256,384]{1,0:T(8,128)(2,1)}, bf16[384,384]{1,0:T(8,128)(2,1)}, bf16[384,4096]{1,0:T(8,128)(2,1)}, bf16[4096,384]{1,0:T(8,128)(2,1)}) custom-call(s32[96]{0:T(128)} %bitcast.22, s32[96]{0:T(128)} %bitcast.23, s32[16]{0:T(128)} %bitcast.24, s32[16]{0:T(128)} %bitcast.25, bf16[512,384]{1,0:T(8,128)(2,1)} %copy-done.3, ...), custom_call_target="tpu_custom_call" | custom-call | flops 4831838208 | bytes 3145728 | tf_op jit(solution)/shard_map/factor/pallas_call | solution.py:431
  32.2 2.0 %collective-permute-start.1 = (bf16[256,384]{1,0:T(8,128)(2,1)}, bf16[256,384]{1,0:T(8,128)(2,1)S(1)}, u32[]{:S(2)}, u32[]{:S(2)}) collective-permute-start(bf16[256,384]{1,0:T(8,128)(2,1)} %get-tuple-element.14), channel_id=1, source_target_pairs={{1,0},{2,1},{3,2},{4,3},{5,4},{6,5},{7,6},{8,7},{9,8},{10,9},{11,1... | collective-permute-start | bytes 589832 | tf_op jit(solution)/shard_map/ppermute | solution.py:402
  34.2 3.7 %collective-permute-start.2 = (bf16[384,384]{1,0:T(8,128)(2,1)}, bf16[384,384]{1,0:T(8,128)(2,1)S(1)}, u32[]{:S(2)}, u32[]{:S(2)}) collective-permute-start(bf16[384,384]{1,0:T(8,128)(2,1)} %get-tuple-element.13.yt_ref), channel_id=1, source_target_pairs={{0,1},{1,2},{2,3},{3,4},{4,5},{5,6},{6,7},{7,8},{8,9},{9,10},{10,1... | collective-permute-start | bytes 884744 | tf_op jit(solution)/shard_map/ppermute | solution.py:402
  38.0 0.0 all-to-all-done
  38.0 0.0 copy-start.2
  38.0 0.6 %copy-done.2 = f32[16,1,128]{2,1,0:T(1,128)} copy-done((f32[16,1,128]{2,1,0:T(1,128)}, f32[16,1,128]{2,1,0:T(1,128)S(1)}, u32[]{:S(2)}) %copy-start.2) | copy-done | bytes 8216
  38.6 0.0 copy-start
  38.6 0.0 copy-start.1
  38.6 6.3 %onsite.1 = f32[384,384]{1,0:T(8,128)} custom-call(s32[1]{0:T(128)} %bitcast.place_ref, bf16[384,4096]{1,0:T(8,128)(2,1)} %get-tuple-element.10.turned_hbm, bf16[4096,384]{1,0:T(8,128)(2,1)} %get-tuple-element.11.spread_hbm, bf16[384,384]{1,0:T(8,128)(2,1)} %get-tuple-element.12.f_ref, f32[16,128]{1,0:T(8,128)} %bitcast.17), custom_call_target="tpu_custom_call" | custom-call | flops 4831838208 | bytes 6291456 | tf_op jit(solution)/shard_map/onsite/pallas_call | solution.py:478
  44.9 0.0 collective-permute-done.1.next_ref
  44.9 0.0 collective-permute-done.2.last_yt_ref
  44.9 0.0 copy-done
  44.9 0.0 copy-done.1
  45.0 1.4 %couple.1 = (f32[384,384]{1,0:T(8,128)}, f32[384,384]{1,0:T(8,128)}) custom-call(bf16[384,384]{1,0:T(8,128)(2,1)S(1)} %copy-done.1, bf16[256,384]{1,0:T(8,128)(2,1)S(1)} %collective-permute-done.1.next_ref, bf16[384,384]{1,0:T(8,128)(2,1)S(1)} %copy-done, bf16[384,384]{1,0:T(8,128)(2,1)S(1)} %collective-permute-done.2.last_yt_ref), custom_call_target="tpu_custom_call" | custom-call | flops 226492416 | bytes 1179648 | tf_op jit(solution)/shard_map/couple/pallas_call | solution.py:494
Async XLA Ops:
  1.7 10.7 %collective-permute-start = (bf16[512,384]{1,0:T(8,128)(2,1)S(1)}, bf16[512,384]{1,0:T(8,128)(2,1)S(1)}, u32[]{:S(2)}, u32[]{:S(2)}) collective-permute-start(bf16[512,384]{1,0:T(8,128)(2,1)S(1)} %slice_bitcast_fusion), channel_id=1, source_target_pairs={{1,0},{2,1},{3,2},{4,3},{5,4},{6,5},{7,6},{8,7},{9,8},{10,9},{11,1... | collective-permute-start | bytes 1179656 | tf_op jit(solution)/shard_map/ppermute | solution.py:402
  4.9 33.1 %all-to-all-start = ((f32[16,1,128]{2,1,0:T(1,128)}), f32[16,1,128]{2,1,0:T(1,128)S(1)}, u32[]{:S(2)}, u32[]{:S(2)}) async-start(f32[16,1,128]{2,1,0:T(1,128)} %broadcast_in_dim.18), calls=%async_computation | async-start | bytes 16384 | tf_op jit(solution)/shard_map/all_to_all | solution.py:427
  12.3 0.7 %copy-start.3 = (bf16[512,384]{1,0:T(8,128)(2,1)}, bf16[512,384]{1,0:T(8,128)(2,1)S(1)}, u32[]{:S(2)}) copy-start(bf16[512,384]{1,0:T(8,128)(2,1)S(1)} %collective-permute-done.next_hbm) | copy-start | bytes 1179652
  32.2 12.7 %collective-permute-start.1 = (bf16[256,384]{1,0:T(8,128)(2,1)}, bf16[256,384]{1,0:T(8,128)(2,1)S(1)}, u32[]{:S(2)}, u32[]{:S(2)}) collective-permute-start(bf16[256,384]{1,0:T(8,128)(2,1)} %get-tuple-element.14), channel_id=1, source_target_pairs={{1,0},{2,1},{3,2},{4,3},{5,4},{6,5},{7,6},{8,7},{9,8},{10,9},{11,1... | collective-permute-start | bytes 589832 | tf_op jit(solution)/shard_map/ppermute | solution.py:402
  34.2 10.7 %collective-permute-start.2 = (bf16[384,384]{1,0:T(8,128)(2,1)}, bf16[384,384]{1,0:T(8,128)(2,1)S(1)}, u32[]{:S(2)}, u32[]{:S(2)}) collective-permute-start(bf16[384,384]{1,0:T(8,128)(2,1)} %get-tuple-element.13.yt_ref), channel_id=1, source_target_pairs={{0,1},{1,2},{2,3},{3,4},{4,5},{5,6},{6,7},{7,8},{8,9},{9,10},{10,1... | collective-permute-start | bytes 884744 | tf_op jit(solution)/shard_map/ppermute | solution.py:402
  38.0 0.6 %copy-start.2 = (f32[16,1,128]{2,1,0:T(1,128)}, f32[16,1,128]{2,1,0:T(1,128)S(1)}, u32[]{:S(2)}) copy-start(f32[16,1,128]{2,1,0:T(1,128)S(1)} %all-to-all-done) | copy-start | bytes 24580
  38.6 6.4 %copy-start = (bf16[384,384]{1,0:T(8,128)(2,1)S(1)}, bf16[384,384]{1,0:T(8,128)(2,1)}, u32[]{:S(2)}) copy-start(bf16[384,384]{1,0:T(8,128)(2,1)} %get-tuple-element.12.f_ref) | copy-start | bytes 884740
  38.6 6.4 %copy-start.1 = (bf16[384,384]{1,0:T(8,128)(2,1)S(1)}, bf16[384,384]{1,0:T(8,128)(2,1)}, u32[]{:S(2)}) copy-start(bf16[384,384]{1,0:T(8,128)(2,1)} %get-tuple-element.13.yt_ref) | copy-start | bytes 884740

commit v8 on v6

--- a/solution.py
+++ b/solution.py
@@ -135,11 +135,47 @@
     acc_ref[pl.ds(to, TILE), :] = acc_ref[pl.ds(to, TILE), :] + product
 
 
+def add_pair(t, table_ref, acc_ref, source_ref, blocks_ref):
+    a, b = table_ref[0, 2 * t], table_ref[0, 2 * t + 1]
+    to = pl.multiple_of(table_ref[1, 2 * t] * TILE, TILE)
+    at_a = pl.multiple_of(table_ref[2, 2 * t] * TILE, TILE)
+    at_b = pl.multiple_of(table_ref[2, 2 * t + 1] * TILE, TILE)
+    left = jnp.concatenate([blocks_ref[a], blocks_ref[b]], axis=1)
+    right = jnp.concatenate(
+        [source_ref[pl.ds(at_a, TILE), :], source_ref[pl.ds(at_b, TILE), :]], axis=0
+    )
+    acc_ref[pl.ds(to, TILE), :] = acc_ref[pl.ds(to, TILE), :] + bf_dot(left, right, NN)
+
+
+def pair_table(rows, cols, count):
+    shape = (TILE, TILE)
+    i = lax.broadcasted_iota(jnp.int32, shape, 0)
+    j = lax.broadcasted_iota(jnp.int32, shape, 1)
+    row_j, col_j = (jnp.broadcast_to(v.astype(F32), shape) for v in (rows, cols))
+    row_i, col_i = row_j.T, col_j.T
+    ones, none = jnp.ones(shape, F32), jnp.zeros(shape, F32)
+    same = (row_i == row_j) & (i < count)
+    rank_j = jnp.sum(jnp.where(same & (i < j), ones, none), axis=0, keepdims=True)
+    size_j = jnp.sum(jnp.where(same, ones, none), axis=0, keepdims=True)
+    half = jnp.floor(size_j * 0.5)
+    odd_last = (size_j - 2.0 * half) * jnp.where(rank_j == size_j - 1.0, 1.0, 0.0)
+    ahead = jnp.where(row_j < row_i, ones + odd_last, none)
+    ahead = ahead + jnp.where((row_j == row_i) & (j < i), ones, none)
+    place_i = jnp.sum(jnp.where(j < count, ahead, none), axis=1, keepdims=True)
+    match = (place_i == j.astype(F32)) & (i < count)
+    found = jnp.sum(jnp.where(match, ones, none), axis=0, keepdims=True)
+    block = jnp.sum(jnp.where(match, i.astype(F32), none), axis=0, keepdims=True)
+    block = block + (1.0 - found) * count
+    row_of = jnp.sum(jnp.where(match, row_i, none), axis=0, keepdims=True)
+    col_of = jnp.sum(jnp.where(match, col_i, none), axis=0, keepdims=True)
+    return jnp.concatenate([block, row_of, col_of], axis=0).astype(jnp.int32)
+
+
 def factor_kernel(
+    crows_ref,
+    ccols_ref,
     rows_ref,
     cols_ref,
-    crows_ref,
-    ccols_ref,
     next_hbm,
     u_hbm,
     blocks_hbm,
@@ -162,11 +198,16 @@
     cblocks_ref,
     hop_ref,
     m_ref,
+    index_ref,
+    made_ref,
+    table_ref,
     sems,
     u_sems,
 ):
     orbitals, modes = u_ref.shape
     surface = hop_ref.shape[0]
+    count = blocks_hbm.shape[0]
+    slots = (count + orbitals // TILE) // 2
     tiles = modes // TILE
     panels = TILE // ROWS
     step = orbitals // panels
@@ -181,12 +222,19 @@
         for c in range(chunks)
     ]
     more = [
-        pltpu.make_async_copy(blocks_hbm, blocks_ref, sems.at[0]),
+        pltpu.make_async_copy(blocks_hbm, blocks_ref.at[pl.ds(0, count)], sems.at[0]),
         pltpu.make_async_copy(cblocks_hbm, cblocks_ref, sems.at[1]),
         pltpu.make_async_copy(next_hbm, next_ref, sems.at[2]),
     ]
     for copy in copies + more:
         copy.start()
+    index_ref[...] = jnp.zeros_like(index_ref)
+    index_ref[0:1, :count] = rows_ref[...]
+    index_ref[1:2, :count] = cols_ref[...]
+    made_ref[0:3, :] = pair_table(index_ref[0:1, :], index_ref[1:2, :], count)
+    more.append(pltpu.make_async_copy(made_ref, table_ref, sems.at[3]))
+    more[-1].start()
+    blocks_ref[count] = jnp.zeros_like(blocks_ref[count])
     acc_ref[...] = jnp.zeros_like(acc_ref)
     hop_ref[...] = jnp.zeros_like(hop_ref)
     inv_ref[...] = jnp.zeros_like(inv_ref)
@@ -212,8 +260,8 @@
         for copy in more:
             copy.wait()
 
-    def onsite_product(j):
-        add_product(j, None, acc_ref, u_ref, blocks_ref, rows_ref, cols_ref, 0)
+    def onsite_product(t):
+        add_pair(t, table_ref, acc_ref, u_ref, blocks_ref)
 
     def coupling_product(j):
         base = (orbitals - surface) // TILE
@@ -242,10 +290,10 @@
         )
 
     call = functools.partial
-    products = [call(onsite_product, j) for j in range(blocks_ref.shape[0])]
-    products += [call(coupling_product, j) for j in range(cblocks_ref.shape[0])]
+    products = [call(onsite_product, t) for t in range(slots)]
+    links = [call(coupling_product, j) for j in range(cblocks_ref.shape[0])]
     reductions = [call(reduce_part, w_ref, 0, acc_ref, c * step) for c in range(panels)]
-    reductions += [
+    finish = [
         call(reduce_part, m_ref, orbitals - surface, hop_ref, first)
         for first in range(0, surface, step)
     ]
@@ -253,11 +301,16 @@
     for g in range(panels):
         plan[0, g].append(call(gram_part, TILE, modes, g * step, step))
     plan[0, 3].append(wait_more)
-    room = [(t, g) for t in range(tiles - 1) for g in range(panels)][4:]
+    room = [(0, g) for g in range(4, panels)]
+    room += [(t, g) for t in range(1, tiles - 1) for g in range(panels) for _ in range(2)]
     for n, work in enumerate(products):
         plan[room[n * len(room) // len(products)]].append(work)
     for n, work in enumerate(reductions):
         plan[tiles - 1, n * panels // len(reductions)].append(work)
+    for n, work in enumerate(links):
+        plan[tiles - 1, n * (panels - 4) // len(links)].append(work)
+    for n, work in enumerate(finish):
+        plan[tiles - 1, panels - 3 + n].append(work)
     for t in range(1, tiles):
         late = []
         if t > 1:
@@ -390,7 +443,7 @@
             struct((modes, modes), BF16),
             struct((modes, modes), F32),
         ),
-        in_specs=[INTO_SMEM] * 4 + [ANY] * 4,
+        in_specs=[INTO_SMEM] * 2 + [INTO_VMEM] * 2 + [ANY] * 4,
         out_specs=(INTO_VMEM,) * 4,
         scratch_shapes=[
             pltpu.VMEM((modes, modes), F32),
@@ -401,23 +454,26 @@
             pltpu.VMEM((2, ROWS, ROWS, TILE), F32),
             pltpu.VMEM((orbitals, modes), BF16),
             pltpu.VMEM((modes, orbitals), BF16),
-            pltpu.VMEM((count, TILE, TILE), BF16),
+            pltpu.VMEM((count + 1, TILE, TILE), BF16),
             pltpu.VMEM((orbitals, modes), F32),
             pltpu.VMEM((surface, modes), BF16),
             pltpu.VMEM((links, TILE, TILE), BF16),
             pltpu.VMEM((surface, modes), F32),
             pltpu.VMEM((modes, modes), F32),
-            pltpu.SemaphoreType.DMA((3,)),
+            pltpu.VMEM((ROWS, TILE), jnp.int32),
+            pltpu.VMEM((ROWS, TILE), jnp.int32),
+            pltpu.SMEM((ROWS, TILE), jnp.int32),
+            pltpu.SemaphoreType.DMA((4,)),
             pltpu.SemaphoreType.DMA((8,)),
         ],
-        compiler_params=params(40),
+        compiler_params=params(59),
         cost_estimate=cost(8 * orbitals * modes * modes, orbitals * modes * 2),
         name="factor",
     )(
-        onsite_rows[0],
-        onsite_cols[0],
         coupling_rows[0],
         coupling_cols[0],
+        onsite_rows,
+        onsite_cols,
         next_head,
         u,
         onsite_blocks[0],
@@ -431,7 +487,7 @@
         out_shape=struct((modes, modes), F32),
         in_specs=[INTO_SMEM] + [INTO_VMEM] * 3,
         out_specs=INTO_VMEM,
-        compiler_params=params(40),
+        compiler_params=params(60),
         cost_estimate=cost(8 * orbitals * modes * modes, 4 * orbitals * modes),
         name="onsite",
     )(place, w, factor, steps)
@@ -442,7 +498,7 @@
         in_specs=[INTO_VMEM] * 4,
         out_specs=(INTO_VMEM,) * 2,
         scratch_shapes=[pltpu.VMEM((modes, modes), BF16)],
-        compiler_params=params(40),
+        compiler_params=params(8),
         cost_estimate=cost(4 * modes * modes * modes, 8 * modes * modes),
         name="couple",
     )(yt, next_packed, factor, last_yt)

time: 51.7 us -> 44.4 us (0.86)
  local copies, waits for them, and re-layouts: 9.08 us -> 2.98 us
  waiting for transfers between devices: 3.02 us -> 1.52 us
    unnamed x14 -> x8, local copies, waits for them, and re-layouts: 7.43 us -> 1.34 us
    ppermute x3, waiting for transfers between devices: 3.02 us -> 1.51 us  [passed_along(): return lax.ppermute(block, axis, route)]
    pallas_call x1, Pallas kernels: 1.94 us -> 3.15 us  [shards(): pl.pallas_call(onsite_kernel, out_shape=struct((modes, modes), F32), in_s...]
    pallas_call x1, Pallas kernels: 19.1 us -> 18.3 us  [shards(): pl.pallas_call(factor_kernel, out_shape=(struct((modes, modes), BF16), st...]
  transfers between devices with their start and end apart: 4 -> 4, of which waited for: 1 -> 1; matrix products, arithmetic and copies ran while one was open for 1% -> 1% of each run, Pallas kernels for 41% -> 49%
where the time goes in v8:
time: 44.4 us; the launch traced here: 43.7 us
  Pallas kernels  22.9 us (52%)
  starting transfers between devices  15 us (34%)
  local copies, waits for them, and re-layouts  2.98 us (7%)
  waiting for transfers between devices  1.52 us (3%)
  between operations  1.34 us (3%)
    pallas_call x1, Pallas kernels, shards(): pl.pallas_call(factor_kernel, out_shape=(struct((modes, modes), BF16), st...  18.3 us
    ppermute x3, starting transfers between devices, passed_along(): return lax.ppermute(block, axis, route)  7.53 us
    all_to_all x1, starting transfers between devices, shards(): lax.all_to_all(jnp.broadcast_to(potential_step[:, None], (slabs, TILE)),...  7.43 us
    pallas_call x1, Pallas kernels, shards(): pl.pallas_call(onsite_kernel, out_shape=struct((modes, modes), F32), in_s...  3.15 us
    ppermute x3, waiting for transfers between devices, passed_along(): return lax.ppermute(block, axis, route)  1.51 us
    pallas_call x1, Pallas kernels, shards(): pl.pallas_call(couple_kernel, out_shape=(struct((modes, modes), F32),) *...  1.41 us
    unnamed x8, local copies, waits for them, and re-layouts  1.34 us
    slice x1, local copies, waits for them, and re-layouts, shards(): next_head = passed_along(u[:surface], 'slab', -1)  1.04 us
  transfers between devices with their start and end apart: 4, of which 1 were waited for; matrix products, arithmetic and copies ran while one was open for 1% of the time, Pallas kernels for 49%

profile of v8, /device:TPU:1, one launch (start us, length us, event | category | flops | bytes accessed | tf_op | source)
XLA Modules:
  0.0 43.7 jit_solution(16806976326640635327)
XLA Ops:
  0.6 1.0 %slice_bitcast_fusion = bf16[512,384]{1,0:T(8,128)(2,1)S(1)} fusion(bf16[1,4096,384]{2,1,0:T(8,128)(2,1)} %param.8), kind=kLoop, calls=%fused_computation | loop fusion | bytes 786432 | tf_op jit(solution)/shard_map/slice | solution.py:433
  1.7 2.0 %collective-permute-start = (bf16[512,384]{1,0:T(8,128)(2,1)S(1)}, bf16[512,384]{1,0:T(8,128)(2,1)S(1)}, u32[]{:S(2)}, u32[]{:S(2)}) collective-permute-start(bf16[512,384]{1,0:T(8,128)(2,1)S(1)} %slice_bitcast_fusion), channel_id=1, source_target_pairs={{1,0},{2,1},{3,2},{4,3},{5,4},{6,5},{7,6},{8,7},{9,8},{10,9},{11,1... | collective-permute-start | bytes 1179656 | tf_op jit(solution)/shard_map/ppermute | solution.py:409
  4.3 0.6 %broadcast_in_dim.18 = f32[16,1,128]{2,1,0:T(1,128)} broadcast(f32[]{:T(128)} %bitcast.13), dimensions={} | broadcast | bytes 8196 | tf_op jit(solution)/shard_map/broadcast_in_dim | solution.py:435
  4.9 7.4 %all-to-all-start = ((f32[16,1,128]{2,1,0:T(1,128)}), f32[16,1,128]{2,1,0:T(1,128)S(1)}, u32[]{:S(2)}, u32[]{:S(2)}) async-start(f32[16,1,128]{2,1,0:T(1,128)} %broadcast_in_dim.18), calls=%async_computation | async-start | bytes 16384 | tf_op jit(solution)/shard_map/all_to_all | solution.py:434
  12.3 0.0 collective-permute-done.next_hbm
  12.3 0.0 copy-start.3
  12.3 0.7 %copy-done.3 = bf16[512,384]{1,0:T(8,128)(2,1)} copy-done((bf16[512,384]{1,0:T(8,128)(2,1)}, bf16[512,384]{1,0:T(8,128)(2,1)S(1)}, u32[]{:S(2)}) %copy-start.3) | copy-done | bytes 393240
  13.1 18.3 %factor.1 = (bf16[384,384]{1,0:T(8,128)(2,1)}, bf16[256,384]{1,0:T(8,128)(2,1)}, bf16[384,384]{1,0:T(8,128)(2,1)}, f32[384,384]{1,0:T(8,128)}) custom-call(s32[16]{0:T(128)} %bitcast.20, s32[16]{0:T(128)} %bitcast.21, s32[1,96]{1,0:T(1,128)} %rows_ref.1, s32[1,96]{1,0:T(1,128)} %cols_ref.1, bf16[512,384]{1,0:T(8,128)(2,1)} %copy-done.3, ...), custom_call_target="tpu_custom_call" | custom-call | flops 4831838208 | bytes 3145728 | tf_op jit(solution)/shard_map/factor/pallas_call | solution.py:438
  31.4 2.0 %collective-permute-start.1 = (bf16[256,384]{1,0:T(8,128)(2,1)}, bf16[256,384]{1,0:T(8,128)(2,1)S(1)}, u32[]{:S(2)}, u32[]{:S(2)}) collective-permute-start(bf16[256,384]{1,0:T(8,128)(2,1)} %get-tuple-element.12), channel_id=1, source_target_pairs={{1,0},{2,1},{3,2},{4,3},{5,4},{6,5},{7,6},{8,7},{9,8},{10,9},{11,1... | collective-permute-start | bytes 589832 | tf_op jit(solution)/shard_map/ppermute | solution.py:409
  33.5 3.5 %collective-permute-start.2 = (bf16[384,384]{1,0:T(8,128)(2,1)}, bf16[384,384]{1,0:T(8,128)(2,1)S(1)}, u32[]{:S(2)}, u32[]{:S(2)}) collective-permute-start(bf16[384,384]{1,0:T(8,128)(2,1)} %get-tuple-element.11.yt_ref), channel_id=1, source_target_pairs={{0,1},{1,2},{2,3},{3,4},{4,5},{5,6},{6,7},{7,8},{8,9},{9,10},{10,1... | collective-permute-start | bytes 884744 | tf_op jit(solution)/shard_map/ppermute | solution.py:409
  37.0 0.0 all-to-all-done
  37.0 0.0 copy-start.2
  37.0 0.6 %copy-done.2 = f32[16,1,128]{2,1,0:T(1,128)} copy-done((f32[16,1,128]{2,1,0:T(1,128)}, f32[16,1,128]{2,1,0:T(1,128)S(1)}, u32[]{:S(2)}) %copy-start.2) | copy-done | bytes 8216
  37.6 0.0 copy-start
  37.6 0.0 copy-start.1
  37.6 3.1 %onsite.1 = f32[384,384]{1,0:T(8,128)} custom-call(s32[1]{0:T(128)} %bitcast.place_ref, f32[384,384]{1,0:T(8,128)} %get-tuple-element.9.w_ref, bf16[384,384]{1,0:T(8,128)(2,1)} %get-tuple-element.10.f_ref, f32[16,128]{1,0:T(8,128)} %bitcast.15), custom_call_target="tpu_custom_call" | custom-call | flops 4831838208 | bytes 6291456 | tf_op jit(solution)/shard_map/onsite/pallas_call | solution.py:485
  40.8 0.0 collective-permute-done.1.next_ref
  40.8 1.5 %collective-permute-done.2.last_yt_ref = bf16[384,384]{1,0:T(8,128)(2,1)S(1)} collective-permute-done((bf16[384,384]{1,0:T(8,128)(2,1)}, bf16[384,384]{1,0:T(8,128)(2,1)S(1)}, u32[]{:S(2)}, u32[]{:S(2)}) %collective-permute-start.2) | collective-permute-done | bytes 294944 | tf_op jit(solution)/shard_map/ppermute | solution.py:409
  42.3 0.0 copy-done
  42.3 0.0 copy-done.1
  42.3 1.4 %couple.1 = (f32[384,384]{1,0:T(8,128)}, f32[384,384]{1,0:T(8,128)}) custom-call(bf16[384,384]{1,0:T(8,128)(2,1)S(1)} %copy-done.1, bf16[256,384]{1,0:T(8,128)(2,1)S(1)} %collective-permute-done.1.next_ref, bf16[384,384]{1,0:T(8,128)(2,1)S(1)} %copy-done, bf16[384,384]{1,0:T(8,128)(2,1)S(1)} %collective-permute-done.2.last_yt_ref), custom_call_target="tpu_custom_call" | custom-call | flops 226492416 | bytes 1179648 | tf_op jit(solution)/shard_map/couple/pallas_call | solution.py:495
Async XLA Ops:
  1.7 10.7 %collective-permute-start = (bf16[512,384]{1,0:T(8,128)(2,1)S(1)}, bf16[512,384]{1,0:T(8,128)(2,1)S(1)}, u32[]{:S(2)}, u32[]{:S(2)}) collective-permute-start(bf16[512,384]{1,0:T(8,128)(2,1)S(1)} %slice_bitcast_fusion), channel_id=1, source_target_pairs={{1,0},{2,1},{3,2},{4,3},{5,4},{6,5},{7,6},{8,7},{9,8},{10,9},{11,1... | collective-permute-start | bytes 1179656 | tf_op jit(solution)/shard_map/ppermute | solution.py:409
  4.9 32.1 %all-to-all-start = ((f32[16,1,128]{2,1,0:T(1,128)}), f32[16,1,128]{2,1,0:T(1,128)S(1)}, u32[]{:S(2)}, u32[]{:S(2)}) async-start(f32[16,1,128]{2,1,0:T(1,128)} %broadcast_in_dim.18), calls=%async_computation | async-start | bytes 16384 | tf_op jit(solution)/shard_map/all_to_all | solution.py:434
  12.3 0.7 %copy-start.3 = (bf16[512,384]{1,0:T(8,128)(2,1)}, bf16[512,384]{1,0:T(8,128)(2,1)S(1)}, u32[]{:S(2)}) copy-start(bf16[512,384]{1,0:T(8,128)(2,1)S(1)} %collective-permute-done.next_hbm) | copy-start | bytes 1179652
  31.4 9.3 %collective-permute-start.1 = (bf16[256,384]{1,0:T(8,128)(2,1)}, bf16[256,384]{1,0:T(8,128)(2,1)S(1)}, u32[]{:S(2)}, u32[]{:S(2)}) collective-permute-start(bf16[256,384]{1,0:T(8,128)(2,1)} %get-tuple-element.12), channel_id=1, source_target_pairs={{1,0},{2,1},{3,2},{4,3},{5,4},{6,5},{7,6},{8,7},{9,8},{10,9},{11,1... | collective-permute-start | bytes 589832 | tf_op jit(solution)/shard_map/ppermute | solution.py:409
  33.5 8.8 %collective-permute-start.2 = (bf16[384,384]{1,0:T(8,128)(2,1)}, bf16[384,384]{1,0:T(8,128)(2,1)S(1)}, u32[]{:S(2)}, u32[]{:S(2)}) collective-permute-start(bf16[384,384]{1,0:T(8,128)(2,1)} %get-tuple-element.11.yt_ref), channel_id=1, source_target_pairs={{0,1},{1,2},{2,3},{3,4},{4,5},{5,6},{6,7},{7,8},{8,9},{9,10},{10,1... | collective-permute-start | bytes 884744 | tf_op jit(solution)/shard_map/ppermute | solution.py:409
  37.0 0.6 %copy-start.2 = (f32[16,1,128]{2,1,0:T(1,128)}, f32[16,1,128]{2,1,0:T(1,128)S(1)}, u32[]{:S(2)}) copy-start(f32[16,1,128]{2,1,0:T(1,128)S(1)} %all-to-all-done) | copy-start | bytes 24580
  37.6 4.7 %copy-start = (bf16[384,384]{1,0:T(8,128)(2,1)S(1)}, bf16[384,384]{1,0:T(8,128)(2,1)}, u32[]{:S(2)}) copy-start(bf16[384,384]{1,0:T(8,128)(2,1)} %get-tuple-element.10.f_ref) | copy-start | bytes 884740
  37.6 4.7 %copy-start.1 = (bf16[384,384]{1,0:T(8,128)(2,1)S(1)}, bf16[384,384]{1,0:T(8,128)(2,1)}, u32[]{:S(2)}) copy-start(bf16[384,384]{1,0:T(8,128)(2,1)} %get-tuple-element.11.yt_ref) | copy-start | bytes 884740

commit v9 on v8

--- a/solution.py
+++ b/solution.py
@@ -198,6 +198,7 @@
     cblocks_ref,
     hop_ref,
     m_ref,
+    mt_ref,
     index_ref,
     made_ref,
     table_ref,
@@ -308,9 +309,22 @@
     for n, work in enumerate(reductions):
         plan[tiles - 1, n * panels // len(reductions)].append(work)
     for n, work in enumerate(links):
-        plan[tiles - 1, n * (panels - 4) // len(links)].append(work)
+        plan[tiles - 1, n * (panels // 2) // len(links)].append(work)
     for n, work in enumerate(finish):
-        plan[tiles - 1, panels - 3 + n].append(work)
+        plan[tiles - 1, panels // 2 + n].append(work)
+    ready = modes - TILE
+
+    def turn_early():
+        mt_ref[0], mt_ref[1] = split(m_ref[...].T)
+        f_ref[:, :ready] = inv_ref[:ready, :].T.astype(BF16)
+
+    def link_columns(columns):
+        part = f_ref[:, columns]
+        yt = bf_dot(mt_ref[0], part, NN) + bf_dot(mt_ref[1], part, NN)
+        yt_ref[:, columns] = yt.astype(BF16)
+
+    plan[tiles - 1, panels - 5].append(turn_early)
+    plan[tiles - 1, panels - 3].append(call(link_columns, slice(0, ready)))
     for t in range(1, tiles):
         late = []
         if t > 1:
@@ -351,12 +365,12 @@
         return carry
 
     lax.fori_loop(0, tiles, step_of, 0)
-    factor = inv_ref[...].T.astype(BF16)
-    f_ref[...] = factor
-    packed_ref[...] = factor[: 2 * TILE, :]
-    packed_ref[TILE:, :TILE] = factor[2 * TILE :, 2 * TILE :]
-    high, low = split(m_ref[...])
-    yt_ref[...] = (bf_dot(high, factor, TN) + bf_dot(low, factor, TN)).astype(BF16)
+    last = inv_ref[ready:, :].T.astype(BF16)
+    f_ref[:, ready:] = last
+    link_columns(slice(ready, modes))
+    packed_ref[:, :ready] = f_ref[:ready, :ready]
+    packed_ref[:, ready:] = last[:ready, :]
+    packed_ref[TILE:, :TILE] = last[ready:, :]
 
 
 def couple_kernel(yt_ref, next_ref, f_ref, last_yt_ref, right_ref, left_ref, full_ref):
@@ -460,6 +474,7 @@
             pltpu.VMEM((links, TILE, TILE), BF16),
             pltpu.VMEM((surface, modes), F32),
             pltpu.VMEM((modes, modes), F32),
+            pltpu.VMEM((2, modes, modes), BF16),
             pltpu.VMEM((ROWS, TILE), jnp.int32),
             pltpu.VMEM((ROWS, TILE), jnp.int32),
             pltpu.SMEM((ROWS, TILE), jnp.int32),

time: 44.4 us -> 44.6 us (level)
  no operation moved by 1% of the time
where the time goes in v9:
time: 44.6 us; the launch traced here: 43.9 us
  Pallas kernels  23.1 us (52%)
  starting transfers between devices  15 us (34%)
  local copies, waits for them, and re-layouts  2.98 us (7%)
  waiting for transfers between devices  1.52 us (3%)
  between operations  1.34 us (3%)
    pallas_call x1, Pallas kernels, shards(): pl.pallas_call(factor_kernel, out_shape=(struct((modes, modes), BF16), st...  18.5 us
    ppermute x3, starting transfers between devices, passed_along(): return lax.ppermute(block, axis, route)  7.53 us
    all_to_all x1, starting transfers between devices, shards(): lax.all_to_all(jnp.broadcast_to(potential_step[:, None], (slabs, TILE)),...  7.43 us
    pallas_call x1, Pallas kernels, shards(): pl.pallas_call(onsite_kernel, out_shape=struct((modes, modes), F32), in_s...  3.15 us
    ppermute x3, waiting for transfers between devices, passed_along(): return lax.ppermute(block, axis, route)  1.52 us
    pallas_call x1, Pallas kernels, shards(): pl.pallas_call(couple_kernel, out_shape=(struct((modes, modes), F32),) *...  1.41 us
    unnamed x8, local copies, waits for them, and re-layouts  1.34 us
    slice x1, local copies, waits for them, and re-layouts, shards(): next_head = passed_along(u[:surface], 'slab', -1)  1.04 us
  transfers between devices with their start and end apart: 4, of which 1 were waited for; matrix products, arithmetic and copies ran while one was open for 1% of the time, Pallas kernels for 49%

profile of v9, /device:TPU:1, one launch (start us, length us, event | category | flops | bytes accessed | tf_op | source)
XLA Modules:
  0.0 43.9 jit_solution(15053644323125610510)
XLA Ops:
  0.6 1.0 %slice_bitcast_fusion = bf16[512,384]{1,0:T(8,128)(2,1)S(1)} fusion(bf16[1,4096,384]{2,1,0:T(8,128)(2,1)} %param.8), kind=kLoop, calls=%fused_computation | loop fusion | bytes 786432 | tf_op jit(solution)/shard_map/slice | solution.py:447
  1.7 2.0 %collective-permute-start = (bf16[512,384]{1,0:T(8,128)(2,1)S(1)}, bf16[512,384]{1,0:T(8,128)(2,1)S(1)}, u32[]{:S(2)}, u32[]{:S(2)}) collective-permute-start(bf16[512,384]{1,0:T(8,128)(2,1)S(1)} %slice_bitcast_fusion), channel_id=1, source_target_pairs={{1,0},{2,1},{3,2},{4,3},{5,4},{6,5},{7,6},{8,7},{9,8},{10,9},{11,1... | collective-permute-start | bytes 1179656 | tf_op jit(solution)/shard_map/ppermute | solution.py:423
  4.3 0.6 %broadcast_in_dim.18 = f32[16,1,128]{2,1,0:T(1,128)} broadcast(f32[]{:T(128)} %bitcast.13), dimensions={} | broadcast | bytes 8196 | tf_op jit(solution)/shard_map/broadcast_in_dim | solution.py:449
  4.9 7.4 %all-to-all-start = ((f32[16,1,128]{2,1,0:T(1,128)}), f32[16,1,128]{2,1,0:T(1,128)S(1)}, u32[]{:S(2)}, u32[]{:S(2)}) async-start(f32[16,1,128]{2,1,0:T(1,128)} %broadcast_in_dim.18), calls=%async_computation | async-start | bytes 16384 | tf_op jit(solution)/shard_map/all_to_all | solution.py:448
  12.3 0.0 collective-permute-done.next_hbm
  12.3 0.0 copy-start.3
  12.3 0.7 %copy-done.3 = bf16[512,384]{1,0:T(8,128)(2,1)} copy-done((bf16[512,384]{1,0:T(8,128)(2,1)}, bf16[512,384]{1,0:T(8,128)(2,1)S(1)}, u32[]{:S(2)}) %copy-start.3) | copy-done | bytes 393240
  13.1 18.5 %factor.1 = (bf16[384,384]{1,0:T(8,128)(2,1)}, bf16[256,384]{1,0:T(8,128)(2,1)}, bf16[384,384]{1,0:T(8,128)(2,1)}, f32[384,384]{1,0:T(8,128)}) custom-call(s32[16]{0:T(128)} %bitcast.20, s32[16]{0:T(128)} %bitcast.21, s32[1,96]{1,0:T(1,128)} %rows_ref.1, s32[1,96]{1,0:T(1,128)} %cols_ref.1, bf16[512,384]{1,0:T(8,128)(2,1)} %copy-done.3, ...), custom_call_target="tpu_custom_call" | custom-call | flops 4831838208 | bytes 3145728 | tf_op jit(solution)/shard_map/factor/pallas_call | solution.py:452
  31.6 2.0 %collective-permute-start.1 = (bf16[256,384]{1,0:T(8,128)(2,1)}, bf16[256,384]{1,0:T(8,128)(2,1)S(1)}, u32[]{:S(2)}, u32[]{:S(2)}) collective-permute-start(bf16[256,384]{1,0:T(8,128)(2,1)} %get-tuple-element.12), channel_id=1, source_target_pairs={{1,0},{2,1},{3,2},{4,3},{5,4},{6,5},{7,6},{8,7},{9,8},{10,9},{11,1... | collective-permute-start | bytes 589832 | tf_op jit(solution)/shard_map/ppermute | solution.py:423
  33.6 3.5 %collective-permute-start.2 = (bf16[384,384]{1,0:T(8,128)(2,1)}, bf16[384,384]{1,0:T(8,128)(2,1)S(1)}, u32[]{:S(2)}, u32[]{:S(2)}) collective-permute-start(bf16[384,384]{1,0:T(8,128)(2,1)} %get-tuple-element.11.yt_ref), channel_id=1, source_target_pairs={{0,1},{1,2},{2,3},{3,4},{4,5},{5,6},{6,7},{7,8},{8,9},{9,10},{10,1... | collective-permute-start | bytes 884744 | tf_op jit(solution)/shard_map/ppermute | solution.py:423
  37.2 0.0 all-to-all-done
  37.2 0.0 copy-start.2
  37.2 0.6 %copy-done.2 = f32[16,1,128]{2,1,0:T(1,128)} copy-done((f32[16,1,128]{2,1,0:T(1,128)}, f32[16,1,128]{2,1,0:T(1,128)S(1)}, u32[]{:S(2)}) %copy-start.2) | copy-done | bytes 8216
  37.8 0.0 copy-start
  37.8 0.0 copy-start.1
  37.8 3.1 %onsite.1 = f32[384,384]{1,0:T(8,128)} custom-call(s32[1]{0:T(128)} %bitcast.place_ref, f32[384,384]{1,0:T(8,128)} %get-tuple-element.9.w_ref, bf16[384,384]{1,0:T(8,128)(2,1)} %get-tuple-element.10.f_ref, f32[16,128]{1,0:T(8,128)} %bitcast.15), custom_call_target="tpu_custom_call" | custom-call | flops 4831838208 | bytes 6291456 | tf_op jit(solution)/shard_map/onsite/pallas_call | solution.py:500
  40.9 0.0 collective-permute-done.1.next_ref
  41.0 1.5 %collective-permute-done.2.last_yt_ref = bf16[384,384]{1,0:T(8,128)(2,1)S(1)} collective-permute-done((bf16[384,384]{1,0:T(8,128)(2,1)}, bf16[384,384]{1,0:T(8,128)(2,1)S(1)}, u32[]{:S(2)}, u32[]{:S(2)}) %collective-permute-start.2) | collective-permute-done | bytes 294944 | tf_op jit(solution)/shard_map/ppermute | solution.py:423
  42.5 0.0 copy-done
  42.5 0.0 copy-done.1
  42.5 1.4 %couple.1 = (f32[384,384]{1,0:T(8,128)}, f32[384,384]{1,0:T(8,128)}) custom-call(bf16[384,384]{1,0:T(8,128)(2,1)S(1)} %copy-done.1, bf16[256,384]{1,0:T(8,128)(2,1)S(1)} %collective-permute-done.1.next_ref, bf16[384,384]{1,0:T(8,128)(2,1)S(1)} %copy-done, bf16[384,384]{1,0:T(8,128)(2,1)S(1)} %collective-permute-done.2.last_yt_ref), custom_call_target="tpu_custom_call" | custom-call | flops 226492416 | bytes 1179648 | tf_op jit(solution)/shard_map/couple/pallas_call | solution.py:510
Async XLA Ops:
  1.7 10.7 %collective-permute-start = (bf16[512,384]{1,0:T(8,128)(2,1)S(1)}, bf16[512,384]{1,0:T(8,128)(2,1)S(1)}, u32[]{:S(2)}, u32[]{:S(2)}) collective-permute-start(bf16[512,384]{1,0:T(8,128)(2,1)S(1)} %slice_bitcast_fusion), channel_id=1, source_target_pairs={{1,0},{2,1},{3,2},{4,3},{5,4},{6,5},{7,6},{8,7},{9,8},{10,9},{11,1... | collective-permute-start | bytes 1179656 | tf_op jit(solution)/shard_map/ppermute | solution.py:423
  4.9 32.3 %all-to-all-start = ((f32[16,1,128]{2,1,0:T(1,128)}), f32[16,1,128]{2,1,0:T(1,128)S(1)}, u32[]{:S(2)}, u32[]{:S(2)}) async-start(f32[16,1,128]{2,1,0:T(1,128)} %broadcast_in_dim.18), calls=%async_computation | async-start | bytes 16384 | tf_op jit(solution)/shard_map/all_to_all | solution.py:448
  12.3 0.7 %copy-start.3 = (bf16[512,384]{1,0:T(8,128)(2,1)}, bf16[512,384]{1,0:T(8,128)(2,1)S(1)}, u32[]{:S(2)}) copy-start(bf16[512,384]{1,0:T(8,128)(2,1)S(1)} %collective-permute-done.next_hbm) | copy-start | bytes 1179652
  31.6 9.3 %collective-permute-start.1 = (bf16[256,384]{1,0:T(8,128)(2,1)}, bf16[256,384]{1,0:T(8,128)(2,1)S(1)}, u32[]{:S(2)}, u32[]{:S(2)}) collective-permute-start(bf16[256,384]{1,0:T(8,128)(2,1)} %get-tuple-element.12), channel_id=1, source_target_pairs={{1,0},{2,1},{3,2},{4,3},{5,4},{6,5},{7,6},{8,7},{9,8},{10,9},{11,1... | collective-permute-start | bytes 589832 | tf_op jit(solution)/shard_map/ppermute | solution.py:423
  33.6 8.8 %collective-permute-start.2 = (bf16[384,384]{1,0:T(8,128)(2,1)}, bf16[384,384]{1,0:T(8,128)(2,1)S(1)}, u32[]{:S(2)}, u32[]{:S(2)}) collective-permute-start(bf16[384,384]{1,0:T(8,128)(2,1)} %get-tuple-element.11.yt_ref), channel_id=1, source_target_pairs={{0,1},{1,2},{2,3},{3,4},{4,5},{5,6},{6,7},{7,8},{8,9},{9,10},{10,1... | collective-permute-start | bytes 884744 | tf_op jit(solution)/shard_map/ppermute | solution.py:423
  37.2 0.6 %copy-start.2 = (f32[16,1,128]{2,1,0:T(1,128)}, f32[16,1,128]{2,1,0:T(1,128)S(1)}, u32[]{:S(2)}) copy-start(f32[16,1,128]{2,1,0:T(1,128)S(1)} %all-to-all-done) | copy-start | bytes 24580
  37.8 4.7 %copy-start = (bf16[384,384]{1,0:T(8,128)(2,1)S(1)}, bf16[384,384]{1,0:T(8,128)(2,1)}, u32[]{:S(2)}) copy-start(bf16[384,384]{1,0:T(8,128)(2,1)} %get-tuple-element.10.f_ref) | copy-start | bytes 884740
  37.8 4.7 %copy-start.1 = (bf16[384,384]{1,0:T(8,128)(2,1)S(1)}, bf16[384,384]{1,0:T(8,128)(2,1)}, u32[]{:S(2)}) copy-start(bf16[384,384]{1,0:T(8,128)(2,1)} %get-tuple-element.11.yt_ref) | copy-start | bytes 884740
